TPU v7x, 512 devices: a whole 4x4x16 slice. The times are simulated.
512 devices in a mesh: dp: 4 (over z_hi), cin: 32 (over y, x, core), cout: 4 (over z_lo).
Axes of the slice: x: 4, y: 4, z: 16 (z_hi: 4, z_lo: 4; z = z_hi * 4 + z_lo), core: 2. Of those that a mesh axis runs over, the one named last changes fastest.
Arguments:
- weight: bfloat16 [8, 2, 2048, 2048], P(None, None, 'cin', 'cout'), may hold values from -0.09375 to 0.09375
- spectrum: bfloat16 [8, 2, 2048, 2048], P(None, None, ('cin', 'cout'), 'dp'), may hold values from -0.1796875 to 0.1796875
- out_grad: bfloat16 [8, 2, 2048, 2048], P(None, None, ('cout', 'cin'), 'dp'), may hold values from -6 to 6
Outputs:
- spectrum_grad: bfloat16 [8, 2, 2048, 2048], P(None, None, ('cin', 'cout'), 'dp')
- weight_grad: bfloat16 [8, 2, 2048, 2048], P(None, None, 'cin', 'cout')
All inputs are finite; a program needn't handle non-finite values.
Results may differ from a plain program's by a relative error of at most 0.001.
Values may be sent and summed in bfloat16 or wider, within the bound.
No kernel may reach another device: no remote copies, remote signals or barrier semaphores. Data moves between devices by JAX's collectives and lax.ppermute only.
A program may use at most 64 MiB of HBM per device.

v0:
```python
import jax
import jax.numpy as jnp
from jax import lax
from jax.sharding import PartitionSpec as P


def block_terms(columns, rows_in, piece):
    w_real = columns[:, 0]
    w_imag = columns[:, 1]
    g_real = piece[:, 0]
    g_imag = piece[:, 1]
    x_real = rows_in[:, 0]
    x_imag = rows_in[:, 1]
    dx_real = jnp.einsum(
        "mio,mob->mib", w_real, g_real, preferred_element_type=jnp.float32
    ) + jnp.einsum("mio,mob->mib", w_imag, g_imag, preferred_element_type=jnp.float32)
    dx_imag = jnp.einsum(
        "mio,mob->mib", w_real, g_imag, preferred_element_type=jnp.float32
    ) - jnp.einsum("mio,mob->mib", w_imag, g_real, preferred_element_type=jnp.float32)
    dw_real = jnp.einsum(
        "mib,mob->mio", x_real, g_real, preferred_element_type=jnp.float32
    ) + jnp.einsum("mib,mob->mio", x_imag, g_imag, preferred_element_type=jnp.float32)
    dw_imag = jnp.einsum(
        "mib,mob->mio", x_real, g_imag, preferred_element_type=jnp.float32
    ) - jnp.einsum("mib,mob->mio", x_imag, g_real, preferred_element_type=jnp.float32)
    return (jnp.stack([dx_real, dx_imag], axis=1), jnp.stack([dw_real, dw_imag], axis=1))


def accumulate(weight, rows_in, grads):
    part_in, block = block_terms(weight, rows_in, lax.all_gather(grads, "cin", axis=2, tiled=True))
    return (part_in, block)


def on_device(weight, spectrum, out_grad):
    rows_in = lax.all_gather(spectrum, "cout", axis=2, tiled=True)
    term_in, term_weight = accumulate(weight, rows_in, out_grad)
    summed = lax.psum(term_weight, "dp")
    weight_grad = summed.astype(jnp.bfloat16)
    spectrum_grad = lax.psum_scatter(term_in, "cout", scatter_dimension=2, tiled=True).astype(
        jnp.bfloat16
    )
    return (spectrum_grad, weight_grad)


def solution(mesh):
    placed = (
        P(None, None, "cin", "cout"),
        P(None, None, ("cin", "cout"), "dp"),
        P(None, None, ("cout", "cin"), "dp"),
    )
    return jax.shard_map(
        on_device,
        mesh=mesh,
        in_specs=placed,
        out_specs=(P(None, None, ("cin", "cout"), "dp"), P(None, None, "cin", "cout")),
        check_vma=False,
    )
```

profile of v0, /device:TPU:34, one launch (start us, length us, event | category | flops | bytes accessed | tf_op | source)
XLA Modules:
  0.0 329.4 jit_solution(9001423755656557211)
XLA Ops:
  7.2 0.0 all-gather.3.cloned.1.call-start
  7.2 1.7 copy.6
  9.0 0.0 all-gather.3.cloned.1.call-update
  9.0 0.0 all-gather.5.cloned.1.call-start
  9.0 1.7 copy.8
  10.7 0.0 all-gather.5.cloned.1.call-update
  10.7 0.0 reduce-scatter.2.cloned.1.call-start
  10.8 73.4 %all-gather.3.cloned.1.call-done = bf16[8,2,512,512]{3,2,0,1:T(8,128)(2,1)} async-done(((bf16[8,2,16,512]{3,2,0,1:T(8,128)(2,1)}), bf16[8,2,512,512]{3,2,0,1:T(8,128)(2,1)}) %all-gather.3.cloned.1.call-update) | async-done | bytes 8388624 | tf_op jit(solution)/shard_map/all_gather | solution.py:30
  84.2 3.3 %fusion.3 = f32[8,64,512]{2,1,0:T(8,128)S(1)} fusion(bf16[8,2,512,512]{3,2,0,1:T(8,128)(2,1)} %all-gather.3.cloned.1.call-done, bf16[8,2,64,512]{3,2,1,0:T(8,128)(2,1)} %param.3), kind=kOutput, calls=%fused_computation.5 | convolution fusion | flops 268435456 | bytes 5767168 | tf_op jit(solution)/shard_map/mio,mob->mib/dot_general | solution.py:14
  87.5 3.5 %fusion.2 = f32[8,64,512]{2,1,0:T(8,128)S(1)} fusion(bf16[8,2,512,512]{3,2,0,1:T(8,128)(2,1)} %all-gather.3.cloned.1.call-done, bf16[8,2,64,512]{3,2,1,0:T(8,128)(2,1)S(1)} %copy-done.1), kind=kOutput, calls=%fused_computation.4 | convolution fusion | flops 268435456 | bytes 5767168 | tf_op jit(solution)/shard_map/mio,mob->mib/dot_general | solution.py:19
  91.0 0.8 fusion.9
  91.8 0.8 fusion.11
  92.6 1.5 pad_maximum_fusion
  94.1 0.0 reduce-scatter.2.cloned.1.call-update
  94.1 29.1 %all-gather.5.cloned.1.call-done = bf16[8,2,64,512]{3,2,0,1:T(8,128)(2,1)} async-done(((bf16[8,2,16,512]{3,2,0,1:T(8,128)(2,1)}), bf16[8,2,64,512]{3,2,0,1:T(8,128)(2,1)}) %all-gather.5.cloned.1.call-update) | async-done | bytes 1048592 | tf_op jit(solution)/shard_map/all_gather | solution.py:35
  123.2 3.9 %fusion.1 = f32[8,64,512]{2,1,0:T(8,128)S(1)} fusion(bf16[8,2,512,512]{3,2,0,1:T(8,128)(2,1)} %all-gather.3.cloned.1.call-done, bf16[8,2,64,512]{3,2,0,1:T(8,128)(2,1)} %all-gather.5.cloned.1.call-done), kind=kOutput, calls=%fused_computation.3 | convolution fusion | flops 268435456 | bytes 5767168 | tf_op jit(solution)/shard_map/mib,mob->mio/dot_general | solution.py:20
  127.1 3.7 %fusion = f32[8,64,512]{2,1,0:T(8,128)S(1)} fusion(bf16[8,2,512,512]{3,2,0,1:T(8,128)(2,1)} %all-gather.3.cloned.1.call-done, bf16[8,2,64,512]{3,2,0,1:T(8,128)(2,1)S(1)} %copy-done.2), kind=kOutput, calls=%fused_computation.2 | convolution fusion | flops 268435456 | bytes 5767168 | tf_op jit(solution)/shard_map/mib,mob->mio/dot_general | solution.py:25
  130.8 3.6 %fusion.13 = f32[8,1,64,512]{3,2,0,1:T(8,128)S(1)} fusion(f32[8,64,512]{2,1,0:T(8,128)S(1)} %fusion.1, bf16[8,2,512,512]{3,2,0,1:T(8,128)(2,1)} %all-gather.3.cloned.1.call-done, bf16[8,2,64,512]{3,2,0,1:T(8,128)(2,1)S(1)} %copy-done.2), kind=kOutput, calls=%fused_computation.17 | convolution fusion | flops 268697600 | bytes 6815744 | tf_op jit(solution)/shard_map/mib,mob->mio/dot_general | solution.py:22
  134.4 1.4 fusion.15
  135.8 0.2 pad_maximum_fusion.1
  136.0 184.0 %all-reduce.1 = bf16[8,2,64,512]{3,2,0,1:T(8,128)(2,1)S(1)} all-reduce(f32[8,2,64,512]{3,2,0,1:T(8,128)S(1)} %pad_maximum_fusion.1), channel_id=1, replica_groups=mesh['dp'=4,'cin'=32,'cout'=4] {'dp'}, use_global_device_ids=true, to_apply=%region_1.0 | all-reduce | flops 524288 | bytes 3145728 | tf_op jit(solution)/shard_map/psum | solution.py:37
  320.1 1.1 copy.10
  321.1 1.1 convert_element_type.6
  322.2 0.7 copy.9
  (12 shorter events, 0.0 us)
Async XLA Ops:
  7.2 80.3 %copy-start.1 = (bf16[8,2,64,512]{3,2,1,0:T(8,128)(2,1)S(1)}, bf16[8,2,64,512]{3,2,1,0:T(8,128)(2,1)}, u32[]{:S(2)}) copy-start(bf16[8,2,64,512]{3,2,1,0:T(8,128)(2,1)} %param.3) | copy-start | bytes 3145732
  7.2 77.0 %all-gather.3.cloned.1.call-start = ((), (), s32[]{:S(2)}) async-start(), calls=%async_computation.1 | async-start | bytes 8650752 | tf_op jit(solution)/shard_map/all_gather | solution.py:30
  9.0 114.2 %all-gather.5.cloned.1.call-start = ((), (), s32[]{:S(2)}) async-start(), calls=%async_computation.3 | async-start | bytes 1310720 | tf_op jit(solution)/shard_map/all_gather | solution.py:35
  10.7 310.4 %reduce-scatter.2.cloned.1.call-start = ((), (), s32[]{:S(2)}) async-start(), calls=%async_computation.2 | async-start | bytes 2621440 | tf_op jit(solution)/shard_map/reduce_scatter | solution.py:39
  84.2 6.8 %copy-start = (bf16[8,2,512,512]{3,2,0,1:T(8,128)(2,1)S(1)}, bf16[8,2,512,512]{3,2,0,1:T(8,128)(2,1)}, u32[]{:S(2)}) copy-start(bf16[8,2,512,512]{3,2,0,1:T(8,128)(2,1)} %all-gather.3.cloned.1.call-done) | copy-start | bytes 25165828
  123.2 3.9 %copy-start.2 = (bf16[8,2,64,512]{3,2,0,1:T(8,128)(2,1)S(1)}, bf16[8,2,64,512]{3,2,0,1:T(8,128)(2,1)}, u32[]{:S(2)}) copy-start(bf16[8,2,64,512]{3,2,0,1:T(8,128)(2,1)} %all-gather.5.cloned.1.call-done) | copy-start | bytes 3145732
  123.2 11.2 %slice-start = ((s8[8388608]{0:T(1024)(128)(4,1)}), s8[4194304]{0:T(1024)(128)(4,1)S(1)}, s32[]{:S(2)}) async-start(s8[8388608]{0:T(1024)(128)(4,1)} %bitcast.58), calls=%async_computation.4 | async-start | bytes 8388608
  127.1 7.3 %slice-start.1 = ((s8[8388608]{0:T(1024)(128)(4,1)}), s8[4194304]{0:T(1024)(128)(4,1)S(1)}, s32[]{:S(2)}) async-start(s8[8388608]{0:T(1024)(128)(4,1)} %bitcast.58), calls=%async_computation.5 | async-start | bytes 8388608
Sparse Core Ops, SparseCore 0:
  11.8 72.3 all-gather.2
  86.8 36.3 all-gather.4
  126.0 147.0 reduce-scatter.1
where the time goes:
time: 330 us; the launch traced here: 329 us
  blocking collectives  184 us (56%)
  waiting for transfers between devices  102 us (31%)
  matrix products  20.9 us (6%)
  between operations  13.9 us (4%)
  local copies, waits for them, and re-layouts  5.23 us (2%)
    psum x1, blocking collectives, on_device(): summed = lax.psum(term_weight, 'dp')  184 us
    all_gather x1, waiting for transfers between devices, accumulate(): lax.all_gather(grads, 'cin', axis=2, tiled=True)  73.4 us
    all_gather x1, waiting for transfers between devices, on_device(): rows_in = lax.all_gather(spectrum, 'cout', axis=2, tiled=True)  29.1 us
  transfers between devices with their start and end apart: 3, of which 2 were waited for; matrix products, arithmetic and copies ran while one was open for 8% of the time, Pallas kernels for 0%

commit v1 on v0

v1 whole, which is shorter than its diff:
```python
import functools

import jax
import jax.numpy as jnp
from jax import lax
from jax.experimental import pallas as pl
from jax.experimental.pallas import tpu as pltpu
from jax.sharding import PartitionSpec as P

HEARD = (0, 3, 1, 2)
SHIFTS = (1, 3, 2)
MIB = 1 << 20
ANY = pl.BlockSpec(memory_space=pl.ANY)
SMEM = pl.BlockSpec(memory_space=pltpu.SMEM)
VMEM = pl.BlockSpec(memory_space=pltpu.VMEM)


def ring(value, axis, shift):
    return lax.ppermute(value, axis, [(i, (i + shift) % 4) for i in range(4)])


def flip(value, axis, bits, size=4):
    return lax.ppermute(value, axis, [(i, i ^ bits) for i in range(size)])


def swap_cores(value):
    return flip(value, "cin", 1, 32)


def hop(value, shift, stage):
    pairs = []
    for i in range(32):
        y, x, core = i // 8, (i // 2) % 4, i % 2
        if core == stage:
            x = (x + shift) % 4
        else:
            y = (y + shift) % 4
        pairs.append((i, (y * 4 + x) * 2 + core))
    return lax.ppermute(value, "cin", pairs)


def plane_gather(mine, theirs):
    first = jnp.stack([mine, swap_cores(theirs)])
    line = jnp.stack([first] + [hop(first, shift, 0) for shift in SHIFTS])
    held = [line] + [hop(line, shift, 1) for shift in SHIFTS]
    return held, [swap_cores(piece) for piece in held]


def plane_blocks():
    place = lax.axis_index("cin")
    y, x, core = place // 8, (place // 2) % 4, place % 2
    heard = jnp.array(HEARD, jnp.int32)
    tables = []
    for owner in (core, 1 - core):
        along_x = (x + heard) % 4
        along_y = (y + heard) % 4
        second, first, source = jnp.meshgrid(
            jnp.arange(4), jnp.arange(4), jnp.arange(2), indexing="ij"
        )
        across = jnp.where(owner == 0, along_x[first], along_x[second])
        down = jnp.where(owner == 0, along_y[second], along_y[first])
        origin = jnp.where(source == 0, owner, 1 - owner)
        tables.append(((down * 4 + across) * 2 + origin).astype(jnp.int32).reshape(32))
    return jnp.stack(tables)


def input_terms(half, blocks, scalars, w, p0, p1, p2, p3, keep, send, grads, sem):
    pieces = (p0, p1, p2, p3)
    for second in range(4):
        for first in range(4):
            for source in range(2):
                row = pl.multiple_of(blocks[half, (second * 4 + first) * 2 + source] * 16, 16)
                pltpu.make_async_copy(
                    pieces[second].at[first, source], grads.at[:, :, pl.ds(row, 16), :], sem
                ).start()
    pltpu.make_async_copy(grads, grads, sem).wait()
    base = scalars[half]
    rows = [pl.multiple_of(scalars[2 + r], 16) for r in range(4)]
    for mode in range(4):
        real = jnp.concatenate([w[base + mode, 0, pl.ds(row, 16), :] for row in rows], axis=0)
        imag = jnp.concatenate([w[base + mode, 1, pl.ds(row, 16), :] for row in rows], axis=0)
        total = jnp.dot(
            jnp.concatenate([real, -imag], axis=0), grads[mode, 0], preferred_element_type=jnp.float32
        ) + jnp.dot(
            jnp.concatenate([imag, real], axis=0), grads[mode, 1], preferred_element_type=jnp.float32
        )
        for part in range(2):
            for r in range(2):
                start = part * 64 + r * 16
                keep[r, mode, part] = total[start : start + 16]
                send[r, mode, part] = total[start + 32 : start + 48]


def input_half(half, blocks, scalars, weight, held):
    out = jax.ShapeDtypeStruct((2, 4, 2, 16, 512), jnp.float32)
    return pl.pallas_call(
        functools.partial(input_terms, half),
        out_shape=(out, out),
        in_specs=[SMEM, SMEM, VMEM] + [ANY] * 4,
        out_specs=(VMEM, VMEM),
        scratch_shapes=[pltpu.VMEM((4, 2, 512, 512), jnp.bfloat16), pltpu.SemaphoreType.DMA],
        compiler_params=pltpu.CompilerParams(vmem_limit_bytes=20 * MIB),
        cost_estimate=pl.CostEstimate(flops=1 << 30, bytes_accessed=7 * MIB, transcendentals=0),
        name="input_terms",
    )(blocks, scalars, weight, *held)


def weight_terms(slot, blocks, scalars, *refs):
    own, other, late, xs, out, grads, rows, sem = refs[:4], refs[4:8], refs[8:12], refs[12:15], *refs[15:]
    mode = scalars[6 + slot]
    near = scalars[8 + slot]

    def place(half, index):
        return pl.ds(pl.multiple_of(blocks[half, index] * 16, 16), 16)

    for second in range(4):
        for first in range(4):
            for source in range(2):
                index = (second * 4 + first) * 2 + source
                pltpu.make_async_copy(
                    late[second].at[first, source], grads.at[pl.ds(1, 3), :, place(slot, index), :], sem
                ).start()

    def local(half, pieces):
        for second in range(4):
            for first in range(4):
                for source in range(2):
                    index = (second * 4 + first) * 2 + source
                    pltpu.make_async_copy(
                        pieces[second].at[first, source, near], grads.at[0, :, place(half, index), :], sem
                    ).start()

    @pl.when(scalars[10] == 0)
    def _():
        local(0, own)

    @pl.when(scalars[10] != 0)
    def _():
        local(1, other)

    for index, piece in enumerate((xs[0], xs[1], xs[2].at[0], xs[2].at[1])):
        row = pl.multiple_of(scalars[11 + index], 16)
        for block in range(4):
            pltpu.make_async_copy(
                piece.at[block, mode], rows.at[block, :, pl.ds(row, 16), :], sem
            ).start()
    pltpu.make_async_copy(grads, grads, sem).wait()
    pltpu.make_async_copy(rows, rows, sem).wait()

    total = jnp.zeros((128, 512), jnp.float32)
    contract = (((1,), (1,)), ((), ()))
    for block in range(4):
        real = rows[block, 0]
        imag = rows[block, 1]
        total += lax.dot_general(
            jnp.concatenate([real, -imag], axis=0), grads[block, 0], contract, preferred_element_type=jnp.float32
        )
        total += lax.dot_general(
            jnp.concatenate([imag, real], axis=0), grads[block, 1], contract, preferred_element_type=jnp.float32
        )
    out[0] = total[:64].astype(jnp.bfloat16)
    out[1] = total[64:].astype(jnp.bfloat16)


def weight_mode(slot, blocks, scalars, own, other, late, xs):
    return pl.pallas_call(
        functools.partial(weight_terms, slot),
        out_shape=jax.ShapeDtypeStruct((2, 64, 512), jnp.bfloat16),
        in_specs=[SMEM, SMEM] + [ANY] * 15,
        out_specs=VMEM,
        scratch_shapes=[
            pltpu.VMEM((4, 2, 512, 512), jnp.bfloat16),
            pltpu.VMEM((4, 2, 64, 512), jnp.bfloat16),
            pltpu.SemaphoreType.DMA,
        ],
        compiler_params=pltpu.CompilerParams(vmem_limit_bytes=20 * MIB),
        cost_estimate=pl.CostEstimate(flops=1 << 30, bytes_accessed=5 * MIB, transcendentals=0),
        name="weight_terms",
    )(blocks, scalars, *own, *other, *late, *xs)


def place_modes(scalars, *refs):
    out, sem = refs[-2:]
    copies = []
    for slot in range(2):
        mine, back, ahead, far_real, far_imag = refs[5 * slot : 5 * slot + 5]
        for source, step in ((mine, 0), (back, 1), (ahead, 2)):
            copies.append((source, out.at[scalars[15 + 4 * slot + step]]))
        far = scalars[15 + 4 * slot + 3]
        copies.append((far_real, out.at[far, 0]))
        copies.append((far_imag, out.at[far, 1]))
    for source, target in copies:
        pltpu.make_async_copy(source, target, sem).start()
    pltpu.make_async_copy(out, out, sem).wait()


def on_device(weight, spectrum, out_grad):
    dp, place, cout = lax.axis_index("dp"), lax.axis_index("cin"), lax.axis_index("cout")
    core = place % 2
    blocks = plane_blocks()
    slots = (core, 1 - core)
    scalars = jnp.stack(
        [4 * core, 4 - 4 * core]
        + [16 * (cout ^ r) for r in (0, 2, 1, 3)]
        + list(slots)
        + [(2 * dp + slot) % 4 for slot in slots]
        + [(dp // 2) ^ core]
        + [16 * (cout ^ r) for r in (0, 2, 1, 3)]
        + [2 * ((dp + step) % 4) + slot for slot in slots for step in HEARD]
    ).astype(jnp.int32)

    def modes_of(value, start, count):
        return lax.dynamic_slice_in_dim(value, start, count, 0)

    with jax.named_scope("exchange_modes"):
        exchanged = []
        for shift in SHIFTS:
            start = 2 * ((dp + shift) % 4)
            packed = jnp.stack([modes_of(spectrum, start, 2), modes_of(out_grad, start, 2)])
            exchanged.append(ring(packed, "dp", shift))

    with jax.named_scope("gather_grad"):
        own, other = plane_gather(modes_of(out_grad, 4 * core, 4), modes_of(out_grad, 4 - 4 * core, 4))

    with jax.named_scope("gather_rows"):
        xs = jnp.stack([modes_of(spectrum, 2 * dp, 2)] + [block[0] for block in exchanged])
        xs_across = flip(xs, "cout", 2)
        xs_beside = flip(jnp.stack([xs, xs_across]), "cout", 1)

    with jax.named_scope("gather_late_grad"):
        late = jnp.stack([block[1] for block in exchanged], axis=1)
        late_own, late_other = plane_gather(
            modes_of(late, core, 1)[0], modes_of(late, 1 - core, 1)[0]
        )

    halves = []
    for half, held in enumerate((own, other)):
        keep, send = input_half(half, blocks, scalars, weight, held)
        with jax.named_scope("sum_input"):
            beside = flip(send, "cout", 1)
            across = flip(keep[1] + beside[1], "cout", 2)
            halves.append(((keep[0] + beside[0]) + across).astype(jnp.bfloat16))
    spectrum_grad = jnp.concatenate(
        [jnp.where(core == 0, halves[0], halves[1]), jnp.where(core == 0, halves[1], halves[0])], axis=0
    )

    parts = []
    for slot, held in enumerate((late_own, late_other)):
        mine = weight_mode(slot, blocks, scalars, own, other, held, (xs, xs_across, xs_beside))
        with jax.named_scope("spread_weight"):
            back, ahead = ring(mine, "dp", 1), ring(mine, "dp", 3)
            parts += [mine, back, ahead, ring(back[0], "dp", 1), ring(ahead[1], "dp", 3)]
    weight_grad = pl.pallas_call(
        place_modes,
        out_shape=jax.ShapeDtypeStruct(weight.shape, jnp.bfloat16),
        in_specs=[SMEM] + [ANY] * 10,
        out_specs=ANY,
        scratch_shapes=[pltpu.SemaphoreType.DMA],
        cost_estimate=pl.CostEstimate(flops=0, bytes_accessed=2 * MIB, transcendentals=0),
        name="place_modes",
    )(scalars, *parts)
    return (spectrum_grad, weight_grad)


def solution(mesh):
    placed = (
        P(None, None, "cin", "cout"),
        P(None, None, ("cin", "cout"), "dp"),
        P(None, None, ("cout", "cin"), "dp"),
    )
    return jax.shard_map(
        on_device,
        mesh=mesh,
        in_specs=placed,
        out_specs=(P(None, None, ("cin", "cout"), "dp"), P(None, None, "cin", "cout")),
        check_vma=False,
    )
```

time: 330 us -> 287 us (0.87)
  the two profiles are of different devices: /device:TPU:34 before, /device:TPU:1 now
where the time goes in v1:
time: 287 us; the launch traced here: 282 us
  starting transfers between devices  156 us (54%)
  waiting for transfers between devices  52 us (18%)
  Pallas kernels  48.1 us (17%)
  local copies, waits for them, and re-layouts  16.1 us (6%)
  other arithmetic  8.38 us (3%)
    ppermute x11, starting transfers between devices, ring(): return lax.ppermute(value, axis, [(i, (i + shift) % 4) for i in range(4)])  59.3 us
    ppermute x16, starting transfers between devices, flip(): return lax.ppermute(value, axis, [(i, i ^ bits) for i in range(size)])  57.2 us
    ppermute x12, starting transfers between devices, hop(): return lax.ppermute(value, 'cin', pairs)  39.2 us
    pallas_call x1, Pallas kernels, on_device(): pl.pallas_call(place_modes, out_shape=jax.ShapeDtypeStruct(weight.shape,...  33.5 us
    ppermute x16, waiting for transfers between devices, flip(): return lax.ppermute(value, axis, [(i, i ^ bits) for i in range(size)])  22.3 us
    ppermute x12, waiting for transfers between devices, hop(): return lax.ppermute(value, 'cin', pairs)  15.9 us
    ppermute x11, waiting for transfers between devices, ring(): return lax.ppermute(value, axis, [(i, (i + shift) % 4) for i in range(4)])  13.7 us
    pallas_call x2, Pallas kernels, weight_mode(): pl.pallas_call(functools.partial(weight_terms, slot), out_shape=jax.Shape...  9.17 us
  transfers between devices with their start and end apart: 39, of which 7 were waited for; matrix products, arithmetic and copies ran while one was open for 7% of the time, Pallas kernels for 17%

profile of v1, /device:TPU:1, one launch (start us, length us, event | category | flops | bytes accessed | tf_op | source)
XLA Modules:
  0.0 282.1 jit_solution(9119659521113636042)
XLA Ops:
  2.3 9.8 %collective-permute-start.15 = (bf16[2,2,2,16,512]{4,3,2,1,0:T(8,128)(2,1)S(1)}, bf16[2,2,2,16,512]{4,3,2,1,0:T(8,128)(2,1)S(1)}, u32[]{:S(2)}, u32[]{:S(2)}) collective-permute-start(bf16[2,2,2,16,512]{4,3,2,1,0:T(8,128)(2,1)S(1)} %pad_maximum_fusion.8), channel_id=1, source_target_pairs={{0,128},{128,256},{256,384},{384,0},{1,129},{129,257},{257,385},{3... | collective-permute-start | bytes 393224 | tf_op jit(solution)/shard_map/exchange_modes/ppermute | solution.py:19
  15.1 5.7 %collective-permute-start.16 = (bf16[2,2,2,16,512]{4,3,2,1,0:T(8,128)(2,1)S(1)}, bf16[2,2,2,16,512]{4,3,2,1,0:T(8,128)(2,1)S(1)}, u32[]{:S(2)}, u32[]{:S(2)}) collective-permute-start(bf16[2,2,2,16,512]{4,3,2,1,0:T(8,128)(2,1)S(1)} %pad_maximum_fusion.9), channel_id=1, source_target_pairs={{0,384},{128,0},{256,128},{384,256},{1,385},{129,1},{257,129},{385... | collective-permute-start | bytes 393224 | tf_op jit(solution)/shard_map/exchange_modes/ppermute | solution.py:19
  20.9 10.1 %collective-permute-start.17 = (bf16[2,2,2,16,512]{4,3,2,1,0:T(8,128)(2,1)S(1)}, bf16[2,2,2,16,512]{4,3,2,1,0:T(8,128)(2,1)S(1)}, u32[]{:S(2)}, u32[]{:S(2)}) collective-permute-start(bf16[2,2,2,16,512]{4,3,2,1,0:T(8,128)(2,1)S(1)} %pad_maximum_fusion.10), channel_id=1, source_target_pairs={{0,256},{128,384},{256,0},{384,128},{1,257},{129,385},{257,1},{385... | collective-permute-start | bytes 393224 | tf_op jit(solution)/shard_map/exchange_modes/ppermute | solution.py:19
  34.3 5.9 %collective-permute-done.16 = bf16[2,2,2,16,512]{4,3,2,1,0:T(8,128)(2,1)S(1)} collective-permute-done((bf16[2,2,2,16,512]{4,3,2,1,0:T(8,128)(2,1)S(1)}, bf16[2,2,2,16,512]{4,3,2,1,0:T(8,128)(2,1)S(1)}, u32[]{:S(2)}, u32[]{:S(2)}) %collective-permute-start.16) | collective-permute-done | bytes 131104 | tf_op jit(solution)/shard_map/exchange_modes/ppermute | solution.py:19
  43.6 4.8 %collective-permute-start.2 = (bf16[2,4,2,16,512]{4,3,2,1,0:T(8,128)(2,1)S(1)}, bf16[2,4,2,16,512]{4,3,2,1,0:T(8,128)(2,1)S(1)}, u32[]{:S(2)}, u32[]{:S(2)}) collective-permute-start(bf16[2,4,2,16,512]{4,3,2,1,0:T(8,128)(2,1)S(1)} %get-tuple-element.23), channel_id=1, source_target_pairs={{0,24},{4,100},{8,0},{12,108},{16,8},{20,116},{24,16},{28,124},{32... | collective-permute-start | bytes 786440 | tf_op jit(solution)/shard_map/gather_grad/ppermute | solution.py:39
  54.0 3.9 %collective-permute-start.20 = (bf16[2,3,2,16,512]{4,3,2,0,1:T(8,128)(2,1)}, bf16[2,3,2,16,512]{4,3,2,0,1:T(8,128)(2,1)}, u32[]{:S(2)}, u32[]{:S(2)}) collective-permute-start(bf16[2,3,2,16,512]{4,3,2,0,1:T(8,128)(2,1)} %get-tuple-element.27), channel_id=1, source_target_pairs={{0,24},{4,100},{8,0},{12,108},{16,8},{20,116},{24,16},{28,124},{32... | collective-permute-start | bytes 589832 | tf_op jit(solution)/shard_map/gather_late_grad/ppermute | solution.py:39
  64.5 3.4 %collective-permute-start.5 = (bf16[4,2,4,2,16,512]{5,4,3,2,1,0:T(8,128)(2,1)S(1)}, bf16[4,2,4,2,16,512]{5,4,3,2,1,0:T(8,128)(2,1)S(1)}, u32[]{:S(2)}, u32[]{:S(2)}) collective-permute-start(bf16[4,2,4,2,16,512]{5,4,3,2,1,0:T(8,128)(2,1)S(1)} %pad_maximum_fusion.p0.refs_0_), channel_id=1, source_target_pairs={{0,96},{4,28},{8,104},{12,4},{16,112},{20,12},{24,120},{28,20},{32... | collective-permute-start | bytes 3145736 | tf_op jit(solution)/shard_map/gather_grad/ppermute | solution.py:39
  67.9 3.4 %collective-permute-start.6 = (bf16[4,2,4,2,16,512]{5,4,3,2,1,0:T(8,128)(2,1)S(1)}, bf16[4,2,4,2,16,512]{5,4,3,2,1,0:T(8,128)(2,1)}, u32[]{:S(2)}, u32[]{:S(2)}) collective-permute-start(bf16[4,2,4,2,16,512]{5,4,3,2,1,0:T(8,128)(2,1)S(1)} %pad_maximum_fusion.p0.refs_0_), channel_id=1, source_target_pairs={{0,64},{4,20},{8,72},{12,28},{16,80},{20,4},{24,88},{28,12},{32,96... | collective-permute-start | bytes 3145736 | tf_op jit(solution)/shard_map/gather_grad/ppermute | solution.py:39
  76.7 4.3 %collective-permute-start.23 = (bf16[4,2,3,2,16,512]{5,4,3,1,2,0:T(8,128)(2,1)}, bf16[4,2,3,2,16,512]{5,4,3,1,2,0:T(8,128)(2,1)}, u32[]{:S(2)}, u32[]{:S(2)}) collective-permute-start(bf16[4,2,3,2,16,512]{5,4,3,1,2,0:T(8,128)(2,1)} %pad_maximum_fusion.1), channel_id=1, source_target_pairs={{0,96},{4,28},{8,104},{12,4},{16,112},{20,12},{24,120},{28,20},{32... | collective-permute-start | bytes 2359304 | tf_op jit(solution)/shard_map/gather_late_grad/ppermute | solution.py:39
  83.3 15.9 %collective-permute-done.22 = bf16[4,2,3,2,16,512]{5,4,3,1,2,0:T(8,128)(2,1)} collective-permute-done((bf16[4,2,3,2,16,512]{5,4,3,1,2,0:T(8,128)(2,1)}, bf16[4,2,3,2,16,512]{5,4,3,1,2,0:T(8,128)(2,1)}, u32[]{:S(2)}, u32[]{:S(2)}) %collective-permute-start.22) | collective-permute-done | bytes 786464 | tf_op jit(solution)/shard_map/gather_late_grad/ppermute | solution.py:39
  103.6 7.0 %collective-permute-start.25 = (bf16[4,2,2,16,512]{4,3,2,1,0:T(8,128)(2,1)S(1)}, bf16[4,2,2,16,512]{4,3,2,1,0:T(8,128)(2,1)}, u32[]{:S(2)}, u32[]{:S(2)}) collective-permute-start(bf16[4,2,2,16,512]{4,3,2,1,0:T(8,128)(2,1)S(1)} %get-tuple-element.14.refs_12_), channel_id=1, source_target_pairs={{0,2},{1,3},{2,0},{3,1},{4,6},{5,7},{6,4},{7,5},{8,10},{9,11},{10,... | collective-permute-start | bytes 786440 | tf_op jit(solution)/shard_map/gather_rows/ppermute | solution.py:23
  110.6 4.4 %collective-permute-start.31 = (bf16[4,2,3,2,16,512]{5,4,3,1,2,0:T(8,128)(2,1)}, bf16[4,2,3,2,16,512]{5,4,3,1,2,0:T(8,128)(2,1)}, u32[]{:S(2)}, u32[]{:S(2)}) collective-permute-start(bf16[4,2,3,2,16,512]{5,4,3,1,2,0:T(8,128)(2,1)} %pad_maximum_fusion.1), channel_id=1, source_target_pairs={{0,4},{4,0},{8,12},{12,8},{16,20},{20,16},{24,28},{28,24},{32,36},... | collective-permute-start | bytes 2359304 | tf_op jit(solution)/shard_map/gather_late_grad/ppermute | solution.py:23
  124.2 10.9 %collective-permute-start.7 = (f32[2,4,2,16,512]{4,3,2,1,0:T(8,128)S(1)}, f32[2,4,2,16,512]{4,3,2,1,0:T(8,128)S(1)}, u32[]{:S(2)}, u32[]{:S(2)}) collective-permute-start(f32[2,4,2,16,512]{4,3,2,1,0:T(8,128)S(1)} %get-tuple-element.7), channel_id=1, source_target_pairs={{0,1},{1,0},{2,3},{3,2},{4,5},{5,4},{6,7},{7,6},{8,9},{9,8},{10,11... | collective-permute-start | bytes 1572872 | tf_op jit(solution)/shard_map/sum_input/ppermute | solution.py:23
  139.5 7.9 %collective-permute-done.7 = f32[2,4,2,16,512]{4,3,2,1,0:T(8,128)S(1)} collective-permute-done((f32[2,4,2,16,512]{4,3,2,1,0:T(8,128)S(1)}, f32[2,4,2,16,512]{4,3,2,1,0:T(8,128)S(1)}, u32[]{:S(2)}, u32[]{:S(2)}) %collective-permute-start.7) | collective-permute-done | bytes 524320 | tf_op jit(solution)/shard_map/sum_input/ppermute | solution.py:23
  172.7 4.6 %weight_terms.3.refs_5_ = bf16[2,64,512]{2,1,0:T(8,128)(2,1)S(1)} custom-call(s32[2,32]{1,0:T(2,128)S(1)} %pad_add_fusion.blocks, s32[23]{0:T(128)S(1)} %stack.177.scalars, bf16[4,2,4,2,16,512]{5,4,3,2,1,0:T(8,128)(2,1)S(1)} %pad_maximum_fusion.p0.refs_0_, bf16[4,2,4,2,16,512]{5,4,3,2,1,0:T(8,128)(2,1)S(1)} %collective-permute-done.4.p1.refs_1_, ...), custom_call_target="tpu_custom_call" | custom-call | flops 1073741824 | bytes 5242880 | tf_op jit(solution)/shard_map/weight_terms/pallas_call | solution.py:166
  179.2 7.3 %collective-permute-start.36 = (bf16[2,64,512]{2,1,0:T(8,128)(2,1)S(1)}, bf16[2,64,512]{2,1,0:T(8,128)(2,1)S(1)}, u32[]{:S(2)}, u32[]{:S(2)}) collective-permute-start(bf16[2,64,512]{2,1,0:T(8,128)(2,1)S(1)} %weight_terms.3.refs_5_), channel_id=1, source_target_pairs={{0,384},{128,0},{256,128},{384,256},{1,385},{129,1},{257,129},{385... | collective-permute-start | bytes 393224 | tf_op jit(solution)/shard_map/spread_weight/ppermute | solution.py:19
  186.5 4.6 %weight_terms.2.refs_0_ = bf16[2,64,512]{2,1,0:T(8,128)(2,1)S(1)} custom-call(s32[2,32]{1,0:T(2,128)S(1)} %pad_add_fusion.blocks, s32[23]{0:T(128)S(1)} %stack.177.scalars, bf16[4,2,4,2,16,512]{5,4,3,2,1,0:T(8,128)(2,1)S(1)} %pad_maximum_fusion.p0.refs_0_, bf16[4,2,4,2,16,512]{5,4,3,2,1,0:T(8,128)(2,1)S(1)} %collective-permute-done.4.p1.refs_1_, ...), custom_call_target="tpu_custom_call" | custom-call | flops 1073741824 | bytes 5242880 | tf_op jit(solution)/shard_map/weight_terms/pallas_call | solution.py:166
  193.0 7.3 %collective-permute-start.28 = (bf16[2,64,512]{2,1,0:T(8,128)(2,1)S(1)}, bf16[2,64,512]{2,1,0:T(8,128)(2,1)S(1)}, u32[]{:S(2)}, u32[]{:S(2)}) collective-permute-start(bf16[2,64,512]{2,1,0:T(8,128)(2,1)S(1)} %weight_terms.2.refs_0_), channel_id=1, source_target_pairs={{0,384},{128,0},{256,128},{384,256},{1,385},{129,1},{257,129},{385... | collective-permute-start | bytes 393224 | tf_op jit(solution)/shard_map/spread_weight/ppermute | solution.py:19
  208.6 6.5 %collective-permute-start.38 = (bf16[64,512]{1,0:T(8,128)(2,1)S(1)}, bf16[64,512]{1,0:T(8,128)(2,1)S(1)}, u32[]{:S(2)}, u32[]{:S(2)}) collective-permute-start(bf16[64,512]{1,0:T(8,128)(2,1)S(1)} %slice_bitcast_fusion), channel_id=1, source_target_pairs={{0,384},{128,0},{256,128},{384,256},{1,385},{129,1},{257,129},{385... | collective-permute-start | bytes 196616 | tf_op jit(solution)/shard_map/spread_weight/ppermute | solution.py:19
  215.2 11.5 %collective-permute-done.13 = f32[2,4,2,16,512]{4,3,2,1,0:T(8,128)S(1)} collective-permute-done((f32[2,4,2,16,512]{4,3,2,1,0:T(8,128)S(1)}, f32[2,4,2,16,512]{4,3,2,1,0:T(8,128)S(1)}, u32[]{:S(2)}, u32[]{:S(2)}) %collective-permute-start.13) | collective-permute-done | bytes 524320 | tf_op jit(solution)/shard_map/sum_input/ppermute | solution.py:23
  229.4 5.2 %collective-permute-start.14 = (f32[4,2,16,512]{3,2,1,0:T(8,128)S(1)}, f32[4,2,16,512]{3,2,1,0:T(8,128)S(1)}, u32[]{:S(2)}, u32[]{:S(2)}) collective-permute-start(f32[4,2,16,512]{3,2,1,0:T(8,128)S(1)} %fusion), channel_id=1, source_target_pairs={{0,2},{1,3},{2,0},{3,1},{4,6},{5,7},{6,4},{7,5},{8,10},{9,11},{10,... | collective-permute-start | bytes 786440 | tf_op jit(solution)/shard_map/sum_input/ppermute | solution.py:23
  234.8 4.2 %collective-permute-start.30 = (bf16[64,512]{1,0:T(8,128)(2,1)S(1)}, bf16[64,512]{1,0:T(8,128)(2,1)S(1)}, u32[]{:S(2)}, u32[]{:S(2)}) collective-permute-start(bf16[64,512]{1,0:T(8,128)(2,1)S(1)} %slice_bitcast_fusion.2), channel_id=1, source_target_pairs={{0,384},{128,0},{256,128},{384,256},{1,385},{129,1},{257,129},{385... | collective-permute-start | bytes 196616 | tf_op jit(solution)/shard_map/spread_weight/ppermute | solution.py:19
  239.0 7.0 %collective-permute-done.30.refs_4_ = bf16[64,512]{1,0:T(8,128)(2,1)S(1)} collective-permute-done((bf16[64,512]{1,0:T(8,128)(2,1)S(1)}, bf16[64,512]{1,0:T(8,128)(2,1)S(1)}, u32[]{:S(2)}, u32[]{:S(2)}) %collective-permute-start.30) | collective-permute-done | bytes 65568 | tf_op jit(solution)/shard_map/spread_weight/ppermute | solution.py:19
  246.7 33.5 %place_modes.1 = bf16[8,2,64,512]{3,2,1,0:T(8,128)(2,1)} custom-call(s32[23]{0:T(128)} %copy-done.5, bf16[2,64,512]{2,1,0:T(8,128)(2,1)} %copy-done.2, bf16[2,64,512]{2,1,0:T(8,128)(2,1)} %copy-done.12, bf16[2,64,512]{2,1,0:T(8,128)(2,1)} %copy-done.13, bf16[64,512]{1,0:T(8,128)(2,1)} %copy-done.17, bf16[64,512]{1,0:T(8,128)(2,1)} %copy-done.18, ...), custom_call_target="tpu_custom_call" | custom-call | bytes 2097152 | tf_op jit(solution)/shard_map/place_modes/pallas_call | solution.py:253
  (154 shorter events, 91.2 us)
Async XLA Ops:
  2.3 31.9 %collective-permute-start.15 = (bf16[2,2,2,16,512]{4,3,2,1,0:T(8,128)(2,1)S(1)}, bf16[2,2,2,16,512]{4,3,2,1,0:T(8,128)(2,1)S(1)}, u32[]{:S(2)}, u32[]{:S(2)}) collective-permute-start(bf16[2,2,2,16,512]{4,3,2,1,0:T(8,128)(2,1)S(1)} %pad_maximum_fusion.8), channel_id=1, source_target_pairs={{0,128},{128,256},{256,384},{384,0},{1,129},{129,257},{257,385},{3... | collective-permute-start | bytes 393224 | tf_op jit(solution)/shard_map/exchange_modes/ppermute | solution.py:19
  15.1 25.1 %collective-permute-start.16 = (bf16[2,2,2,16,512]{4,3,2,1,0:T(8,128)(2,1)S(1)}, bf16[2,2,2,16,512]{4,3,2,1,0:T(8,128)(2,1)S(1)}, u32[]{:S(2)}, u32[]{:S(2)}) collective-permute-start(bf16[2,2,2,16,512]{4,3,2,1,0:T(8,128)(2,1)S(1)} %pad_maximum_fusion.9), channel_id=1, source_target_pairs={{0,384},{128,0},{256,128},{384,256},{1,385},{129,1},{257,129},{385... | collective-permute-start | bytes 393224 | tf_op jit(solution)/shard_map/exchange_modes/ppermute | solution.py:19
  31.0 26.8 %collective-permute-start.1 = (bf16[2,4,2,16,512]{4,3,2,1,0:T(8,128)(2,1)S(1)}, bf16[2,4,2,16,512]{4,3,2,1,0:T(8,128)(2,1)S(1)}, u32[]{:S(2)}, u32[]{:S(2)}) collective-permute-start(bf16[2,4,2,16,512]{4,3,2,1,0:T(8,128)(2,1)S(1)} %get-tuple-element.23), channel_id=1, source_target_pairs={{0,8},{4,36},{8,16},{12,44},{16,24},{20,52},{24,0},{28,60},{32,40}... | collective-permute-start | bytes 786440 | tf_op jit(solution)/shard_map/gather_grad/ppermute | solution.py:39
  61.4 49.2 %collective-permute-start.4 = (bf16[4,2,4,2,16,512]{5,4,3,2,1,0:T(8,128)(2,1)S(1)}, bf16[4,2,4,2,16,512]{5,4,3,2,1,0:T(8,128)(2,1)S(1)}, u32[]{:S(2)}, u32[]{:S(2)}) collective-permute-start(bf16[4,2,4,2,16,512]{5,4,3,2,1,0:T(8,128)(2,1)S(1)} %pad_maximum_fusion.p0.refs_0_), channel_id=1, source_target_pairs={{0,32},{4,12},{8,40},{12,20},{16,48},{20,28},{24,56},{28,4},{32,64... | collective-permute-start | bytes 3145736 | tf_op jit(solution)/shard_map/gather_grad/ppermute | solution.py:39
  64.5 50.4 %collective-permute-start.5 = (bf16[4,2,4,2,16,512]{5,4,3,2,1,0:T(8,128)(2,1)S(1)}, bf16[4,2,4,2,16,512]{5,4,3,2,1,0:T(8,128)(2,1)S(1)}, u32[]{:S(2)}, u32[]{:S(2)}) collective-permute-start(bf16[4,2,4,2,16,512]{5,4,3,2,1,0:T(8,128)(2,1)S(1)} %pad_maximum_fusion.p0.refs_0_), channel_id=1, source_target_pairs={{0,96},{4,28},{8,104},{12,4},{16,112},{20,12},{24,120},{28,20},{32... | collective-permute-start | bytes 3145736 | tf_op jit(solution)/shard_map/gather_grad/ppermute | solution.py:39
  67.9 49.0 %collective-permute-start.6 = (bf16[4,2,4,2,16,512]{5,4,3,2,1,0:T(8,128)(2,1)S(1)}, bf16[4,2,4,2,16,512]{5,4,3,2,1,0:T(8,128)(2,1)}, u32[]{:S(2)}, u32[]{:S(2)}) collective-permute-start(bf16[4,2,4,2,16,512]{5,4,3,2,1,0:T(8,128)(2,1)S(1)} %pad_maximum_fusion.p0.refs_0_), channel_id=1, source_target_pairs={{0,64},{4,20},{8,72},{12,28},{16,80},{20,4},{24,88},{28,12},{32,96... | collective-permute-start | bytes 3145736 | tf_op jit(solution)/shard_map/gather_grad/ppermute | solution.py:39
  73.5 25.7 %collective-permute-start.22 = (bf16[4,2,3,2,16,512]{5,4,3,1,2,0:T(8,128)(2,1)}, bf16[4,2,3,2,16,512]{5,4,3,1,2,0:T(8,128)(2,1)}, u32[]{:S(2)}, u32[]{:S(2)}) collective-permute-start(bf16[4,2,3,2,16,512]{5,4,3,1,2,0:T(8,128)(2,1)} %pad_maximum_fusion.1), channel_id=1, source_target_pairs={{0,32},{4,12},{8,40},{12,20},{16,48},{20,28},{24,56},{28,4},{32,64... | collective-permute-start | bytes 2359304 | tf_op jit(solution)/shard_map/gather_late_grad/ppermute | solution.py:39
  76.7 26.9 %collective-permute-start.23 = (bf16[4,2,3,2,16,512]{5,4,3,1,2,0:T(8,128)(2,1)}, bf16[4,2,3,2,16,512]{5,4,3,1,2,0:T(8,128)(2,1)}, u32[]{:S(2)}, u32[]{:S(2)}) collective-permute-start(bf16[4,2,3,2,16,512]{5,4,3,1,2,0:T(8,128)(2,1)} %pad_maximum_fusion.1), channel_id=1, source_target_pairs={{0,96},{4,28},{8,104},{12,4},{16,112},{20,12},{24,120},{28,20},{32... | collective-permute-start | bytes 2359304 | tf_op jit(solution)/shard_map/gather_late_grad/ppermute | solution.py:39
  99.2 35.9 %collective-permute-start.24 = (bf16[4,2,3,2,16,512]{5,4,3,1,2,0:T(8,128)(2,1)}, bf16[4,2,3,2,16,512]{5,4,3,1,2,0:T(8,128)(2,1)}, u32[]{:S(2)}, u32[]{:S(2)}) collective-permute-start(bf16[4,2,3,2,16,512]{5,4,3,1,2,0:T(8,128)(2,1)} %pad_maximum_fusion.1), channel_id=1, source_target_pairs={{0,64},{4,20},{8,72},{12,28},{16,80},{20,4},{24,88},{28,12},{32,96... | collective-permute-start | bytes 2359304 | tf_op jit(solution)/shard_map/gather_late_grad/ppermute | solution.py:39
  110.6 26.8 %collective-permute-start.31 = (bf16[4,2,3,2,16,512]{5,4,3,1,2,0:T(8,128)(2,1)}, bf16[4,2,3,2,16,512]{5,4,3,1,2,0:T(8,128)(2,1)}, u32[]{:S(2)}, u32[]{:S(2)}) collective-permute-start(bf16[4,2,3,2,16,512]{5,4,3,1,2,0:T(8,128)(2,1)} %pad_maximum_fusion.1), channel_id=1, source_target_pairs={{0,4},{4,0},{8,12},{12,8},{16,20},{20,16},{24,28},{28,24},{32,36},... | collective-permute-start | bytes 2359304 | tf_op jit(solution)/shard_map/gather_late_grad/ppermute | solution.py:23
  115.0 34.9 %collective-permute-start.32 = (bf16[4,2,3,2,16,512]{5,4,3,1,2,0:T(8,128)(2,1)}, bf16[4,2,3,2,16,512]{5,4,3,1,2,0:T(8,128)(2,1)}, u32[]{:S(2)}, u32[]{:S(2)}) collective-permute-start(bf16[4,2,3,2,16,512]{5,4,3,1,2,0:T(8,128)(2,1)} %collective-permute-done.22), channel_id=1, source_target_pairs={{0,4},{4,0},{8,12},{12,8},{16,20},{20,16},{24,28},{28,24},{32,36},... | collective-permute-start | bytes 2359304 | tf_op jit(solution)/shard_map/gather_late_grad/ppermute | solution.py:23
  116.9 34.9 %collective-permute-start.33 = (bf16[4,2,3,2,16,512]{5,4,3,1,2,0:T(8,128)(2,1)}, bf16[4,2,3,2,16,512]{5,4,3,1,2,0:T(8,128)(2,1)}, u32[]{:S(2)}, u32[]{:S(2)}) collective-permute-start(bf16[4,2,3,2,16,512]{5,4,3,1,2,0:T(8,128)(2,1)} %collective-permute-done.23), channel_id=1, source_target_pairs={{0,4},{4,0},{8,12},{12,8},{16,20},{20,16},{24,28},{28,24},{32,36},... | collective-permute-start | bytes 2359304 | tf_op jit(solution)/shard_map/gather_late_grad/ppermute | solution.py:23
  124.2 23.2 %collective-permute-start.7 = (f32[2,4,2,16,512]{4,3,2,1,0:T(8,128)S(1)}, f32[2,4,2,16,512]{4,3,2,1,0:T(8,128)S(1)}, u32[]{:S(2)}, u32[]{:S(2)}) collective-permute-start(f32[2,4,2,16,512]{4,3,2,1,0:T(8,128)S(1)} %get-tuple-element.7), channel_id=1, source_target_pairs={{0,1},{1,0},{2,3},{3,2},{4,5},{5,4},{6,7},{7,6},{8,9},{9,8},{10,11... | collective-permute-start | bytes 1572872 | tf_op jit(solution)/shard_map/sum_input/ppermute | solution.py:23
  137.3 35.3 %collective-permute-start.9 = (bf16[4,2,4,2,16,512]{5,4,3,2,1,0:T(8,128)(2,1)S(1)}, bf16[4,2,4,2,16,512]{5,4,3,2,1,0:T(8,128)(2,1)S(1)}, u32[]{:S(2)}, u32[]{:S(2)}) collective-permute-start(bf16[4,2,4,2,16,512]{5,4,3,2,1,0:T(8,128)(2,1)S(1)} %pad_maximum_fusion.p0.refs_0_), channel_id=1, source_target_pairs={{0,4},{4,0},{8,12},{12,8},{16,20},{20,16},{24,28},{28,24},{32,36},... | collective-permute-start | bytes 3145736 | tf_op jit(solution)/shard_map/gather_grad/ppermute | solution.py:23
  147.4 25.3 %collective-permute-start.10 = (bf16[4,2,4,2,16,512]{5,4,3,2,1,0:T(8,128)(2,1)S(1)}, bf16[4,2,4,2,16,512]{5,4,3,2,1,0:T(8,128)(2,1)S(1)}, u32[]{:S(2)}, u32[]{:S(2)}) collective-permute-start(bf16[4,2,4,2,16,512]{5,4,3,2,1,0:T(8,128)(2,1)S(1)} %collective-permute-done.4.p1.refs_1_), channel_id=1, source_target_pairs={{0,4},{4,0},{8,12},{12,8},{16,20},{20,16},{24,28},{28,24},{32,36},... | collective-permute-start | bytes 3145736 | tf_op jit(solution)/shard_map/gather_grad/ppermute | solution.py:23
  149.9 22.8 %collective-permute-start.11 = (bf16[4,2,4,2,16,512]{5,4,3,2,1,0:T(8,128)(2,1)S(1)}, bf16[4,2,4,2,16,512]{5,4,3,2,1,0:T(8,128)(2,1)S(1)}, u32[]{:S(2)}, u32[]{:S(2)}) collective-permute-start(bf16[4,2,4,2,16,512]{5,4,3,2,1,0:T(8,128)(2,1)S(1)} %collective-permute-done.5.p2.refs_2_), channel_id=1, source_target_pairs={{0,4},{4,0},{8,12},{12,8},{16,20},{20,16},{24,28},{28,24},{32,36},... | collective-permute-start | bytes 3145736 | tf_op jit(solution)/shard_map/gather_grad/ppermute | solution.py:23
  170.7 109.5 %collective-permute-start.8 = (f32[4,2,16,512]{3,2,1,0:T(8,128)}, f32[4,2,16,512]{3,2,1,0:T(8,128)}, u32[]{:S(2)}, u32[]{:S(2)}) collective-permute-start(f32[4,2,16,512]{3,2,1,0:T(8,128)} %fusion.4), channel_id=1, source_target_pairs={{0,2},{1,3},{2,0},{3,1},{4,6},{5,7},{6,4},{7,5},{8,10},{9,11},{10,... | collective-permute-start | bytes 786440 | tf_op jit(solution)/shard_map/sum_input/ppermute | solution.py:23
  177.3 25.2 %collective-permute-start.35 = (bf16[2,64,512]{2,1,0:T(8,128)(2,1)S(1)}, bf16[2,64,512]{2,1,0:T(8,128)(2,1)S(1)}, u32[]{:S(2)}, u32[]{:S(2)}) collective-permute-start(bf16[2,64,512]{2,1,0:T(8,128)(2,1)S(1)} %weight_terms.3.refs_5_), channel_id=1, source_target_pairs={{0,128},{128,256},{256,384},{384,0},{1,129},{129,257},{257,385},{3... | collective-permute-start | bytes 393224 | tf_op jit(solution)/shard_map/spread_weight/ppermute | solution.py:19
  179.2 26.7 %collective-permute-start.36 = (bf16[2,64,512]{2,1,0:T(8,128)(2,1)S(1)}, bf16[2,64,512]{2,1,0:T(8,128)(2,1)S(1)}, u32[]{:S(2)}, u32[]{:S(2)}) collective-permute-start(bf16[2,64,512]{2,1,0:T(8,128)(2,1)S(1)} %weight_terms.3.refs_5_), channel_id=1, source_target_pairs={{0,384},{128,0},{256,128},{384,256},{1,385},{129,1},{257,129},{385... | collective-permute-start | bytes 393224 | tf_op jit(solution)/shard_map/spread_weight/ppermute | solution.py:19
  193.0 36.4 %collective-permute-start.28 = (bf16[2,64,512]{2,1,0:T(8,128)(2,1)S(1)}, bf16[2,64,512]{2,1,0:T(8,128)(2,1)S(1)}, u32[]{:S(2)}, u32[]{:S(2)}) collective-permute-start(bf16[2,64,512]{2,1,0:T(8,128)(2,1)S(1)} %weight_terms.2.refs_0_), channel_id=1, source_target_pairs={{0,384},{128,0},{256,128},{384,256},{1,385},{129,1},{257,129},{385... | collective-permute-start | bytes 393224 | tf_op jit(solution)/shard_map/spread_weight/ppermute | solution.py:19
  202.5 24.1 %collective-permute-start.13 = (f32[2,4,2,16,512]{4,3,2,1,0:T(8,128)S(1)}, f32[2,4,2,16,512]{4,3,2,1,0:T(8,128)S(1)}, u32[]{:S(2)}, u32[]{:S(2)}) collective-permute-start(f32[2,4,2,16,512]{4,3,2,1,0:T(8,128)S(1)} %get-tuple-element.9), channel_id=1, source_target_pairs={{0,1},{1,0},{2,3},{3,2},{4,5},{5,4},{6,7},{7,6},{8,9},{9,8},{10,11... | collective-permute-start | bytes 1572872 | tf_op jit(solution)/shard_map/sum_input/ppermute | solution.py:23
  205.9 28.8 %collective-permute-start.37 = (bf16[64,512]{1,0:T(8,128)(2,1)S(1)}, bf16[64,512]{1,0:T(8,128)(2,1)S(1)}, u32[]{:S(2)}, u32[]{:S(2)}) collective-permute-start(bf16[64,512]{1,0:T(8,128)(2,1)S(1)} %slice_bitcast_fusion.1), channel_id=1, source_target_pairs={{0,128},{128,256},{256,384},{384,0},{1,129},{129,257},{257,385},{3... | collective-permute-start | bytes 196616 | tf_op jit(solution)/shard_map/spread_weight/ppermute | solution.py:19
  208.6 30.3 %collective-permute-start.38 = (bf16[64,512]{1,0:T(8,128)(2,1)S(1)}, bf16[64,512]{1,0:T(8,128)(2,1)S(1)}, u32[]{:S(2)}, u32[]{:S(2)}) collective-permute-start(bf16[64,512]{1,0:T(8,128)(2,1)S(1)} %slice_bitcast_fusion), channel_id=1, source_target_pairs={{0,384},{128,0},{256,128},{384,256},{1,385},{129,1},{257,129},{385... | collective-permute-start | bytes 196616 | tf_op jit(solution)/shard_map/spread_weight/ppermute | solution.py:19
  229.4 50.8 %collective-permute-start.14 = (f32[4,2,16,512]{3,2,1,0:T(8,128)S(1)}, f32[4,2,16,512]{3,2,1,0:T(8,128)S(1)}, u32[]{:S(2)}, u32[]{:S(2)}) collective-permute-start(f32[4,2,16,512]{3,2,1,0:T(8,128)S(1)} %fusion), channel_id=1, source_target_pairs={{0,2},{1,3},{2,0},{3,1},{4,6},{5,7},{6,4},{7,5},{8,10},{9,11},{10,... | collective-permute-start | bytes 786440 | tf_op jit(solution)/shard_map/sum_input/ppermute | solution.py:23
  (35 other events, 626.2 us)

commit v2 on v0

v2 whole, which is shorter than its diff:
```python
import jax
import jax.numpy as jnp
from jax import lax
from jax.experimental import pallas as pl
from jax.experimental.pallas import tpu as pltpu
from jax.sharding import PartitionSpec as P

HEARD = (0, 3, 1, 2)
SHIFTS = (1, 3, 2)
TREE = (0, 2, 1, 3)
MIB = 1 << 20
ANY = pl.BlockSpec(memory_space=pl.ANY)
SMEM = pl.BlockSpec(memory_space=pltpu.SMEM)
VMEM = pl.BlockSpec(memory_space=pltpu.VMEM)


def ring(value, axis, shift):
    return lax.ppermute(value, axis, [(i, (i + shift) % 4) for i in range(4)])


def flip(value, axis, bits, size=4):
    return lax.ppermute(value, axis, [(i, i ^ bits) for i in range(size)])


def swap_cores(value):
    return flip(value, "cin", 1, 32)


def hop(value, shift, stage):
    pairs = []
    for i in range(32):
        y, x, core = i // 8, (i // 2) % 4, i % 2
        if core == stage:
            x = (x + shift) % 4
        else:
            y = (y + shift) % 4
        pairs.append((i, (y * 4 + x) * 2 + core))
    return lax.ppermute(value, "cin", pairs)


def plane_blocks(y, x, core):
    heard = jnp.array(HEARD, jnp.int32)
    along_x = (x + heard) % 4
    along_y = (y + heard) % 4
    blocks = []
    for second in range(4):
        for first in range(4):
            for source in range(2):
                across = jnp.where(core == 0, along_x[first], along_x[second])
                down = jnp.where(core == 0, along_y[second], along_y[first])
                blocks.append((down * 4 + across) * 2 + (core ^ source))
    return blocks


def fetch_plane(blocks, pieces, target, sem):
    for second in range(4):
        for first in range(4):
            for source in range(2):
                row = pl.multiple_of(blocks[(second * 4 + first) * 2 + source] * 16, 16)
                pltpu.make_async_copy(
                    pieces[second](first, source), target(pl.ds(row, 16)), sem
                ).start()


def input_terms(blocks, scalars, w, w_other, p0, p1, p2, p3, keep, send, grads, sem):
    fetch_plane(
        blocks,
        [lambda first, source, p=p: p.at[first, source] for p in (p0, p1, p2, p3)],
        lambda rows: grads.at[:, :, rows, :],
        sem,
    )
    base = scalars[0]
    rows = [pl.ds(pl.multiple_of(scalars[2 + r], 16), 16) for r in range(4)]
    pltpu.make_async_copy(grads, grads, sem).wait()
    for mode in range(4):
        real, imag = (
            jnp.concatenate(
                [block for row in rows for block in (w[base + mode, part, row, :], w_other[mode, part, row, :])],
                axis=0,
            )
            for part in range(2)
        )
        total = jnp.dot(
            jnp.concatenate([real, -imag], axis=0), grads[mode, 0], preferred_element_type=jnp.float32
        ) + jnp.dot(
            jnp.concatenate([imag, real], axis=0), grads[mode, 1], preferred_element_type=jnp.float32
        )
        total = total.reshape(2, 4, 2, 16, 512)
        for part in range(2):
            for r in range(2):
                keep[r, mode, part] = total[part, r]
                send[r, mode, part] = total[part, r + 2]


def weight_terms(blocks, scalars, p0, p1, p2, p3, l0, l1, l2, l3, x0, x1, x2, out, grads, rows, sem):
    mode = scalars[1]
    fetch_plane(
        blocks,
        [lambda first, source, p=p: p.at[first, source, mode] for p in (p0, p1, p2, p3)],
        lambda place: grads.at[0, :, place, :],
        sem,
    )
    for index, piece in enumerate((x0, x1, x2.at[0], x2.at[1])):
        for source in range(2):
            row = pl.multiple_of(scalars[2 + index] + 64 * source, 16)
            pltpu.make_async_copy(piece.at[source], rows.at[:, :, pl.ds(row, 16), :], sem).start()
    fetch_plane(
        blocks,
        [lambda first, source, p=p: p.at[first, source] for p in (l0, l1, l2, l3)],
        lambda place: grads.at[pl.ds(1, 3), :, place, :],
        sem,
    )
    pltpu.make_async_copy(grads, grads, sem).wait()
    pltpu.make_async_copy(rows, rows, sem).wait()

    total = jnp.zeros((256, 512), jnp.float32)
    contract = (((1,), (1,)), ((), ()))
    for block in range(4):
        real = rows[block, 0]
        imag = rows[block, 1]
        total += lax.dot_general(
            jnp.concatenate([real, -imag], axis=0), grads[block, 0], contract, preferred_element_type=jnp.float32
        )
        total += lax.dot_general(
            jnp.concatenate([imag, real], axis=0), grads[block, 1], contract, preferred_element_type=jnp.float32
        )
    for part in range(2):
        for source in range(2):
            start = part * 128 + source * 64
            out[source, part] = total[start : start + 64].astype(jnp.bfloat16)


def place_modes(scalars, own, back, ahead, far, out, sem):
    for step, piece in enumerate((own, back, ahead, far)):
        for slot in range(2):
            pltpu.make_async_copy(piece.at[slot], out.at[scalars[6 + 2 * step + slot]], sem).start()
    pltpu.make_async_copy(out, out, sem).wait()


def on_device(weight, spectrum, out_grad):
    dp, place, cout = lax.axis_index("dp"), lax.axis_index("cin"), lax.axis_index("cout")
    core = place % 2
    blocks = jnp.stack(plane_blocks(place // 8, (place // 2) % 4, core)).astype(jnp.int32)
    scalars = jnp.stack(
        [4 * core, dp]
        + [16 * (cout ^ r) for r in TREE]
        + [4 * (core ^ slot) + (dp + step) % 4 for step in HEARD for slot in range(2)]
    ).astype(jnp.int32)

    def modes_of(value, start, count):
        return lax.dynamic_slice_in_dim(value, start, count, 0)

    mine, theirs = 4 * core, 4 - 4 * core
    with jax.named_scope("swap_modes"):
        packed = swap_cores(jnp.stack([modes_of(spectrum, theirs, 4), modes_of(out_grad, theirs, 4)]))
        w_other = swap_cores(modes_of(weight, theirs, 4))
        spec = jnp.stack([modes_of(spectrum, mine, 4), packed[0]])
        grad = jnp.stack([modes_of(out_grad, mine, 4), packed[1]])

    with jax.named_scope("gather_grad"):
        line = jnp.stack([grad] + [hop(grad, shift, 0) for shift in SHIFTS])
        held = [line] + [hop(line, shift, 1) for shift in SHIFTS]

    with jax.named_scope("exchange_modes"):
        exchanged = []
        for shift in SHIFTS:
            at = (dp + shift) % 4
            both = jnp.stack([lax.dynamic_index_in_dim(v, at, 1, False) for v in (spec, grad)])
            exchanged.append(ring(both, "dp", shift))

    with jax.named_scope("gather_rows"):
        xs = jnp.stack(
            [lax.dynamic_index_in_dim(spec, dp, 1, False)] + [block[0] for block in exchanged], axis=1
        )
        xs_across = flip(xs, "cout", 2)
        xs_beside = flip(jnp.stack([xs, xs_across]), "cout", 1)

    with jax.named_scope("gather_late_grad"):
        late = jnp.stack([block[1] for block in exchanged], axis=1)
        late_line = jnp.stack([late] + [hop(late, shift, 0) for shift in SHIFTS])

    tree = jax.ShapeDtypeStruct((2, 4, 2, 2, 16, 512), jnp.float32)
    keep, send = pl.pallas_call(
        input_terms,
        out_shape=(tree, tree),
        in_specs=[SMEM, SMEM, VMEM, VMEM] + [ANY] * 4,
        out_specs=(VMEM, VMEM),
        scratch_shapes=[pltpu.VMEM((4, 2, 512, 512), jnp.bfloat16), pltpu.SemaphoreType.DMA],
        compiler_params=pltpu.CompilerParams(vmem_limit_bytes=24 * MIB),
        cost_estimate=pl.CostEstimate(flops=1 << 30, bytes_accessed=8 * MIB, transcendentals=0),
        name="input_terms",
    )(blocks, scalars, weight, w_other, *held)
    with jax.named_scope("sum_input"):
        beside = flip(send, "cout", 1)
        across = flip(keep[1] + beside[1], "cout", 2)
        summed = ((keep[0] + beside[0]) + across).astype(jnp.bfloat16)
        own, other = summed[:, :, 0], swap_cores(summed[:, :, 1])
        spectrum_grad = jnp.where(
            core == 0, jnp.concatenate([own, other], axis=0), jnp.concatenate([other, own], axis=0)
        )

    with jax.named_scope("gather_late_grad"):
        late_held = [late_line] + [hop(late_line, shift, 1) for shift in SHIFTS]
    terms = pl.pallas_call(
        weight_terms,
        out_shape=jax.ShapeDtypeStruct((2, 2, 64, 512), jnp.bfloat16),
        in_specs=[SMEM, SMEM] + [ANY] * 11,
        out_specs=VMEM,
        scratch_shapes=[
            pltpu.VMEM((4, 2, 512, 512), jnp.bfloat16),
            pltpu.VMEM((4, 2, 128, 512), jnp.bfloat16),
            pltpu.SemaphoreType.DMA,
        ],
        compiler_params=pltpu.CompilerParams(vmem_limit_bytes=24 * MIB),
        cost_estimate=pl.CostEstimate(flops=1 << 30, bytes_accessed=5 * MIB, transcendentals=0),
        name="weight_terms",
    )(blocks, scalars, *held, *late_held, xs, xs_across, xs_beside)

    with jax.named_scope("spread_weight"):
        finished = jnp.stack([terms[0], swap_cores(terms[1])])
        spread = [ring(finished, "dp", shift) for shift in SHIFTS]
    weight_grad = pl.pallas_call(
        place_modes,
        out_shape=jax.ShapeDtypeStruct(weight.shape, jnp.bfloat16),
        in_specs=[SMEM] + [ANY] * 4,
        out_specs=VMEM,
        scratch_shapes=[pltpu.SemaphoreType.DMA],
        compiler_params=pltpu.CompilerParams(vmem_limit_bytes=8 * MIB),
        cost_estimate=pl.CostEstimate(flops=0, bytes_accessed=2 * MIB, transcendentals=0),
        name="place_modes",
    )(scalars, finished, *spread)
    return (spectrum_grad, weight_grad)


def solution(mesh):
    placed = (
        P(None, None, "cin", "cout"),
        P(None, None, ("cin", "cout"), "dp"),
        P(None, None, ("cout", "cin"), "dp"),
    )
    return jax.shard_map(
        on_device,
        mesh=mesh,
        in_specs=placed,
        out_specs=(P(None, None, ("cin", "cout"), "dp"), P(None, None, "cin", "cout")),
        check_vma=False,
    )
```

time: 330 us -> 256 us (0.78)
  the two profiles are of different devices: /device:TPU:34 before, /device:TPU:1 now
where the time goes in v2:
time: 256 us; the launch traced here: 255 us
  starting transfers between devices  116 us (45%)
  waiting for transfers between devices  86.5 us (34%)
  between operations  37.4 us (15%)
  Pallas kernels  9.25 us (4%)
  local copies, waits for them, and re-layouts  3.16 us (1%)
  other arithmetic  2.59 us (1%)
    ppermute x6, waiting for transfers between devices, ring(): return lax.ppermute(value, axis, [(i, (i + shift) % 4) for i in range(4)])  65 us
    ppermute x8, starting transfers between devices, flip(): return lax.ppermute(value, axis, [(i, i ^ bits) for i in range(size)])  44.9 us
    ppermute x6, starting transfers between devices, ring(): return lax.ppermute(value, axis, [(i, (i + shift) % 4) for i in range(4)])  37 us
    ppermute x12, starting transfers between devices, hop(): return lax.ppermute(value, 'cin', pairs)  33.9 us
    ppermute x8, waiting for transfers between devices, flip(): return lax.ppermute(value, axis, [(i, i ^ bits) for i in range(size)])  20.1 us
  transfers between devices with their start and end apart: 26, of which 9 were waited for; matrix products, arithmetic and copies ran while one was open for 1% of the time, Pallas kernels for 4%

profile of v2, /device:TPU:1, one launch (start us, length us, event | category | flops | bytes accessed | tf_op | source)
XLA Modules:
  0.0 254.6 jit_solution(8102313342565599601)
XLA Ops:
  1.9 8.8 %collective-permute-start.1 = (bf16[2,4,2,16,512]{4,3,2,1,0:T(8,128)(2,1)S(1)}, bf16[2,4,2,16,512]{4,3,2,1,0:T(8,128)(2,1)S(1)}, u32[]{:S(2)}, u32[]{:S(2)}) collective-permute-start(bf16[2,4,2,16,512]{4,3,2,1,0:T(8,128)(2,1)S(1)} %pad_maximum_fusion.4), channel_id=1, source_target_pairs={{0,4},{4,0},{8,12},{12,8},{16,20},{20,16},{24,28},{28,24},{32,36},... | collective-permute-start | bytes 786440 | tf_op jit(solution)/shard_map/swap_modes/ppermute | solution.py:22
  15.4 4.6 %collective-permute-start.3 = (bf16[2,4,2,16,512]{4,3,2,1,0:T(8,128)(2,1)S(1)}, bf16[2,4,2,16,512]{4,3,2,1,0:T(8,128)(2,1)}, u32[]{:S(2)}, u32[]{:S(2)}) collective-permute-start(bf16[2,4,2,16,512]{4,3,2,1,0:T(8,128)(2,1)S(1)} %get-tuple-element.24), channel_id=1, source_target_pairs={{0,24},{4,100},{8,0},{12,108},{16,8},{20,116},{24,16},{28,124},{32... | collective-permute-start | bytes 786440 | tf_op jit(solution)/shard_map/gather_grad/ppermute | solution.py:38
  62.1 4.6 %collective-permute-start.6 = (bf16[4,2,4,2,16,512]{5,4,3,2,1,0:T(8,128)(2,1)S(1)}, bf16[4,2,4,2,16,512]{5,4,3,2,1,0:T(8,128)(2,1)S(1)}, u32[]{:S(2)}, u32[]{:S(2)}) collective-permute-start(bf16[4,2,4,2,16,512]{5,4,3,2,1,0:T(8,128)(2,1)S(1)} %pad_maximum_fusion.p0), channel_id=1, source_target_pairs={{0,96},{4,28},{8,104},{12,4},{16,112},{20,12},{24,120},{28,20},{32... | collective-permute-start | bytes 3145736 | tf_op jit(solution)/shard_map/gather_grad/ppermute | solution.py:38
  68.7 6.7 %collective-permute-start.11 = (bf16[2,2,2,16,512]{4,3,2,1,0:T(8,128)(2,1)S(1)}, bf16[2,2,2,16,512]{4,3,2,1,0:T(8,128)(2,1)S(1)}, u32[]{:S(2)}, u32[]{:S(2)}) collective-permute-start(bf16[2,2,2,16,512]{4,3,2,1,0:T(8,128)(2,1)S(1)} %pad_maximum_fusion.8), channel_id=1, source_target_pairs={{0,128},{128,256},{256,384},{384,0},{1,129},{129,257},{257,385},{3... | collective-permute-start | bytes 393224 | tf_op jit(solution)/shard_map/exchange_modes/ppermute | solution.py:18
  75.4 6.2 %collective-permute-done.11 = bf16[2,2,2,16,512]{4,3,2,1,0:T(8,128)(2,1)S(1)} collective-permute-done((bf16[2,2,2,16,512]{4,3,2,1,0:T(8,128)(2,1)S(1)}, bf16[2,2,2,16,512]{4,3,2,1,0:T(8,128)(2,1)S(1)}, u32[]{:S(2)}, u32[]{:S(2)}) %collective-permute-start.11) | collective-permute-done | bytes 131104 | tf_op jit(solution)/shard_map/exchange_modes/ppermute | solution.py:18
  81.6 7.3 %collective-permute-start.12 = (bf16[2,2,2,16,512]{4,3,2,1,0:T(8,128)(2,1)S(1)}, bf16[2,2,2,16,512]{4,3,2,1,0:T(8,128)(2,1)S(1)}, u32[]{:S(2)}, u32[]{:S(2)}) collective-permute-start(bf16[2,2,2,16,512]{4,3,2,1,0:T(8,128)(2,1)S(1)} %pad_maximum_fusion.9), channel_id=1, source_target_pairs={{0,384},{128,0},{256,128},{384,256},{1,385},{129,1},{257,129},{385... | collective-permute-start | bytes 393224 | tf_op jit(solution)/shard_map/exchange_modes/ppermute | solution.py:18
  88.9 13.1 %collective-permute-done.12 = bf16[2,2,2,16,512]{4,3,2,1,0:T(8,128)(2,1)S(1)} collective-permute-done((bf16[2,2,2,16,512]{4,3,2,1,0:T(8,128)(2,1)S(1)}, bf16[2,2,2,16,512]{4,3,2,1,0:T(8,128)(2,1)S(1)}, u32[]{:S(2)}, u32[]{:S(2)}) %collective-permute-start.12) | collective-permute-done | bytes 131104 | tf_op jit(solution)/shard_map/exchange_modes/ppermute | solution.py:18
  102.0 8.3 %collective-permute-start.13 = (bf16[2,2,2,16,512]{4,3,2,1,0:T(8,128)(2,1)S(1)}, bf16[2,2,2,16,512]{4,3,2,1,0:T(8,128)(2,1)S(1)}, u32[]{:S(2)}, u32[]{:S(2)}) collective-permute-start(bf16[2,2,2,16,512]{4,3,2,1,0:T(8,128)(2,1)S(1)} %pad_maximum_fusion.10), channel_id=1, source_target_pairs={{0,256},{128,384},{256,0},{384,128},{1,257},{129,385},{257,1},{385... | collective-permute-start | bytes 393224 | tf_op jit(solution)/shard_map/exchange_modes/ppermute | solution.py:18
  110.3 9.3 %collective-permute-done.13 = bf16[2,2,2,16,512]{4,3,2,1,0:T(8,128)(2,1)S(1)} collective-permute-done((bf16[2,2,2,16,512]{4,3,2,1,0:T(8,128)(2,1)S(1)}, bf16[2,2,2,16,512]{4,3,2,1,0:T(8,128)(2,1)S(1)}, u32[]{:S(2)}, u32[]{:S(2)}) %collective-permute-start.13) | collective-permute-done | bytes 131104 | tf_op jit(solution)/shard_map/exchange_modes/ppermute | solution.py:18
  122.0 4.2 %collective-permute-start.15 = (bf16[2,3,2,16,512]{4,3,2,0,1:T(8,128)(2,1)S(1)}, bf16[2,3,2,16,512]{4,3,2,0,1:T(8,128)(2,1)S(1)}, u32[]{:S(2)}, u32[]{:S(2)}) collective-permute-start(bf16[2,3,2,16,512]{4,3,2,0,1:T(8,128)(2,1)S(1)} %get-tuple-element.28), channel_id=1, source_target_pairs={{0,24},{4,100},{8,0},{12,108},{16,8},{20,116},{24,16},{28,124},{32... | collective-permute-start | bytes 589832 | tf_op jit(solution)/shard_map/gather_late_grad/ppermute | solution.py:38
  136.5 4.3 %collective-permute-start.18 = (bf16[4,2,3,2,16,512]{5,4,3,1,2,0:T(8,128)(2,1)S(1)}, bf16[4,2,3,2,16,512]{5,4,3,1,2,0:T(8,128)(2,1)S(1)}, u32[]{:S(2)}, u32[]{:S(2)}) collective-permute-start(bf16[4,2,3,2,16,512]{5,4,3,1,2,0:T(8,128)(2,1)S(1)} %pad_maximum_fusion.1), channel_id=1, source_target_pairs={{0,96},{4,28},{8,104},{12,4},{16,112},{20,12},{24,120},{28,20},{32... | collective-permute-start | bytes 2359304 | tf_op jit(solution)/shard_map/gather_late_grad/ppermute | solution.py:38
  143.0 10.0 %collective-permute-start.20 = (bf16[2,4,2,16,512]{4,3,2,1,0:T(8,128)(2,1)S(1)}, bf16[2,4,2,16,512]{4,3,2,1,0:T(8,128)(2,1)S(1)}, u32[]{:S(2)}, u32[]{:S(2)}) collective-permute-start(bf16[2,4,2,16,512]{4,3,2,1,0:T(8,128)(2,1)S(1)} %get-tuple-element.9.x0), channel_id=1, source_target_pairs={{0,2},{1,3},{2,0},{3,1},{4,6},{5,7},{6,4},{7,5},{8,10},{9,11},{10,... | collective-permute-start | bytes 786440 | tf_op jit(solution)/shard_map/gather_rows/ppermute | solution.py:22
  153.0 6.2 %collective-permute-done.20.x1 = bf16[2,4,2,16,512]{4,3,2,1,0:T(8,128)(2,1)S(1)} collective-permute-done((bf16[2,4,2,16,512]{4,3,2,1,0:T(8,128)(2,1)S(1)}, bf16[2,4,2,16,512]{4,3,2,1,0:T(8,128)(2,1)S(1)}, u32[]{:S(2)}, u32[]{:S(2)}) %collective-permute-start.20) | collective-permute-done | bytes 262176 | tf_op jit(solution)/shard_map/gather_rows/ppermute | solution.py:22
  159.2 12.2 %collective-permute-start.21 = (bf16[2,2,4,2,16,512]{5,4,3,2,1,0:T(8,128)(2,1)S(1)}, bf16[2,2,4,2,16,512]{5,4,3,2,1,0:T(8,128)(2,1)S(1)}, u32[]{:S(2)}, u32[]{:S(2)}) collective-permute-start(bf16[2,2,4,2,16,512]{5,4,3,2,1,0:T(8,128)(2,1)S(1)} %pad_maximum_fusion.2), channel_id=1, source_target_pairs={{0,1},{1,0},{2,3},{3,2},{4,5},{5,4},{6,7},{7,6},{8,9},{9,8},{10,11... | collective-permute-start | bytes 1572872 | tf_op jit(solution)/shard_map/gather_rows/ppermute | solution.py:22
  173.8 12.9 %collective-permute-done.21.x2 = bf16[2,2,4,2,16,512]{5,4,3,2,1,0:T(8,128)(2,1)S(1)} collective-permute-done((bf16[2,2,4,2,16,512]{5,4,3,2,1,0:T(8,128)(2,1)S(1)}, bf16[2,2,4,2,16,512]{5,4,3,2,1,0:T(8,128)(2,1)S(1)}, u32[]{:S(2)}, u32[]{:S(2)}) %collective-permute-start.21) | collective-permute-done | bytes 524320 | tf_op jit(solution)/shard_map/gather_rows/ppermute | solution.py:22
  186.7 3.7 %weight_terms.1 = bf16[2,2,64,512]{3,2,1,0:T(8,128)(2,1)S(1)} custom-call(s32[32]{0:T(128)S(1)} %stack.276.blocks, s32[14]{0:T(128)S(1)} %stack.291.scalars, bf16[4,2,4,2,16,512]{5,4,3,2,1,0:T(8,128)(2,1)S(1)} %pad_maximum_fusion.p0, bf16[4,2,4,2,16,512]{5,4,3,2,1,0:T(8,128)(2,1)S(1)} %collective-permute-done.5.p1, ...), custom_call_target="tpu_custom_call" | custom-call | flops 1073741824 | bytes 5242880 | tf_op jit(solution)/shard_map/weight_terms/pallas_call | solution.py:204
  190.4 5.1 %collective-permute-start.22 = (bf16[2,64,512]{2,1,0:T(8,128)(2,1)S(1)}, bf16[2,64,512]{2,1,0:T(8,128)(2,1)S(1)}, u32[]{:S(2)}, u32[]{:S(2)}) collective-permute-start(bf16[2,64,512]{2,1,0:T(8,128)(2,1)S(1)} %get-tuple-element.7), channel_id=1, source_target_pairs={{0,4},{4,0},{8,12},{12,8},{16,20},{20,16},{24,28},{28,24},{32,36},... | collective-permute-start | bytes 393224 | tf_op jit(solution)/shard_map/spread_weight/ppermute | solution.py:22
  196.4 3.0 %collective-permute-start.23 = (bf16[2,2,64,512]{3,2,1,0:T(8,128)(2,1)S(1)}, bf16[2,2,64,512]{3,2,1,0:T(8,128)(2,1)S(1)}, u32[]{:S(2)}, u32[]{:S(2)}) collective-permute-start(bf16[2,2,64,512]{3,2,1,0:T(8,128)(2,1)S(1)} %pad_maximum_fusion.6.own), channel_id=1, source_target_pairs={{0,128},{128,256},{256,384},{384,0},{1,129},{129,257},{257,385},{3... | collective-permute-start | bytes 786440 | tf_op jit(solution)/shard_map/spread_weight/ppermute | solution.py:18
  199.5 6.2 %collective-permute-start.24 = (bf16[2,2,64,512]{3,2,1,0:T(8,128)(2,1)S(1)}, bf16[2,2,64,512]{3,2,1,0:T(8,128)(2,1)S(1)}, u32[]{:S(2)}, u32[]{:S(2)}) collective-permute-start(bf16[2,2,64,512]{3,2,1,0:T(8,128)(2,1)S(1)} %pad_maximum_fusion.6.own), channel_id=1, source_target_pairs={{0,384},{128,0},{256,128},{384,256},{1,385},{129,1},{257,129},{385... | collective-permute-start | bytes 786440 | tf_op jit(solution)/shard_map/spread_weight/ppermute | solution.py:18
  205.6 5.6 %collective-permute-start.25 = (bf16[2,2,64,512]{3,2,1,0:T(8,128)(2,1)S(1)}, bf16[2,2,64,512]{3,2,1,0:T(8,128)(2,1)S(1)}, u32[]{:S(2)}, u32[]{:S(2)}) collective-permute-start(bf16[2,2,64,512]{3,2,1,0:T(8,128)(2,1)S(1)} %pad_maximum_fusion.6.own), channel_id=1, source_target_pairs={{0,256},{128,384},{256,0},{384,128},{1,257},{129,385},{257,1},{385... | collective-permute-start | bytes 786440 | tf_op jit(solution)/shard_map/spread_weight/ppermute | solution.py:18
  211.5 3.1 %collective-permute-start.10 = (bf16[4,2,16,512]{3,2,1,0:T(8,128)(2,1)S(1)}, bf16[4,2,16,512]{3,2,1,0:T(8,128)(2,1)S(1)}, u32[]{:S(2)}, u32[]{:S(2)}) collective-permute-start(bf16[4,2,16,512]{3,2,1,0:T(8,128)(2,1)S(1)} %get-tuple-element.22), channel_id=1, source_target_pairs={{0,4},{4,0},{8,12},{12,8},{16,20},{20,16},{24,28},{28,24},{32,36},... | collective-permute-start | bytes 393224 | tf_op jit(solution)/shard_map/sum_input/ppermute | solution.py:22
  214.6 14.6 %collective-permute-done.24.ahead = bf16[2,2,64,512]{3,2,1,0:T(8,128)(2,1)S(1)} collective-permute-done((bf16[2,2,64,512]{3,2,1,0:T(8,128)(2,1)S(1)}, bf16[2,2,64,512]{3,2,1,0:T(8,128)(2,1)S(1)}, u32[]{:S(2)}, u32[]{:S(2)}) %collective-permute-start.24) | collective-permute-done | bytes 262176 | tf_op jit(solution)/shard_map/spread_weight/ppermute | solution.py:18
  229.3 21.7 %collective-permute-done.25.far = bf16[2,2,64,512]{3,2,1,0:T(8,128)(2,1)S(1)} collective-permute-done((bf16[2,2,64,512]{3,2,1,0:T(8,128)(2,1)S(1)}, bf16[2,2,64,512]{3,2,1,0:T(8,128)(2,1)S(1)}, u32[]{:S(2)}, u32[]{:S(2)}) %collective-permute-start.25) | collective-permute-done | bytes 262176 | tf_op jit(solution)/shard_map/spread_weight/ppermute | solution.py:18
  251.0 2.9 %place_modes.1 = bf16[8,2,64,512]{3,2,1,0:T(8,128)(2,1)} custom-call(s32[14]{0:T(128)S(1)} %stack.291.scalars, bf16[2,2,64,512]{3,2,1,0:T(8,128)(2,1)S(1)} %pad_maximum_fusion.6.own, bf16[2,2,64,512]{3,2,1,0:T(8,128)(2,1)S(1)} %collective-permute-done.23.back, bf16[2,2,64,512]{3,2,1,0:T(8,128)(2,1)S(1)} %collective-permute-done.24.ahead, ...), custom_call_target="tpu_custom_call" | custom-call | bytes 2097152 | tf_op jit(solution)/shard_map/place_modes/pallas_call | solution.py:222
  (67 shorter events, 32.8 us)
Async XLA Ops:
  1.9 11.5 %collective-permute-start.1 = (bf16[2,4,2,16,512]{4,3,2,1,0:T(8,128)(2,1)S(1)}, bf16[2,4,2,16,512]{4,3,2,1,0:T(8,128)(2,1)S(1)}, u32[]{:S(2)}, u32[]{:S(2)}) collective-permute-start(bf16[2,4,2,16,512]{4,3,2,1,0:T(8,128)(2,1)S(1)} %pad_maximum_fusion.4), channel_id=1, source_target_pairs={{0,4},{4,0},{8,12},{12,8},{16,20},{20,16},{24,28},{28,24},{32,36},... | collective-permute-start | bytes 786440 | tf_op jit(solution)/shard_map/swap_modes/ppermute | solution.py:22
  10.8 111.2 %collective-permute-start = (bf16[4,2,64,512]{3,2,1,0:T(8,128)(2,1)S(1)}, bf16[4,2,64,512]{3,2,1,0:T(8,128)(2,1)S(1)}, u32[]{:S(2)}, u32[]{:S(2)}) collective-permute-start(bf16[4,2,64,512]{3,2,1,0:T(8,128)(2,1)S(1)} %constant_dynamic-slice_fusion), channel_id=1, source_target_pairs={{0,4},{4,0},{8,12},{12,8},{16,20},{20,16},{24,28},{28,24},{32,36},... | collective-permute-start | bytes 1572872 | tf_op jit(solution)/shard_map/swap_modes/ppermute | solution.py:22
  13.5 45.5 %collective-permute-start.2 = (bf16[2,4,2,16,512]{4,3,2,1,0:T(8,128)(2,1)S(1)}, bf16[2,4,2,16,512]{4,3,2,1,0:T(8,128)(2,1)S(1)}, u32[]{:S(2)}, u32[]{:S(2)}) collective-permute-start(bf16[2,4,2,16,512]{4,3,2,1,0:T(8,128)(2,1)S(1)} %get-tuple-element.24), channel_id=1, source_target_pairs={{0,8},{4,36},{8,16},{12,44},{16,24},{20,52},{24,0},{28,60},{32,40}... | collective-permute-start | bytes 786440 | tf_op jit(solution)/shard_map/gather_grad/ppermute | solution.py:38
  15.4 43.6 %collective-permute-start.3 = (bf16[2,4,2,16,512]{4,3,2,1,0:T(8,128)(2,1)S(1)}, bf16[2,4,2,16,512]{4,3,2,1,0:T(8,128)(2,1)}, u32[]{:S(2)}, u32[]{:S(2)}) collective-permute-start(bf16[2,4,2,16,512]{4,3,2,1,0:T(8,128)(2,1)S(1)} %get-tuple-element.24), channel_id=1, source_target_pairs={{0,24},{4,100},{8,0},{12,108},{16,8},{20,116},{24,16},{28,124},{32... | collective-permute-start | bytes 786440 | tf_op jit(solution)/shard_map/gather_grad/ppermute | solution.py:38
  20.0 39.0 %collective-permute-start.4 = (bf16[2,4,2,16,512]{4,3,2,1,0:T(8,128)(2,1)S(1)}, bf16[2,4,2,16,512]{4,3,2,1,0:T(8,128)(2,1)}, u32[]{:S(2)}, u32[]{:S(2)}) collective-permute-start(bf16[2,4,2,16,512]{4,3,2,1,0:T(8,128)(2,1)S(1)} %get-tuple-element.24), channel_id=1, source_target_pairs={{0,16},{4,68},{8,24},{12,76},{16,0},{20,84},{24,8},{28,92},{32,48}... | collective-permute-start | bytes 786440 | tf_op jit(solution)/shard_map/gather_grad/ppermute | solution.py:38
  60.2 66.0 %collective-permute-start.5 = (bf16[4,2,4,2,16,512]{5,4,3,2,1,0:T(8,128)(2,1)S(1)}, bf16[4,2,4,2,16,512]{5,4,3,2,1,0:T(8,128)(2,1)S(1)}, u32[]{:S(2)}, u32[]{:S(2)}) collective-permute-start(bf16[4,2,4,2,16,512]{5,4,3,2,1,0:T(8,128)(2,1)S(1)} %pad_maximum_fusion.p0), channel_id=1, source_target_pairs={{0,32},{4,12},{8,40},{12,20},{16,48},{20,28},{24,56},{28,4},{32,64... | collective-permute-start | bytes 3145736 | tf_op jit(solution)/shard_map/gather_grad/ppermute | solution.py:38
  62.1 66.0 %collective-permute-start.6 = (bf16[4,2,4,2,16,512]{5,4,3,2,1,0:T(8,128)(2,1)S(1)}, bf16[4,2,4,2,16,512]{5,4,3,2,1,0:T(8,128)(2,1)S(1)}, u32[]{:S(2)}, u32[]{:S(2)}) collective-permute-start(bf16[4,2,4,2,16,512]{5,4,3,2,1,0:T(8,128)(2,1)S(1)} %pad_maximum_fusion.p0), channel_id=1, source_target_pairs={{0,96},{4,28},{8,104},{12,4},{16,112},{20,12},{24,120},{28,20},{32... | collective-permute-start | bytes 3145736 | tf_op jit(solution)/shard_map/gather_grad/ppermute | solution.py:38
  66.7 61.5 %collective-permute-start.7 = (bf16[4,2,4,2,16,512]{5,4,3,2,1,0:T(8,128)(2,1)S(1)}, bf16[4,2,4,2,16,512]{5,4,3,2,1,0:T(8,128)(2,1)S(1)}, u32[]{:S(2)}, u32[]{:S(2)}) collective-permute-start(bf16[4,2,4,2,16,512]{5,4,3,2,1,0:T(8,128)(2,1)S(1)} %pad_maximum_fusion.p0), channel_id=1, source_target_pairs={{0,64},{4,20},{8,72},{12,28},{16,80},{20,4},{24,88},{28,12},{32,96... | collective-permute-start | bytes 3145736 | tf_op jit(solution)/shard_map/gather_grad/ppermute | solution.py:38
  68.7 12.9 %collective-permute-start.11 = (bf16[2,2,2,16,512]{4,3,2,1,0:T(8,128)(2,1)S(1)}, bf16[2,2,2,16,512]{4,3,2,1,0:T(8,128)(2,1)S(1)}, u32[]{:S(2)}, u32[]{:S(2)}) collective-permute-start(bf16[2,2,2,16,512]{4,3,2,1,0:T(8,128)(2,1)S(1)} %pad_maximum_fusion.8), channel_id=1, source_target_pairs={{0,128},{128,256},{256,384},{384,0},{1,129},{129,257},{257,385},{3... | collective-permute-start | bytes 393224 | tf_op jit(solution)/shard_map/exchange_modes/ppermute | solution.py:18
  81.6 20.4 %collective-permute-start.12 = (bf16[2,2,2,16,512]{4,3,2,1,0:T(8,128)(2,1)S(1)}, bf16[2,2,2,16,512]{4,3,2,1,0:T(8,128)(2,1)S(1)}, u32[]{:S(2)}, u32[]{:S(2)}) collective-permute-start(bf16[2,2,2,16,512]{4,3,2,1,0:T(8,128)(2,1)S(1)} %pad_maximum_fusion.9), channel_id=1, source_target_pairs={{0,384},{128,0},{256,128},{384,256},{1,385},{129,1},{257,129},{385... | collective-permute-start | bytes 393224 | tf_op jit(solution)/shard_map/exchange_modes/ppermute | solution.py:18
  102.0 17.7 %collective-permute-start.13 = (bf16[2,2,2,16,512]{4,3,2,1,0:T(8,128)(2,1)S(1)}, bf16[2,2,2,16,512]{4,3,2,1,0:T(8,128)(2,1)S(1)}, u32[]{:S(2)}, u32[]{:S(2)}) collective-permute-start(bf16[2,2,2,16,512]{4,3,2,1,0:T(8,128)(2,1)S(1)} %pad_maximum_fusion.10), channel_id=1, source_target_pairs={{0,256},{128,384},{256,0},{384,128},{1,257},{129,385},{257,1},{385... | collective-permute-start | bytes 393224 | tf_op jit(solution)/shard_map/exchange_modes/ppermute | solution.py:18
  119.7 13.1 %collective-permute-start.14 = (bf16[2,3,2,16,512]{4,3,2,0,1:T(8,128)(2,1)S(1)}, bf16[2,3,2,16,512]{4,3,2,0,1:T(8,128)(2,1)S(1)}, u32[]{:S(2)}, u32[]{:S(2)}) collective-permute-start(bf16[2,3,2,16,512]{4,3,2,0,1:T(8,128)(2,1)S(1)} %get-tuple-element.28), channel_id=1, source_target_pairs={{0,8},{4,36},{8,16},{12,44},{16,24},{20,52},{24,0},{28,60},{32,40}... | collective-permute-start | bytes 589832 | tf_op jit(solution)/shard_map/gather_late_grad/ppermute | solution.py:38
  122.0 10.8 %collective-permute-start.15 = (bf16[2,3,2,16,512]{4,3,2,0,1:T(8,128)(2,1)S(1)}, bf16[2,3,2,16,512]{4,3,2,0,1:T(8,128)(2,1)S(1)}, u32[]{:S(2)}, u32[]{:S(2)}) collective-permute-start(bf16[2,3,2,16,512]{4,3,2,0,1:T(8,128)(2,1)S(1)} %get-tuple-element.28), channel_id=1, source_target_pairs={{0,24},{4,100},{8,0},{12,108},{16,8},{20,116},{24,16},{28,124},{32... | collective-permute-start | bytes 589832 | tf_op jit(solution)/shard_map/gather_late_grad/ppermute | solution.py:38
  130.9 40.9 %collective-permute-start.8 = (f32[2,4,2,2,16,512]{5,4,3,2,1,0:T(8,128)S(1)}, f32[2,4,2,2,16,512]{5,4,3,2,1,0:T(8,128)S(1)}, u32[]{:S(2)}, u32[]{:S(2)}) collective-permute-start(f32[2,4,2,2,16,512]{5,4,3,2,1,0:T(8,128)S(1)} %get-tuple-element.5), channel_id=1, source_target_pairs={{0,1},{1,0},{2,3},{3,2},{4,5},{5,4},{6,7},{7,6},{8,9},{9,8},{10,11... | collective-permute-start | bytes 3145736 | tf_op jit(solution)/shard_map/sum_input/ppermute | solution.py:22
  134.3 37.2 %collective-permute-start.17 = (bf16[4,2,3,2,16,512]{5,4,3,1,2,0:T(8,128)(2,1)S(1)}, bf16[4,2,3,2,16,512]{5,4,3,1,2,0:T(8,128)(2,1)S(1)}, u32[]{:S(2)}, u32[]{:S(2)}) collective-permute-start(bf16[4,2,3,2,16,512]{5,4,3,1,2,0:T(8,128)(2,1)S(1)} %pad_maximum_fusion.1), channel_id=1, source_target_pairs={{0,32},{4,12},{8,40},{12,20},{16,48},{20,28},{24,56},{28,4},{32,64... | collective-permute-start | bytes 2359304 | tf_op jit(solution)/shard_map/gather_late_grad/ppermute | solution.py:38
  136.5 35.1 %collective-permute-start.18 = (bf16[4,2,3,2,16,512]{5,4,3,1,2,0:T(8,128)(2,1)S(1)}, bf16[4,2,3,2,16,512]{5,4,3,1,2,0:T(8,128)(2,1)S(1)}, u32[]{:S(2)}, u32[]{:S(2)}) collective-permute-start(bf16[4,2,3,2,16,512]{5,4,3,1,2,0:T(8,128)(2,1)S(1)} %pad_maximum_fusion.1), channel_id=1, source_target_pairs={{0,96},{4,28},{8,104},{12,4},{16,112},{20,12},{24,120},{28,20},{32... | collective-permute-start | bytes 2359304 | tf_op jit(solution)/shard_map/gather_late_grad/ppermute | solution.py:38
  140.8 30.9 %collective-permute-start.19 = (bf16[4,2,3,2,16,512]{5,4,3,1,2,0:T(8,128)(2,1)S(1)}, bf16[4,2,3,2,16,512]{5,4,3,1,2,0:T(8,128)(2,1)S(1)}, u32[]{:S(2)}, u32[]{:S(2)}) collective-permute-start(bf16[4,2,3,2,16,512]{5,4,3,1,2,0:T(8,128)(2,1)S(1)} %pad_maximum_fusion.1), channel_id=1, source_target_pairs={{0,64},{4,20},{8,72},{12,28},{16,80},{20,4},{24,88},{28,12},{32,96... | collective-permute-start | bytes 2359304 | tf_op jit(solution)/shard_map/gather_late_grad/ppermute | solution.py:38
  143.0 16.2 %collective-permute-start.20 = (bf16[2,4,2,16,512]{4,3,2,1,0:T(8,128)(2,1)S(1)}, bf16[2,4,2,16,512]{4,3,2,1,0:T(8,128)(2,1)S(1)}, u32[]{:S(2)}, u32[]{:S(2)}) collective-permute-start(bf16[2,4,2,16,512]{4,3,2,1,0:T(8,128)(2,1)S(1)} %get-tuple-element.9.x0), channel_id=1, source_target_pairs={{0,2},{1,3},{2,0},{3,1},{4,6},{5,7},{6,4},{7,5},{8,10},{9,11},{10,... | collective-permute-start | bytes 786440 | tf_op jit(solution)/shard_map/gather_rows/ppermute | solution.py:22
  159.2 27.5 %collective-permute-start.21 = (bf16[2,2,4,2,16,512]{5,4,3,2,1,0:T(8,128)(2,1)S(1)}, bf16[2,2,4,2,16,512]{5,4,3,2,1,0:T(8,128)(2,1)S(1)}, u32[]{:S(2)}, u32[]{:S(2)}) collective-permute-start(bf16[2,2,4,2,16,512]{5,4,3,2,1,0:T(8,128)(2,1)S(1)} %pad_maximum_fusion.2), channel_id=1, source_target_pairs={{0,1},{1,0},{2,3},{3,2},{4,5},{5,4},{6,7},{7,6},{8,9},{9,8},{10,11... | collective-permute-start | bytes 1572872 | tf_op jit(solution)/shard_map/gather_rows/ppermute | solution.py:22
  171.8 39.5 %collective-permute-start.9 = (f32[4,2,2,16,512]{4,3,2,1,0:T(8,128)S(1)}, f32[4,2,2,16,512]{4,3,2,1,0:T(8,128)S(1)}, u32[]{:S(2)}, u32[]{:S(2)}) collective-permute-start(f32[4,2,2,16,512]{4,3,2,1,0:T(8,128)S(1)} %fusion), channel_id=1, source_target_pairs={{0,2},{1,3},{2,0},{3,1},{4,6},{5,7},{6,4},{7,5},{8,10},{9,11},{10,... | collective-permute-start | bytes 1572872 | tf_op jit(solution)/shard_map/sum_input/ppermute | solution.py:22
  196.4 18.2 %collective-permute-start.23 = (bf16[2,2,64,512]{3,2,1,0:T(8,128)(2,1)S(1)}, bf16[2,2,64,512]{3,2,1,0:T(8,128)(2,1)S(1)}, u32[]{:S(2)}, u32[]{:S(2)}) collective-permute-start(bf16[2,2,64,512]{3,2,1,0:T(8,128)(2,1)S(1)} %pad_maximum_fusion.6.own), channel_id=1, source_target_pairs={{0,128},{128,256},{256,384},{384,0},{1,129},{129,257},{257,385},{3... | collective-permute-start | bytes 786440 | tf_op jit(solution)/shard_map/spread_weight/ppermute | solution.py:18
  199.5 29.8 %collective-permute-start.24 = (bf16[2,2,64,512]{3,2,1,0:T(8,128)(2,1)S(1)}, bf16[2,2,64,512]{3,2,1,0:T(8,128)(2,1)S(1)}, u32[]{:S(2)}, u32[]{:S(2)}) collective-permute-start(bf16[2,2,64,512]{3,2,1,0:T(8,128)(2,1)S(1)} %pad_maximum_fusion.6.own), channel_id=1, source_target_pairs={{0,384},{128,0},{256,128},{384,256},{1,385},{129,1},{257,129},{385... | collective-permute-start | bytes 786440 | tf_op jit(solution)/shard_map/spread_weight/ppermute | solution.py:18
  205.6 45.3 %collective-permute-start.25 = (bf16[2,2,64,512]{3,2,1,0:T(8,128)(2,1)S(1)}, bf16[2,2,64,512]{3,2,1,0:T(8,128)(2,1)S(1)}, u32[]{:S(2)}, u32[]{:S(2)}) collective-permute-start(bf16[2,2,64,512]{3,2,1,0:T(8,128)(2,1)S(1)} %pad_maximum_fusion.6.own), channel_id=1, source_target_pairs={{0,256},{128,384},{256,0},{384,128},{1,257},{129,385},{257,1},{385... | collective-permute-start | bytes 786440 | tf_op jit(solution)/shard_map/spread_weight/ppermute | solution.py:18
  211.5 42.4 %collective-permute-start.10 = (bf16[4,2,16,512]{3,2,1,0:T(8,128)(2,1)S(1)}, bf16[4,2,16,512]{3,2,1,0:T(8,128)(2,1)S(1)}, u32[]{:S(2)}, u32[]{:S(2)}) collective-permute-start(bf16[4,2,16,512]{3,2,1,0:T(8,128)(2,1)S(1)} %get-tuple-element.22), channel_id=1, source_target_pairs={{0,4},{4,0},{8,12},{12,8},{16,20},{20,16},{24,28},{28,24},{32,36},... | collective-permute-start | bytes 393224 | tf_op jit(solution)/shard_map/sum_input/ppermute | solution.py:22
  (4 other events, 24.7 us)

commit v3 on v2

v3 whole, which is shorter than its diff:
```python
import jax
import jax.numpy as jnp
from jax import lax
from jax.experimental import pallas as pl
from jax.experimental.pallas import tpu as pltpu
from jax.sharding import PartitionSpec as P

HEARD = (0, 3, 2, 1)
SHIFTS = (1, 2, 3)
PAIRED = (0, 1, 3, 2)
TREE = (0, 2, 1, 3)
MIB = 1 << 20
ANY = pl.BlockSpec(memory_space=pl.ANY)
SMEM = pl.BlockSpec(memory_space=pltpu.SMEM)
VMEM = pl.BlockSpec(memory_space=pltpu.VMEM)


def ring(value, axis, shift):
    return lax.ppermute(value, axis, [(i, (i + shift) % 4) for i in range(4)])


def flip(value, axis, bits, size=4):
    return lax.ppermute(value, axis, [(i, i ^ bits) for i in range(size)])


def swap_cores(value):
    return flip(value, "cin", 1, 32)


def hop(value, move, stage):
    pairs = []
    for i in range(32):
        y, x, core = i // 8, (i // 2) % 4, i % 2
        if core == stage:
            x = move(x)
        else:
            y = move(y)
        pairs.append((i, (y * 4 + x) * 2 + core))
    return lax.ppermute(value, "cin", pairs)


def after(value, *earlier):
    return lax.optimization_barrier((value, *earlier))[0]


def first_hops(block):
    two = jnp.stack([block, hop(block, lambda at: at ^ 1, 0)])
    return jnp.concatenate([two, hop(two, lambda at: at ^ 3, 0)])


def second_hops(line):
    return [line] + [hop(line, lambda at, shift=shift: (at + shift) % 4, 1) for shift in SHIFTS]


def plane_row(position, second, first, source):
    place = position[1]
    core = place & 1
    along_x, along_y = (place >> 1) & 3, place >> 3
    across = jnp.where(core == 0, along_x ^ PAIRED[first], (along_x + HEARD[second]) & 3)
    down = jnp.where(core == 0, (along_y + HEARD[second]) & 3, along_y ^ PAIRED[first])
    return pl.multiple_of(((down * 4 + across) * 2 + (core ^ source)) * 16, 16)


def tree_row(position, index):
    return pl.multiple_of((position[2] ^ TREE[index]) * 16, 16)


def fetch_plane(position, pieces, source_of, target, sem):
    for second in range(4):
        for first in range(4):
            for source in range(2):
                row = plane_row(position, second, first, source)
                pltpu.make_async_copy(
                    source_of(pieces[second].at[first], source), target(pl.ds(row, 16)), sem
                ).start()


def input_terms(position, w, w_other, *refs):
    pieces, (keep, send, grads, sem) = refs[:4], refs[4:]
    fetch_plane(
        position,
        pieces,
        lambda piece, source: piece.at[source],
        lambda rows: grads.at[:, :, rows, :],
        sem,
    )
    base = (position[1] & 1) * 4
    rows = [pl.ds(tree_row(position, r), 16) for r in range(4)]
    pltpu.make_async_copy(grads, grads, sem).wait()
    for mode in range(4):
        real, imag = (
            jnp.concatenate(
                [block for row in rows for block in (w[base + mode, part, row, :], w_other[mode, part, row, :])],
                axis=0,
            )
            for part in range(2)
        )
        total = jnp.dot(
            jnp.concatenate([real, -imag], axis=0), grads[mode, 0], preferred_element_type=jnp.float32
        ) + jnp.dot(
            jnp.concatenate([imag, real], axis=0), grads[mode, 1], preferred_element_type=jnp.float32
        )
        total = total.reshape(2, 4, 2, 16, 512)
        for part in range(2):
            for r in range(2):
                keep[r, mode, part] = total[part, r]
                send[r, mode, part] = total[part, r + 2]


def weight_terms(position, *refs):
    pieces, late, (x0, x1, x2, out, grads, rows, sem) = refs[:4], refs[4:8], refs[8:]
    mode = position[0]
    fetch_plane(
        position,
        pieces,
        lambda piece, source: piece.at[source, mode],
        lambda place: grads.at[0, :, place, :],
        sem,
    )
    for index, piece in enumerate((x0, x1, x2.at[0], x2.at[1])):
        for source in range(2):
            row = pl.multiple_of(tree_row(position, index) + 64 * source, 16)
            pltpu.make_async_copy(piece.at[source], rows.at[:, :, pl.ds(row, 16), :], sem).start()
    fetch_plane(
        position,
        late,
        lambda piece, source: piece.at[:, source],
        lambda place: grads.at[pl.ds(1, 3), :, place, :],
        sem,
    )
    pltpu.make_async_copy(grads, grads, sem).wait()
    pltpu.make_async_copy(rows, rows, sem).wait()

    total = jnp.zeros((256, 512), jnp.float32)
    contract = (((1,), (1,)), ((), ()))
    for block in range(4):
        real = rows[block, 0]
        imag = rows[block, 1]
        total += lax.dot_general(
            jnp.concatenate([real, -imag], axis=0), grads[block, 0], contract, preferred_element_type=jnp.float32
        )
        total += lax.dot_general(
            jnp.concatenate([imag, real], axis=0), grads[block, 1], contract, preferred_element_type=jnp.float32
        )
    for part in range(2):
        for source in range(2):
            start = part * 128 + source * 64
            out[source, part] = total[start : start + 64].astype(jnp.bfloat16)


def place_modes(position, own, back, far, ahead, out, sem):
    for step, piece in enumerate((own, back, far, ahead)):
        for slot in range(2):
            mode = ((position[1] & 1) ^ slot) * 4 + ((position[0] + HEARD[step]) & 3)
            pltpu.make_async_copy(piece.at[slot], out.at[mode], sem).start()
    pltpu.make_async_copy(out, out, sem).wait()


def on_device(weight, spectrum, out_grad):
    dp, place, cout = lax.axis_index("dp"), lax.axis_index("cin"), lax.axis_index("cout")
    core = place & 1
    position = jnp.stack([dp, place, cout]).astype(jnp.int32)

    def modes_of(value, start, count):
        return lax.dynamic_slice_in_dim(value, start, count, 0)

    mine, theirs = 4 * core, 4 - 4 * core
    with jax.named_scope("swap_modes"):
        swapped = swap_cores(
            jnp.concatenate([modes_of(v, theirs, 4) for v in (weight, spectrum, out_grad)], axis=2)
        )
        spec = jnp.stack([modes_of(spectrum, mine, 4), swapped[:, :, 64:80]])
        grad = jnp.stack([modes_of(out_grad, mine, 4), swapped[:, :, 80:]])

    with jax.named_scope("gather_grad"):
        line = first_hops(grad)
        held = second_hops(line)

    with jax.named_scope("exchange_modes"):
        exchanged = []
        for shift in SHIFTS:
            at = (dp + shift) & 3
            both = jnp.stack([lax.dynamic_index_in_dim(v, at, 1, False) for v in (spec, grad)])
            exchanged.append(ring(both, "dp", shift))

    with jax.named_scope("gather_rows"):
        xs = jnp.stack(
            [lax.dynamic_index_in_dim(spec, dp, 1, False)] + [block[0] for block in exchanged], axis=1
        )
        xs_across = flip(xs, "cout", 2)
        xs_beside = flip(jnp.stack([xs, xs_across]), "cout", 1)

    with jax.named_scope("gather_late_grad"):
        late = jnp.stack([block[1] for block in exchanged])
        late_line = first_hops(late)

    tree = jax.ShapeDtypeStruct((2, 4, 2, 2, 16, 512), jnp.float32)
    keep, send = pl.pallas_call(
        input_terms,
        out_shape=(tree, tree),
        in_specs=[SMEM, VMEM, VMEM] + [ANY] * 4,
        out_specs=(VMEM, VMEM),
        scratch_shapes=[pltpu.VMEM((4, 2, 512, 512), jnp.bfloat16), pltpu.SemaphoreType.DMA],
        compiler_params=pltpu.CompilerParams(vmem_limit_bytes=24 * MIB),
        cost_estimate=pl.CostEstimate(flops=1 << 30, bytes_accessed=8 * MIB, transcendentals=0),
        name="input_terms",
    )(position, weight, swapped, *held)
    with jax.named_scope("sum_input"):
        beside = flip(after(send, xs_across), "cout", 1)
        across = flip(keep[1] + beside[1], "cout", 2)
        summed = ((keep[0] + beside[0]) + across).astype(jnp.bfloat16)
        own, other = summed[:, :, 0], swap_cores(summed[:, :, 1])
        spectrum_grad = jnp.where(
            core == 0, jnp.concatenate([own, other], axis=0), jnp.concatenate([other, own], axis=0)
        )

    with jax.named_scope("gather_late_grad"):
        late_held = second_hops(late_line)
    terms = pl.pallas_call(
        weight_terms,
        out_shape=jax.ShapeDtypeStruct((2, 2, 64, 512), jnp.bfloat16),
        in_specs=[SMEM] + [ANY] * 11,
        out_specs=VMEM,
        scratch_shapes=[
            pltpu.VMEM((4, 2, 512, 512), jnp.bfloat16),
            pltpu.VMEM((4, 2, 128, 512), jnp.bfloat16),
            pltpu.SemaphoreType.DMA,
        ],
        compiler_params=pltpu.CompilerParams(vmem_limit_bytes=24 * MIB),
        cost_estimate=pl.CostEstimate(flops=1 << 30, bytes_accessed=5 * MIB, transcendentals=0),
        name="weight_terms",
    )(position, *held, *late_held, xs, xs_across, xs_beside)

    with jax.named_scope("spread_weight"):
        finished = jnp.stack([terms[0], swap_cores(terms[1])])
        spread = [ring(finished, "dp", shift) for shift in SHIFTS]
    weight_grad = pl.pallas_call(
        place_modes,
        out_shape=jax.ShapeDtypeStruct(weight.shape, jnp.bfloat16),
        in_specs=[SMEM] + [ANY] * 4,
        out_specs=VMEM,
        scratch_shapes=[pltpu.SemaphoreType.DMA],
        compiler_params=pltpu.CompilerParams(vmem_limit_bytes=8 * MIB),
        cost_estimate=pl.CostEstimate(flops=0, bytes_accessed=2 * MIB, transcendentals=0),
        name="place_modes",
    )(position, finished, *spread)
    return (spectrum_grad, weight_grad)


def solution(mesh):
    placed = (
        P(None, None, "cin", "cout"),
        P(None, None, ("cin", "cout"), "dp"),
        P(None, None, ("cout", "cin"), "dp"),
    )
    return jax.shard_map(
        on_device,
        mesh=mesh,
        in_specs=placed,
        out_specs=(P(None, None, ("cin", "cout"), "dp"), P(None, None, "cin", "cout")),
        check_vma=False,
    )
```

time: 256 us -> 197 us (0.77)
  the two profiles are of different devices: /device:TPU:1 before, /device:TPU:65 now
where the time goes in v3:
time: 197 us
  starting transfers between devices  98.6 us (50%)
  waiting for transfers between devices  84.1 us (43%)
  Pallas kernels  9.9 us (5%)
    ppermute x6, waiting for transfers between devices, ring(): return lax.ppermute(value, axis, [(i, (i + shift) % 4) for i in range(4)])  52.6 us
    ppermute x6, starting transfers between devices, ring(): return lax.ppermute(value, axis, [(i, (i + shift) % 4) for i in range(4)])  41.6 us
    ppermute x10, starting transfers between devices, hop(): return lax.ppermute(value, 'cin', pairs)  38.6 us
    ppermute x7, waiting for transfers between devices, flip(): return lax.ppermute(value, axis, [(i, i ^ bits) for i in range(size)])  22.2 us
    ppermute x7, starting transfers between devices, flip(): return lax.ppermute(value, axis, [(i, i ^ bits) for i in range(size)])  18.4 us
    ppermute x10, waiting for transfers between devices, hop(): return lax.ppermute(value, 'cin', pairs)  9.37 us
    pallas_call x1, Pallas kernels, on_device(): pl.pallas_call(weight_terms, out_shape=jax.ShapeDtypeStruct((2, 2, 64, 51...  4.14 us
  transfers between devices with their start and end apart: 23, of which 11 were waited for; matrix products, arithmetic and copies ran while one was open for 0% of the time, Pallas kernels for 5%

profile of v3, /device:TPU:65, one launch (start us, length us, event | category | flops | bytes accessed | tf_op | source)
XLA Modules:
  0.0 196.7 jit_solution(8315766849763009582)
XLA Ops:
  6.5 3.2 %collective-permute-start.1 = (bf16[2,4,2,16,512]{4,3,2,1,0:T(8,128)(2,1)S(1)}, bf16[2,4,2,16,512]{4,3,2,1,0:T(8,128)(2,1)S(1)}, u32[]{:S(2)}, u32[]{:S(2)}) collective-permute-start(bf16[2,4,2,16,512]{4,3,2,1,0:T(8,128)(2,1)S(1)} %get-tuple-element.26), channel_id=1, source_target_pairs={{0,8},{4,36},{8,0},{12,44},{16,24},{20,52},{24,16},{28,60},{32,40}... | collective-permute-start | bytes 786440 | tf_op jit(solution)/shard_map/gather_grad/ppermute | solution.py:39
  9.7 4.2 %collective-permute-done.1 = bf16[2,4,2,16,512]{4,3,2,1,0:T(8,128)(2,1)S(1)} collective-permute-done((bf16[2,4,2,16,512]{4,3,2,1,0:T(8,128)(2,1)S(1)}, bf16[2,4,2,16,512]{4,3,2,1,0:T(8,128)(2,1)S(1)}, u32[]{:S(2)}, u32[]{:S(2)}) %collective-permute-start.1) | collective-permute-done | bytes 262176 | tf_op jit(solution)/shard_map/gather_grad/ppermute | solution.py:39
  13.9 4.6 %collective-permute-start.2 = (bf16[2,2,4,2,16,512]{5,4,3,2,1,0:T(8,128)(2,1)S(1)}, bf16[2,2,4,2,16,512]{5,4,3,2,1,0:T(8,128)(2,1)S(1)}, u32[]{:S(2)}, u32[]{:S(2)}) collective-permute-start(bf16[2,2,4,2,16,512]{5,4,3,2,1,0:T(8,128)(2,1)S(1)} %pad_maximum_fusion.3), channel_id=1, source_target_pairs={{0,24},{4,100},{8,16},{12,108},{16,8},{20,116},{24,0},{28,124},{32... | collective-permute-start | bytes 1572872 | tf_op jit(solution)/shard_map/gather_grad/ppermute | solution.py:39
  18.7 10.7 %collective-permute-start.8 = (bf16[2,2,2,16,512]{4,3,2,1,0:T(8,128)(2,1)S(1)}, bf16[2,2,2,16,512]{4,3,2,1,0:T(8,128)(2,1)S(1)}, u32[]{:S(2)}, u32[]{:S(2)}) collective-permute-start(bf16[2,2,2,16,512]{4,3,2,1,0:T(8,128)(2,1)S(1)} %pad_maximum_fusion.12), channel_id=1, source_target_pairs={{0,384},{128,0},{256,128},{384,256},{1,385},{129,1},{257,129},{385... | collective-permute-start | bytes 393224 | tf_op jit(solution)/shard_map/exchange_modes/ppermute | solution.py:19
  29.4 5.2 %collective-permute-start.7 = (bf16[2,2,2,16,512]{4,3,2,1,0:T(8,128)(2,1)S(1)}, bf16[2,2,2,16,512]{4,3,2,1,0:T(8,128)(2,1)S(1)}, u32[]{:S(2)}, u32[]{:S(2)}) collective-permute-start(bf16[2,2,2,16,512]{4,3,2,1,0:T(8,128)(2,1)S(1)} %pad_maximum_fusion.11), channel_id=1, source_target_pairs={{0,256},{128,384},{256,0},{384,128},{1,257},{129,385},{257,1},{385... | collective-permute-start | bytes 393224 | tf_op jit(solution)/shard_map/exchange_modes/ppermute | solution.py:19
  34.7 3.1 %collective-permute-start.3 = (bf16[4,2,4,2,16,512]{5,4,3,2,1,0:T(8,128)(2,1)S(1)}, bf16[4,2,4,2,16,512]{5,4,3,2,1,0:T(8,128)(2,1)S(1)}, u32[]{:S(2)}, u32[]{:S(2)}) collective-permute-start(bf16[4,2,4,2,16,512]{5,4,3,2,1,0:T(8,128)(2,1)S(1)} %pad_maximum_fusion.refs_0_), channel_id=1, source_target_pairs={{0,32},{4,12},{8,40},{12,20},{16,48},{20,28},{24,56},{28,4},{32,64... | collective-permute-start | bytes 3145736 | tf_op jit(solution)/shard_map/gather_grad/ppermute | solution.py:39
  37.8 4.4 %collective-permute-start.4 = (bf16[4,2,4,2,16,512]{5,4,3,2,1,0:T(8,128)(2,1)S(1)}, bf16[4,2,4,2,16,512]{5,4,3,2,1,0:T(8,128)(2,1)S(1)}, u32[]{:S(2)}, u32[]{:S(2)}) collective-permute-start(bf16[4,2,4,2,16,512]{5,4,3,2,1,0:T(8,128)(2,1)S(1)} %pad_maximum_fusion.refs_0_), channel_id=1, source_target_pairs={{0,64},{4,20},{8,72},{12,28},{16,80},{20,4},{24,88},{28,12},{32,96... | collective-permute-start | bytes 3145736 | tf_op jit(solution)/shard_map/gather_grad/ppermute | solution.py:39
  42.2 3.1 %collective-permute-start.5 = (bf16[4,2,4,2,16,512]{5,4,3,2,1,0:T(8,128)(2,1)S(1)}, bf16[4,2,4,2,16,512]{5,4,3,2,1,0:T(8,128)(2,1)S(1)}, u32[]{:S(2)}, u32[]{:S(2)}) collective-permute-start(bf16[4,2,4,2,16,512]{5,4,3,2,1,0:T(8,128)(2,1)S(1)} %pad_maximum_fusion.refs_0_), channel_id=1, source_target_pairs={{0,96},{4,28},{8,104},{12,4},{16,112},{20,12},{24,120},{28,20},{32... | collective-permute-start | bytes 3145736 | tf_op jit(solution)/shard_map/gather_grad/ppermute | solution.py:39
  45.3 7.2 %collective-permute-start.6 = (bf16[2,2,2,16,512]{4,3,2,1,0:T(8,128)(2,1)S(1)}, bf16[2,2,2,16,512]{4,3,2,1,0:T(8,128)(2,1)S(1)}, u32[]{:S(2)}, u32[]{:S(2)}) collective-permute-start(bf16[2,2,2,16,512]{4,3,2,1,0:T(8,128)(2,1)S(1)} %pad_maximum_fusion.10), channel_id=1, source_target_pairs={{0,128},{128,256},{256,384},{384,0},{1,129},{129,257},{257,385},{3... | collective-permute-start | bytes 393224 | tf_op jit(solution)/shard_map/exchange_modes/ppermute | solution.py:19
  52.7 12.6 %collective-permute-done.6 = bf16[2,2,2,16,512]{4,3,2,1,0:T(8,128)(2,1)S(1)} collective-permute-done((bf16[2,2,2,16,512]{4,3,2,1,0:T(8,128)(2,1)S(1)}, bf16[2,2,2,16,512]{4,3,2,1,0:T(8,128)(2,1)S(1)}, u32[]{:S(2)}, u32[]{:S(2)}) %collective-permute-start.6) | collective-permute-done | bytes 131104 | tf_op jit(solution)/shard_map/exchange_modes/ppermute | solution.py:19
  72.2 4.4 %collective-permute-done.9.refs_9_ = bf16[2,4,2,16,512]{4,3,2,1,0:T(8,128)(2,1)S(1)} collective-permute-done((bf16[2,4,2,16,512]{4,3,2,1,0:T(8,128)(2,1)S(1)}, bf16[2,4,2,16,512]{4,3,2,1,0:T(8,128)(2,1)S(1)}, u32[]{:S(2)}, u32[]{:S(2)}) %collective-permute-start.9) | collective-permute-done | bytes 262176 | tf_op jit(solution)/shard_map/gather_rows/ppermute | solution.py:23
  78.6 4.9 %collective-permute-start.14 = (bf16[2,3,2,2,16,512]{5,4,3,2,1,0:T(8,128)(2,1)S(1)}, bf16[2,3,2,2,16,512]{5,4,3,2,1,0:T(8,128)(2,1)S(1)}, u32[]{:S(2)}, u32[]{:S(2)}) collective-permute-start(bf16[2,3,2,2,16,512]{5,4,3,2,1,0:T(8,128)(2,1)S(1)} %pad_maximum_fusion.5), channel_id=1, source_target_pairs={{0,24},{4,100},{8,16},{12,108},{16,8},{20,116},{24,0},{28,124},{32... | collective-permute-start | bytes 1179656 | tf_op jit(solution)/shard_map/gather_late_grad/ppermute | solution.py:39
  83.5 5.2 %collective-permute-done.14 = bf16[2,3,2,2,16,512]{5,4,3,2,1,0:T(8,128)(2,1)S(1)} collective-permute-done((bf16[2,3,2,2,16,512]{5,4,3,2,1,0:T(8,128)(2,1)S(1)}, bf16[2,3,2,2,16,512]{5,4,3,2,1,0:T(8,128)(2,1)S(1)}, u32[]{:S(2)}, u32[]{:S(2)}) %collective-permute-start.14) | collective-permute-done | bytes 393248 | tf_op jit(solution)/shard_map/gather_late_grad/ppermute | solution.py:39
  90.6 9.6 %collective-permute-start.16 = (bf16[4,3,2,2,16,512]{5,4,3,2,1,0:T(8,128)(2,1)S(1)}, bf16[4,3,2,2,16,512]{5,4,3,2,1,0:T(8,128)(2,1)S(1)}, u32[]{:S(2)}, u32[]{:S(2)}) collective-permute-start(bf16[4,3,2,2,16,512]{5,4,3,2,1,0:T(8,128)(2,1)S(1)} %pad_maximum_fusion.2.refs_4_), channel_id=1, source_target_pairs={{0,64},{4,20},{8,72},{12,28},{16,80},{20,4},{24,88},{28,12},{32,96... | collective-permute-start | bytes 2359304 | tf_op jit(solution)/shard_map/gather_late_grad/ppermute | solution.py:39
  104.3 3.6 %collective-permute-start.11 = (f32[4,2,2,16,512]{4,3,2,1,0:T(8,128)S(1)}, f32[4,2,2,16,512]{4,3,2,1,0:T(8,128)S(1)}, u32[]{:S(2)}, u32[]{:S(2)}) collective-permute-start(f32[4,2,2,16,512]{4,3,2,1,0:T(8,128)S(1)} %fusion), channel_id=1, source_target_pairs={{0,2},{1,3},{2,0},{3,1},{4,6},{5,7},{6,4},{7,5},{8,10},{9,11},{10,... | collective-permute-start | bytes 1572872 | tf_op jit(solution)/shard_map/sum_input/ppermute | solution.py:23
  107.9 14.9 %collective-permute-done.18.refs_10_ = bf16[2,2,4,2,16,512]{5,4,3,2,1,0:T(8,128)(2,1)S(1)} collective-permute-done((bf16[2,2,4,2,16,512]{5,4,3,2,1,0:T(8,128)(2,1)S(1)}, bf16[2,2,4,2,16,512]{5,4,3,2,1,0:T(8,128)(2,1)S(1)}, u32[]{:S(2)}, u32[]{:S(2)}) %collective-permute-start.18) | collective-permute-done | bytes 524320 | tf_op jit(solution)/shard_map/gather_rows/ppermute | solution.py:23
  122.8 4.1 %weight_terms.1 = bf16[2,2,64,512]{3,2,1,0:T(8,128)(2,1)S(1)} custom-call(s32[3]{0:T(128)S(1)} %pad_add_fusion.position, bf16[4,2,4,2,16,512]{5,4,3,2,1,0:T(8,128)(2,1)S(1)} %pad_maximum_fusion.refs_0_, bf16[4,2,4,2,16,512]{5,4,3,2,1,0:T(8,128)(2,1)S(1)} %collective-permute-done.3.refs_1_, ...), custom_call_target="tpu_custom_call" | custom-call | flops 1073741824 | bytes 5242880 | tf_op jit(solution)/shard_map/weight_terms/pallas_call | solution.py:219
  127.0 3.4 %collective-permute-start.19 = (bf16[2,64,512]{2,1,0:T(8,128)(2,1)S(1)}, bf16[2,64,512]{2,1,0:T(8,128)(2,1)S(1)}, u32[]{:S(2)}, u32[]{:S(2)}) collective-permute-start(bf16[2,64,512]{2,1,0:T(8,128)(2,1)S(1)} %get-tuple-element.11), channel_id=1, source_target_pairs={{0,4},{4,0},{8,12},{12,8},{16,20},{20,16},{24,28},{28,24},{32,36},... | collective-permute-start | bytes 393224 | tf_op jit(solution)/shard_map/spread_weight/ppermute | solution.py:23
  131.3 4.1 %collective-permute-start.20 = (bf16[2,2,64,512]{3,2,1,0:T(8,128)(2,1)S(1)}, bf16[2,2,64,512]{3,2,1,0:T(8,128)(2,1)S(1)}, u32[]{:S(2)}, u32[]{:S(2)}) collective-permute-start(bf16[2,2,64,512]{3,2,1,0:T(8,128)(2,1)S(1)} %pad_maximum_fusion.8.own), channel_id=1, source_target_pairs={{0,128},{128,256},{256,384},{384,0},{1,129},{129,257},{257,385},{3... | collective-permute-start | bytes 786440 | tf_op jit(solution)/shard_map/spread_weight/ppermute | solution.py:19
  135.4 8.8 %collective-permute-start.21 = (bf16[2,2,64,512]{3,2,1,0:T(8,128)(2,1)S(1)}, bf16[2,2,64,512]{3,2,1,0:T(8,128)(2,1)S(1)}, u32[]{:S(2)}, u32[]{:S(2)}) collective-permute-start(bf16[2,2,64,512]{3,2,1,0:T(8,128)(2,1)S(1)} %pad_maximum_fusion.8.own), channel_id=1, source_target_pairs={{0,256},{128,384},{256,0},{384,128},{1,257},{129,385},{257,1},{385... | collective-permute-start | bytes 786440 | tf_op jit(solution)/shard_map/spread_weight/ppermute | solution.py:19
  144.3 5.7 %collective-permute-start.22 = (bf16[2,2,64,512]{3,2,1,0:T(8,128)(2,1)S(1)}, bf16[2,2,64,512]{3,2,1,0:T(8,128)(2,1)S(1)}, u32[]{:S(2)}, u32[]{:S(2)}) collective-permute-start(bf16[2,2,64,512]{3,2,1,0:T(8,128)(2,1)S(1)} %pad_maximum_fusion.8.own), channel_id=1, source_target_pairs={{0,384},{128,0},{256,128},{384,256},{1,385},{129,1},{257,129},{385... | collective-permute-start | bytes 786440 | tf_op jit(solution)/shard_map/spread_weight/ppermute | solution.py:19
  150.2 3.1 %collective-permute-start.12 = (bf16[4,2,16,512]{3,2,1,0:T(8,128)(2,1)S(1)}, bf16[4,2,16,512]{3,2,1,0:T(8,128)(2,1)S(1)}, u32[]{:S(2)}, u32[]{:S(2)}) collective-permute-start(bf16[4,2,16,512]{3,2,1,0:T(8,128)(2,1)S(1)} %get-tuple-element.15), channel_id=1, source_target_pairs={{0,4},{4,0},{8,12},{12,8},{16,20},{20,16},{24,28},{28,24},{32,36},... | collective-permute-start | bytes 393224 | tf_op jit(solution)/shard_map/sum_input/ppermute | solution.py:23
  154.2 18.3 %collective-permute-done.21.far = bf16[2,2,64,512]{3,2,1,0:T(8,128)(2,1)S(1)} collective-permute-done((bf16[2,2,64,512]{3,2,1,0:T(8,128)(2,1)S(1)}, bf16[2,2,64,512]{3,2,1,0:T(8,128)(2,1)S(1)}, u32[]{:S(2)}, u32[]{:S(2)}) %collective-permute-start.21) | collective-permute-done | bytes 262176 | tf_op jit(solution)/shard_map/spread_weight/ppermute | solution.py:19
  172.5 20.6 %collective-permute-done.22.ahead = bf16[2,2,64,512]{3,2,1,0:T(8,128)(2,1)S(1)} collective-permute-done((bf16[2,2,64,512]{3,2,1,0:T(8,128)(2,1)S(1)}, bf16[2,2,64,512]{3,2,1,0:T(8,128)(2,1)S(1)}, u32[]{:S(2)}, u32[]{:S(2)}) %collective-permute-start.22) | collective-permute-done | bytes 262176 | tf_op jit(solution)/shard_map/spread_weight/ppermute | solution.py:19
  (58 shorter events, 26.8 us)
Async XLA Ops:
  1.9 4.5 %collective-permute-start = (bf16[4,2,96,512]{3,2,1,0:T(8,128)(2,1)S(1)}, bf16[4,2,96,512]{3,2,1,0:T(8,128)(2,1)S(1)}, u32[]{:S(2)}, u32[]{:S(2)}) collective-permute-start(bf16[4,2,96,512]{3,2,1,0:T(8,128)(2,1)S(1)} %pad_maximum_fusion.1), channel_id=1, source_target_pairs={{0,4},{4,0},{8,12},{12,8},{16,20},{20,16},{24,28},{28,24},{32,36},... | collective-permute-start | bytes 2359304 | tf_op jit(solution)/shard_map/swap_modes/ppermute | solution.py:23
  6.5 7.4 %collective-permute-start.1 = (bf16[2,4,2,16,512]{4,3,2,1,0:T(8,128)(2,1)S(1)}, bf16[2,4,2,16,512]{4,3,2,1,0:T(8,128)(2,1)S(1)}, u32[]{:S(2)}, u32[]{:S(2)}) collective-permute-start(bf16[2,4,2,16,512]{4,3,2,1,0:T(8,128)(2,1)S(1)} %get-tuple-element.26), channel_id=1, source_target_pairs={{0,8},{4,36},{8,0},{12,44},{16,24},{20,52},{24,16},{28,60},{32,40}... | collective-permute-start | bytes 786440 | tf_op jit(solution)/shard_map/gather_grad/ppermute | solution.py:39
  13.9 20.6 %collective-permute-start.2 = (bf16[2,2,4,2,16,512]{5,4,3,2,1,0:T(8,128)(2,1)S(1)}, bf16[2,2,4,2,16,512]{5,4,3,2,1,0:T(8,128)(2,1)S(1)}, u32[]{:S(2)}, u32[]{:S(2)}) collective-permute-start(bf16[2,2,4,2,16,512]{5,4,3,2,1,0:T(8,128)(2,1)S(1)} %pad_maximum_fusion.3), channel_id=1, source_target_pairs={{0,24},{4,100},{8,16},{12,108},{16,8},{20,116},{24,0},{28,124},{32... | collective-permute-start | bytes 1572872 | tf_op jit(solution)/shard_map/gather_grad/ppermute | solution.py:39
  18.7 26.6 %collective-permute-start.8 = (bf16[2,2,2,16,512]{4,3,2,1,0:T(8,128)(2,1)S(1)}, bf16[2,2,2,16,512]{4,3,2,1,0:T(8,128)(2,1)S(1)}, u32[]{:S(2)}, u32[]{:S(2)}) collective-permute-start(bf16[2,2,2,16,512]{4,3,2,1,0:T(8,128)(2,1)S(1)} %pad_maximum_fusion.12), channel_id=1, source_target_pairs={{0,384},{128,0},{256,128},{384,256},{1,385},{129,1},{257,129},{385... | collective-permute-start | bytes 393224 | tf_op jit(solution)/shard_map/exchange_modes/ppermute | solution.py:19
  29.4 23.3 %collective-permute-start.7 = (bf16[2,2,2,16,512]{4,3,2,1,0:T(8,128)(2,1)S(1)}, bf16[2,2,2,16,512]{4,3,2,1,0:T(8,128)(2,1)S(1)}, u32[]{:S(2)}, u32[]{:S(2)}) collective-permute-start(bf16[2,2,2,16,512]{4,3,2,1,0:T(8,128)(2,1)S(1)} %pad_maximum_fusion.11), channel_id=1, source_target_pairs={{0,256},{128,384},{256,0},{384,128},{1,257},{129,385},{257,1},{385... | collective-permute-start | bytes 393224 | tf_op jit(solution)/shard_map/exchange_modes/ppermute | solution.py:19
  34.7 34.6 %collective-permute-start.3 = (bf16[4,2,4,2,16,512]{5,4,3,2,1,0:T(8,128)(2,1)S(1)}, bf16[4,2,4,2,16,512]{5,4,3,2,1,0:T(8,128)(2,1)S(1)}, u32[]{:S(2)}, u32[]{:S(2)}) collective-permute-start(bf16[4,2,4,2,16,512]{5,4,3,2,1,0:T(8,128)(2,1)S(1)} %pad_maximum_fusion.refs_0_), channel_id=1, source_target_pairs={{0,32},{4,12},{8,40},{12,20},{16,48},{20,28},{24,56},{28,4},{32,64... | collective-permute-start | bytes 3145736 | tf_op jit(solution)/shard_map/gather_grad/ppermute | solution.py:39
  37.8 31.5 %collective-permute-start.4 = (bf16[4,2,4,2,16,512]{5,4,3,2,1,0:T(8,128)(2,1)S(1)}, bf16[4,2,4,2,16,512]{5,4,3,2,1,0:T(8,128)(2,1)S(1)}, u32[]{:S(2)}, u32[]{:S(2)}) collective-permute-start(bf16[4,2,4,2,16,512]{5,4,3,2,1,0:T(8,128)(2,1)S(1)} %pad_maximum_fusion.refs_0_), channel_id=1, source_target_pairs={{0,64},{4,20},{8,72},{12,28},{16,80},{20,4},{24,88},{28,12},{32,96... | collective-permute-start | bytes 3145736 | tf_op jit(solution)/shard_map/gather_grad/ppermute | solution.py:39
  42.2 27.1 %collective-permute-start.5 = (bf16[4,2,4,2,16,512]{5,4,3,2,1,0:T(8,128)(2,1)S(1)}, bf16[4,2,4,2,16,512]{5,4,3,2,1,0:T(8,128)(2,1)S(1)}, u32[]{:S(2)}, u32[]{:S(2)}) collective-permute-start(bf16[4,2,4,2,16,512]{5,4,3,2,1,0:T(8,128)(2,1)S(1)} %pad_maximum_fusion.refs_0_), channel_id=1, source_target_pairs={{0,96},{4,28},{8,104},{12,4},{16,112},{20,12},{24,120},{28,20},{32... | collective-permute-start | bytes 3145736 | tf_op jit(solution)/shard_map/gather_grad/ppermute | solution.py:39
  45.3 24.1 %copy-start = (bf16[8,2,64,512]{3,2,1,0:T(8,128)(2,1)S(1)}, bf16[8,2,64,512]{3,2,1,0:T(8,128)(2,1)}, u32[]{:S(2)}) copy-start(bf16[8,2,64,512]{3,2,1,0:T(8,128)(2,1)} %w.1) | copy-start | bytes 3145732
  45.3 20.0 %collective-permute-start.6 = (bf16[2,2,2,16,512]{4,3,2,1,0:T(8,128)(2,1)S(1)}, bf16[2,2,2,16,512]{4,3,2,1,0:T(8,128)(2,1)S(1)}, u32[]{:S(2)}, u32[]{:S(2)}) collective-permute-start(bf16[2,2,2,16,512]{4,3,2,1,0:T(8,128)(2,1)S(1)} %pad_maximum_fusion.10), channel_id=1, source_target_pairs={{0,128},{128,256},{256,384},{384,0},{1,129},{129,257},{257,385},{3... | collective-permute-start | bytes 393224 | tf_op jit(solution)/shard_map/exchange_modes/ppermute | solution.py:19
  65.3 11.3 %collective-permute-start.9 = (bf16[2,4,2,16,512]{4,3,2,1,0:T(8,128)(2,1)S(1)}, bf16[2,4,2,16,512]{4,3,2,1,0:T(8,128)(2,1)S(1)}, u32[]{:S(2)}, u32[]{:S(2)}) collective-permute-start(bf16[2,4,2,16,512]{4,3,2,1,0:T(8,128)(2,1)S(1)} %get-tuple-element.13.refs_8_), channel_id=1, source_target_pairs={{0,2},{1,3},{2,0},{3,1},{4,6},{5,7},{6,4},{7,5},{8,10},{9,11},{10,... | collective-permute-start | bytes 786440 | tf_op jit(solution)/shard_map/gather_rows/ppermute | solution.py:23
  67.3 11.2 %collective-permute-start.13 = (bf16[3,2,2,16,512]{4,3,2,1,0:T(8,128)(2,1)S(1)}, bf16[3,2,2,16,512]{4,3,2,1,0:T(8,128)(2,1)S(1)}, u32[]{:S(2)}, u32[]{:S(2)}) collective-permute-start(bf16[3,2,2,16,512]{4,3,2,1,0:T(8,128)(2,1)S(1)} %get-tuple-element.30), channel_id=1, source_target_pairs={{0,8},{4,36},{8,0},{12,44},{16,24},{20,52},{24,16},{28,60},{32,40}... | collective-permute-start | bytes 589832 | tf_op jit(solution)/shard_map/gather_late_grad/ppermute | solution.py:39
  76.6 27.6 %collective-permute-start.10 = (f32[2,4,2,2,16,512]{5,4,3,2,1,0:T(8,128)S(1)}, f32[2,4,2,2,16,512]{5,4,3,2,1,0:T(8,128)S(1)}, u32[]{:S(2)}, u32[]{:S(2)}) collective-permute-start(f32[2,4,2,2,16,512]{5,4,3,2,1,0:T(8,128)S(1)} %get-tuple-element.7), channel_id=1, source_target_pairs={{0,1},{1,0},{2,3},{3,2},{4,5},{5,4},{6,7},{7,6},{8,9},{9,8},{10,11... | collective-permute-start | bytes 3145736 | tf_op jit(solution)/shard_map/sum_input/ppermute | solution.py:23
  78.6 10.1 %collective-permute-start.14 = (bf16[2,3,2,2,16,512]{5,4,3,2,1,0:T(8,128)(2,1)S(1)}, bf16[2,3,2,2,16,512]{5,4,3,2,1,0:T(8,128)(2,1)S(1)}, u32[]{:S(2)}, u32[]{:S(2)}) collective-permute-start(bf16[2,3,2,2,16,512]{5,4,3,2,1,0:T(8,128)(2,1)S(1)} %pad_maximum_fusion.5), channel_id=1, source_target_pairs={{0,24},{4,100},{8,16},{12,108},{16,8},{20,116},{24,0},{28,124},{32... | collective-permute-start | bytes 1179656 | tf_op jit(solution)/shard_map/gather_late_grad/ppermute | solution.py:39
  88.7 34.1 %collective-permute-start.15 = (bf16[4,3,2,2,16,512]{5,4,3,2,1,0:T(8,128)(2,1)S(1)}, bf16[4,3,2,2,16,512]{5,4,3,2,1,0:T(8,128)(2,1)S(1)}, u32[]{:S(2)}, u32[]{:S(2)}) collective-permute-start(bf16[4,3,2,2,16,512]{5,4,3,2,1,0:T(8,128)(2,1)S(1)} %pad_maximum_fusion.2.refs_4_), channel_id=1, source_target_pairs={{0,32},{4,12},{8,40},{12,20},{16,48},{20,28},{24,56},{28,4},{32,64... | collective-permute-start | bytes 2359304 | tf_op jit(solution)/shard_map/gather_late_grad/ppermute | solution.py:39
  90.6 32.1 %collective-permute-start.16 = (bf16[4,3,2,2,16,512]{5,4,3,2,1,0:T(8,128)(2,1)S(1)}, bf16[4,3,2,2,16,512]{5,4,3,2,1,0:T(8,128)(2,1)S(1)}, u32[]{:S(2)}, u32[]{:S(2)}) collective-permute-start(bf16[4,3,2,2,16,512]{5,4,3,2,1,0:T(8,128)(2,1)S(1)} %pad_maximum_fusion.2.refs_4_), channel_id=1, source_target_pairs={{0,64},{4,20},{8,72},{12,28},{16,80},{20,4},{24,88},{28,12},{32,96... | collective-permute-start | bytes 2359304 | tf_op jit(solution)/shard_map/gather_late_grad/ppermute | solution.py:39
  100.2 22.5 %collective-permute-start.17 = (bf16[4,3,2,2,16,512]{5,4,3,2,1,0:T(8,128)(2,1)S(1)}, bf16[4,3,2,2,16,512]{5,4,3,2,1,0:T(8,128)(2,1)S(1)}, u32[]{:S(2)}, u32[]{:S(2)}) collective-permute-start(bf16[4,3,2,2,16,512]{5,4,3,2,1,0:T(8,128)(2,1)S(1)} %pad_maximum_fusion.2.refs_4_), channel_id=1, source_target_pairs={{0,96},{4,28},{8,104},{12,4},{16,112},{20,12},{24,120},{28,20},{32... | collective-permute-start | bytes 2359304 | tf_op jit(solution)/shard_map/gather_late_grad/ppermute | solution.py:39
  102.2 20.5 %collective-permute-start.18 = (bf16[2,2,4,2,16,512]{5,4,3,2,1,0:T(8,128)(2,1)S(1)}, bf16[2,2,4,2,16,512]{5,4,3,2,1,0:T(8,128)(2,1)S(1)}, u32[]{:S(2)}, u32[]{:S(2)}) collective-permute-start(bf16[2,2,4,2,16,512]{5,4,3,2,1,0:T(8,128)(2,1)S(1)} %pad_maximum_fusion.4), channel_id=1, source_target_pairs={{0,1},{1,0},{2,3},{3,2},{4,5},{5,4},{6,7},{7,6},{8,9},{9,8},{10,11... | collective-permute-start | bytes 1572872 | tf_op jit(solution)/shard_map/gather_rows/ppermute | solution.py:23
  104.3 45.7 %collective-permute-start.11 = (f32[4,2,2,16,512]{4,3,2,1,0:T(8,128)S(1)}, f32[4,2,2,16,512]{4,3,2,1,0:T(8,128)S(1)}, u32[]{:S(2)}, u32[]{:S(2)}) collective-permute-start(f32[4,2,2,16,512]{4,3,2,1,0:T(8,128)S(1)} %fusion), channel_id=1, source_target_pairs={{0,2},{1,3},{2,0},{3,1},{4,6},{5,7},{6,4},{7,5},{8,10},{9,11},{10,... | collective-permute-start | bytes 1572872 | tf_op jit(solution)/shard_map/sum_input/ppermute | solution.py:23
  127.0 4.3 %collective-permute-start.19 = (bf16[2,64,512]{2,1,0:T(8,128)(2,1)S(1)}, bf16[2,64,512]{2,1,0:T(8,128)(2,1)S(1)}, u32[]{:S(2)}, u32[]{:S(2)}) collective-permute-start(bf16[2,64,512]{2,1,0:T(8,128)(2,1)S(1)} %get-tuple-element.11), channel_id=1, source_target_pairs={{0,4},{4,0},{8,12},{12,8},{16,20},{20,16},{24,28},{28,24},{32,36},... | collective-permute-start | bytes 393224 | tf_op jit(solution)/shard_map/spread_weight/ppermute | solution.py:23
  131.3 22.9 %collective-permute-start.20 = (bf16[2,2,64,512]{3,2,1,0:T(8,128)(2,1)S(1)}, bf16[2,2,64,512]{3,2,1,0:T(8,128)(2,1)S(1)}, u32[]{:S(2)}, u32[]{:S(2)}) collective-permute-start(bf16[2,2,64,512]{3,2,1,0:T(8,128)(2,1)S(1)} %pad_maximum_fusion.8.own), channel_id=1, source_target_pairs={{0,128},{128,256},{256,384},{384,0},{1,129},{129,257},{257,385},{3... | collective-permute-start | bytes 786440 | tf_op jit(solution)/shard_map/spread_weight/ppermute | solution.py:19
  135.4 37.0 %collective-permute-start.21 = (bf16[2,2,64,512]{3,2,1,0:T(8,128)(2,1)S(1)}, bf16[2,2,64,512]{3,2,1,0:T(8,128)(2,1)S(1)}, u32[]{:S(2)}, u32[]{:S(2)}) collective-permute-start(bf16[2,2,64,512]{3,2,1,0:T(8,128)(2,1)S(1)} %pad_maximum_fusion.8.own), channel_id=1, source_target_pairs={{0,256},{128,384},{256,0},{384,128},{1,257},{129,385},{257,1},{385... | collective-permute-start | bytes 786440 | tf_op jit(solution)/shard_map/spread_weight/ppermute | solution.py:19
  144.3 48.8 %collective-permute-start.22 = (bf16[2,2,64,512]{3,2,1,0:T(8,128)(2,1)S(1)}, bf16[2,2,64,512]{3,2,1,0:T(8,128)(2,1)S(1)}, u32[]{:S(2)}, u32[]{:S(2)}) collective-permute-start(bf16[2,2,64,512]{3,2,1,0:T(8,128)(2,1)S(1)} %pad_maximum_fusion.8.own), channel_id=1, source_target_pairs={{0,384},{128,0},{256,128},{384,256},{1,385},{129,1},{257,129},{385... | collective-permute-start | bytes 786440 | tf_op jit(solution)/shard_map/spread_weight/ppermute | solution.py:19
  150.2 45.8 %collective-permute-start.12 = (bf16[4,2,16,512]{3,2,1,0:T(8,128)(2,1)S(1)}, bf16[4,2,16,512]{3,2,1,0:T(8,128)(2,1)S(1)}, u32[]{:S(2)}, u32[]{:S(2)}) collective-permute-start(bf16[4,2,16,512]{3,2,1,0:T(8,128)(2,1)S(1)} %get-tuple-element.15), channel_id=1, source_target_pairs={{0,4},{4,0},{8,12},{12,8},{16,20},{20,16},{24,28},{28,24},{32,36},... | collective-permute-start | bytes 393224 | tf_op jit(solution)/shard_map/sum_input/ppermute | solution.py:23
  (2 other events, 2.3 us)

commit v4 on v3

--- a/solution.py
+++ b/solution.py
@@ -108,7 +108,7 @@
 
 
 def weight_terms(position, *refs):
-    pieces, late, (x0, x1, x2, out, grads, rows, sem) = refs[:4], refs[4:8], refs[8:]
+    pieces, late, (x0, x1, x2, here, there, grads, rows, sem) = refs[:4], refs[4:8], refs[8:]
     mode = position[0]
     fetch_plane(
         position,
@@ -143,16 +143,17 @@
             jnp.concatenate([imag, real], axis=0), grads[block, 1], contract, preferred_element_type=jnp.float32
         )
     for part in range(2):
-        for source in range(2):
+        for source, out in enumerate((here, there)):
             start = part * 128 + source * 64
-            out[source, part] = total[start : start + 64].astype(jnp.bfloat16)
-
-
-def place_modes(position, own, back, far, ahead, out, sem):
-    for step, piece in enumerate((own, back, far, ahead)):
+            out[part] = total[start : start + 64].astype(jnp.bfloat16)
+
+
+def place_modes(position, *refs):
+    pieces, (out, sem) = refs[:8], refs[8:]
+    for step in range(4):
         for slot in range(2):
             mode = ((position[1] & 1) ^ slot) * 4 + ((position[0] + HEARD[step]) & 3)
-            pltpu.make_async_copy(piece.at[slot], out.at[mode], sem).start()
+            pltpu.make_async_copy(pieces[2 * step + slot], out.at[mode], sem).start()
     pltpu.make_async_copy(out, out, sem).wait()
 
 
@@ -216,11 +217,11 @@
 
     with jax.named_scope("gather_late_grad"):
         late_held = second_hops(late_line)
-    terms = pl.pallas_call(
+    here, there = pl.pallas_call(
         weight_terms,
-        out_shape=jax.ShapeDtypeStruct((2, 2, 64, 512), jnp.bfloat16),
+        out_shape=[jax.ShapeDtypeStruct((2, 64, 512), jnp.bfloat16)] * 2,
         in_specs=[SMEM] + [ANY] * 11,
-        out_specs=VMEM,
+        out_specs=[VMEM] * 2,
         scratch_shapes=[
             pltpu.VMEM((4, 2, 512, 512), jnp.bfloat16),
             pltpu.VMEM((4, 2, 128, 512), jnp.bfloat16),
@@ -232,18 +233,20 @@
     )(position, *held, *late_held, xs, xs_across, xs_beside)
 
     with jax.named_scope("spread_weight"):
-        finished = jnp.stack([terms[0], swap_cores(terms[1])])
-        spread = [ring(finished, "dp", shift) for shift in SHIFTS]
+        back_0, ahead_0 = ring(here, "dp", 1), ring(here, "dp", 3)
+        other = swap_cores(there)
+        back_1, ahead_1 = ring(other, "dp", 1), ring(other, "dp", 3)
+        far_0, far_1 = ring(back_0, "dp", 1), ring(ahead_1, "dp", 3)
     weight_grad = pl.pallas_call(
         place_modes,
         out_shape=jax.ShapeDtypeStruct(weight.shape, jnp.bfloat16),
-        in_specs=[SMEM] + [ANY] * 4,
+        in_specs=[SMEM] + [ANY] * 8,
         out_specs=VMEM,
         scratch_shapes=[pltpu.SemaphoreType.DMA],
         compiler_params=pltpu.CompilerParams(vmem_limit_bytes=8 * MIB),
         cost_estimate=pl.CostEstimate(flops=0, bytes_accessed=2 * MIB, transcendentals=0),
         name="place_modes",
-    )(position, finished, *spread)
+    )(position, here, other, back_0, back_1, far_0, far_1, ahead_0, ahead_1)
     return (spectrum_grad, weight_grad)
 
 

time: 197 us -> 185 us (0.939)
  the two profiles are of different devices: /device:TPU:65 before, /device:TPU:1 now
where the time goes in v4:
time: 185 us; the launch traced here: 184 us
  starting transfers between devices  113 us (61%)
  waiting for transfers between devices  56.9 us (31%)
  Pallas kernels  9.9 us (5%)
    ppermute x9, starting transfers between devices, ring(): return lax.ppermute(value, axis, [(i, (i + shift) % 4) for i in range(4)])  50.4 us
    ppermute x7, starting transfers between devices, flip(): return lax.ppermute(value, axis, [(i, i ^ bits) for i in range(size)])  34.5 us
    ppermute x10, starting transfers between devices, hop(): return lax.ppermute(value, 'cin', pairs)  28.5 us
    ppermute x7, waiting for transfers between devices, flip(): return lax.ppermute(value, axis, [(i, i ^ bits) for i in range(size)])  24.9 us
    ppermute x9, waiting for transfers between devices, ring(): return lax.ppermute(value, axis, [(i, (i + shift) % 4) for i in range(4)])  18.4 us
    ppermute x10, waiting for transfers between devices, hop(): return lax.ppermute(value, 'cin', pairs)  13.6 us
    pallas_call x1, Pallas kernels, on_device(): pl.pallas_call(weight_terms, out_shape=[jax.ShapeDtypeStruct((2, 64, 512)...  4.14 us
  transfers between devices with their start and end apart: 26, of which 9 were waited for; matrix products, arithmetic and copies ran while one was open for 0% of the time, Pallas kernels for 5%

profile of v4, /device:TPU:1, one launch (start us, length us, event | category | flops | bytes accessed | tf_op | source)
XLA Modules:
  0.0 184.3 jit_solution(13559580429166523246)
XLA Ops:
  1.9 8.8 %collective-permute-start = (bf16[4,2,96,512]{3,2,1,0:T(8,128)(2,1)S(1)}, bf16[4,2,96,512]{3,2,1,0:T(8,128)(2,1)S(1)}, u32[]{:S(2)}, u32[]{:S(2)}) collective-permute-start(bf16[4,2,96,512]{3,2,1,0:T(8,128)(2,1)S(1)} %pad_maximum_fusion.1), channel_id=1, source_target_pairs={{0,4},{4,0},{8,12},{12,8},{16,20},{20,16},{24,28},{28,24},{32,36},... | collective-permute-start | bytes 2359304 | tf_op jit(solution)/shard_map/swap_modes/ppermute | solution.py:23
  14.6 5.5 %collective-permute-done.1 = bf16[2,4,2,16,512]{4,3,2,1,0:T(8,128)(2,1)S(1)} collective-permute-done((bf16[2,4,2,16,512]{4,3,2,1,0:T(8,128)(2,1)S(1)}, bf16[2,4,2,16,512]{4,3,2,1,0:T(8,128)(2,1)S(1)}, u32[]{:S(2)}, u32[]{:S(2)}) %collective-permute-start.1) | collective-permute-done | bytes 262176 | tf_op jit(solution)/shard_map/gather_grad/ppermute | solution.py:39
  22.2 9.8 %collective-permute-start.8 = (bf16[2,2,2,16,512]{4,3,2,1,0:T(8,128)(2,1)S(1)}, bf16[2,2,2,16,512]{4,3,2,1,0:T(8,128)(2,1)S(1)}, u32[]{:S(2)}, u32[]{:S(2)}) collective-permute-start(bf16[2,2,2,16,512]{4,3,2,1,0:T(8,128)(2,1)S(1)} %pad_maximum_fusion.11), channel_id=1, source_target_pairs={{0,384},{128,0},{256,128},{384,256},{1,385},{129,1},{257,129},{385... | collective-permute-start | bytes 393224 | tf_op jit(solution)/shard_map/exchange_modes/ppermute | solution.py:19
  32.0 4.9 %collective-permute-start.7 = (bf16[2,2,2,16,512]{4,3,2,1,0:T(8,128)(2,1)S(1)}, bf16[2,2,2,16,512]{4,3,2,1,0:T(8,128)(2,1)S(1)}, u32[]{:S(2)}, u32[]{:S(2)}) collective-permute-start(bf16[2,2,2,16,512]{4,3,2,1,0:T(8,128)(2,1)S(1)} %pad_maximum_fusion.10), channel_id=1, source_target_pairs={{0,256},{128,384},{256,0},{384,128},{1,257},{129,385},{257,1},{385... | collective-permute-start | bytes 393224 | tf_op jit(solution)/shard_map/exchange_modes/ppermute | solution.py:19
  37.1 3.1 %collective-permute-start.3 = (bf16[4,2,4,2,16,512]{5,4,3,2,1,0:T(8,128)(2,1)S(1)}, bf16[4,2,4,2,16,512]{5,4,3,2,1,0:T(8,128)(2,1)S(1)}, u32[]{:S(2)}, u32[]{:S(2)}) collective-permute-start(bf16[4,2,4,2,16,512]{5,4,3,2,1,0:T(8,128)(2,1)S(1)} %pad_maximum_fusion.refs_0_), channel_id=1, source_target_pairs={{0,32},{4,12},{8,40},{12,20},{16,48},{20,28},{24,56},{28,4},{32,64... | collective-permute-start | bytes 3145736 | tf_op jit(solution)/shard_map/gather_grad/ppermute | solution.py:39
  40.2 4.4 %collective-permute-start.4 = (bf16[4,2,4,2,16,512]{5,4,3,2,1,0:T(8,128)(2,1)S(1)}, bf16[4,2,4,2,16,512]{5,4,3,2,1,0:T(8,128)(2,1)S(1)}, u32[]{:S(2)}, u32[]{:S(2)}) collective-permute-start(bf16[4,2,4,2,16,512]{5,4,3,2,1,0:T(8,128)(2,1)S(1)} %pad_maximum_fusion.refs_0_), channel_id=1, source_target_pairs={{0,64},{4,20},{8,72},{12,28},{16,80},{20,4},{24,88},{28,12},{32,96... | collective-permute-start | bytes 3145736 | tf_op jit(solution)/shard_map/gather_grad/ppermute | solution.py:39
  44.6 3.1 %collective-permute-start.5 = (bf16[4,2,4,2,16,512]{5,4,3,2,1,0:T(8,128)(2,1)S(1)}, bf16[4,2,4,2,16,512]{5,4,3,2,1,0:T(8,128)(2,1)S(1)}, u32[]{:S(2)}, u32[]{:S(2)}) collective-permute-start(bf16[4,2,4,2,16,512]{5,4,3,2,1,0:T(8,128)(2,1)S(1)} %pad_maximum_fusion.refs_0_), channel_id=1, source_target_pairs={{0,96},{4,28},{8,104},{12,4},{16,112},{20,12},{24,120},{28,20},{32... | collective-permute-start | bytes 3145736 | tf_op jit(solution)/shard_map/gather_grad/ppermute | solution.py:39
  47.7 7.4 %collective-permute-start.6 = (bf16[2,2,2,16,512]{4,3,2,1,0:T(8,128)(2,1)S(1)}, bf16[2,2,2,16,512]{4,3,2,1,0:T(8,128)(2,1)S(1)}, u32[]{:S(2)}, u32[]{:S(2)}) collective-permute-start(bf16[2,2,2,16,512]{4,3,2,1,0:T(8,128)(2,1)S(1)} %pad_maximum_fusion.9), channel_id=1, source_target_pairs={{0,128},{128,256},{256,384},{384,0},{1,129},{129,257},{257,385},{3... | collective-permute-start | bytes 393224 | tf_op jit(solution)/shard_map/exchange_modes/ppermute | solution.py:19
  55.1 3.9 %collective-permute-done.6 = bf16[2,2,2,16,512]{4,3,2,1,0:T(8,128)(2,1)S(1)} collective-permute-done((bf16[2,2,2,16,512]{4,3,2,1,0:T(8,128)(2,1)S(1)}, bf16[2,2,2,16,512]{4,3,2,1,0:T(8,128)(2,1)S(1)}, u32[]{:S(2)}, u32[]{:S(2)}) %collective-permute-start.6) | collective-permute-done | bytes 131104 | tf_op jit(solution)/shard_map/exchange_modes/ppermute | solution.py:19
  59.1 12.0 %collective-permute-start.9 = (bf16[2,4,2,16,512]{4,3,2,1,0:T(8,128)(2,1)S(1)}, bf16[2,4,2,16,512]{4,3,2,1,0:T(8,128)(2,1)S(1)}, u32[]{:S(2)}, u32[]{:S(2)}) collective-permute-start(bf16[2,4,2,16,512]{4,3,2,1,0:T(8,128)(2,1)S(1)} %get-tuple-element.15.refs_8_), channel_id=1, source_target_pairs={{0,2},{1,3},{2,0},{3,1},{4,6},{5,7},{6,4},{7,5},{8,10},{9,11},{10,... | collective-permute-start | bytes 786440 | tf_op jit(solution)/shard_map/gather_rows/ppermute | solution.py:23
  76.0 5.1 %collective-permute-done.9.refs_9_ = bf16[2,4,2,16,512]{4,3,2,1,0:T(8,128)(2,1)S(1)} collective-permute-done((bf16[2,4,2,16,512]{4,3,2,1,0:T(8,128)(2,1)S(1)}, bf16[2,4,2,16,512]{4,3,2,1,0:T(8,128)(2,1)S(1)}, u32[]{:S(2)}, u32[]{:S(2)}) %collective-permute-start.9) | collective-permute-done | bytes 262176 | tf_op jit(solution)/shard_map/gather_rows/ppermute | solution.py:23
  85.1 8.1 %collective-permute-done.14 = bf16[2,3,2,2,16,512]{5,4,3,2,1,0:T(8,128)(2,1)S(1)} collective-permute-done((bf16[2,3,2,2,16,512]{5,4,3,2,1,0:T(8,128)(2,1)S(1)}, bf16[2,3,2,2,16,512]{5,4,3,2,1,0:T(8,128)(2,1)S(1)}, u32[]{:S(2)}, u32[]{:S(2)}) %collective-permute-start.14) | collective-permute-done | bytes 393248 | tf_op jit(solution)/shard_map/gather_late_grad/ppermute | solution.py:39
  95.2 6.4 %collective-permute-start.16 = (bf16[4,3,2,2,16,512]{5,4,3,2,1,0:T(8,128)(2,1)S(1)}, bf16[4,3,2,2,16,512]{5,4,3,2,1,0:T(8,128)(2,1)S(1)}, u32[]{:S(2)}, u32[]{:S(2)}) collective-permute-start(bf16[4,3,2,2,16,512]{5,4,3,2,1,0:T(8,128)(2,1)S(1)} %pad_maximum_fusion.2.refs_4_), channel_id=1, source_target_pairs={{0,64},{4,20},{8,72},{12,28},{16,80},{20,4},{24,88},{28,12},{32,96... | collective-permute-start | bytes 2359304 | tf_op jit(solution)/shard_map/gather_late_grad/ppermute | solution.py:39
  103.6 3.4 %collective-permute-start.18 = (bf16[2,2,4,2,16,512]{5,4,3,2,1,0:T(8,128)(2,1)S(1)}, bf16[2,2,4,2,16,512]{5,4,3,2,1,0:T(8,128)(2,1)S(1)}, u32[]{:S(2)}, u32[]{:S(2)}) collective-permute-start(bf16[2,2,4,2,16,512]{5,4,3,2,1,0:T(8,128)(2,1)S(1)} %pad_maximum_fusion.4), channel_id=1, source_target_pairs={{0,1},{1,0},{2,3},{3,2},{4,5},{5,4},{6,7},{7,6},{8,9},{9,8},{10,11... | collective-permute-start | bytes 1572872 | tf_op jit(solution)/shard_map/gather_rows/ppermute | solution.py:23
  110.0 17.5 %collective-permute-done.18.refs_10_ = bf16[2,2,4,2,16,512]{5,4,3,2,1,0:T(8,128)(2,1)S(1)} collective-permute-done((bf16[2,2,4,2,16,512]{5,4,3,2,1,0:T(8,128)(2,1)S(1)}, bf16[2,2,4,2,16,512]{5,4,3,2,1,0:T(8,128)(2,1)S(1)}, u32[]{:S(2)}, u32[]{:S(2)}) %collective-permute-start.18) | collective-permute-done | bytes 524320 | tf_op jit(solution)/shard_map/gather_rows/ppermute | solution.py:23
  127.5 4.1 %weight_terms.1 = (bf16[2,64,512]{2,1,0:T(8,128)(2,1)S(1)}, bf16[2,64,512]{2,1,0:T(8,128)(2,1)S(1)}) custom-call(s32[3]{0:T(128)S(1)} %pad_add_fusion.position, bf16[4,2,4,2,16,512]{5,4,3,2,1,0:T(8,128)(2,1)S(1)} %pad_maximum_fusion.refs_0_, bf16[4,2,4,2,16,512]{5,4,3,2,1,0:T(8,128)(2,1)S(1)} %collective-permute-done.3.refs_1_, ...), custom_call_target="tpu_custom_call" | custom-call | flops 1073741824 | bytes 5242880 | tf_op jit(solution)/shard_map/weight_terms/pallas_call | solution.py:220
  134.7 3.7 %collective-permute-start.20 = (bf16[2,64,512]{2,1,0:T(8,128)(2,1)S(1)}, bf16[2,64,512]{2,1,0:T(8,128)(2,1)S(1)}, u32[]{:S(2)}, u32[]{:S(2)}) collective-permute-start(bf16[2,64,512]{2,1,0:T(8,128)(2,1)S(1)} %get-tuple-element.10.refs_0_), channel_id=1, source_target_pairs={{0,128},{128,256},{256,384},{384,0},{1,129},{129,257},{257,385},{3... | collective-permute-start | bytes 393224 | tf_op jit(solution)/shard_map/spread_weight/ppermute | solution.py:19
  138.4 5.5 %collective-permute-start.23 = (bf16[2,64,512]{2,1,0:T(8,128)(2,1)S(1)}, bf16[2,64,512]{2,1,0:T(8,128)(2,1)S(1)}, u32[]{:S(2)}, u32[]{:S(2)}) collective-permute-start(bf16[2,64,512]{2,1,0:T(8,128)(2,1)S(1)} %collective-permute-done.19.refs_1_), channel_id=1, source_target_pairs={{0,384},{128,0},{256,128},{384,256},{1,385},{129,1},{257,129},{385... | collective-permute-start | bytes 393224 | tf_op jit(solution)/shard_map/spread_weight/ppermute | solution.py:19
  143.9 3.9 %collective-permute-start.25 = (bf16[2,64,512]{2,1,0:T(8,128)(2,1)S(1)}, bf16[2,64,512]{2,1,0:T(8,128)(2,1)S(1)}, u32[]{:S(2)}, u32[]{:S(2)}) collective-permute-start(bf16[2,64,512]{2,1,0:T(8,128)(2,1)S(1)} %get-tuple-element.10.refs_0_), channel_id=1, source_target_pairs={{0,384},{128,0},{256,128},{384,256},{1,385},{129,1},{257,129},{385... | collective-permute-start | bytes 393224 | tf_op jit(solution)/shard_map/spread_weight/ppermute | solution.py:19
  147.8 5.3 %collective-permute-start.21 = (bf16[2,64,512]{2,1,0:T(8,128)(2,1)S(1)}, bf16[2,64,512]{2,1,0:T(8,128)(2,1)S(1)}, u32[]{:S(2)}, u32[]{:S(2)}) collective-permute-start(bf16[2,64,512]{2,1,0:T(8,128)(2,1)S(1)} %collective-permute-done.19.refs_1_), channel_id=1, source_target_pairs={{0,128},{128,256},{256,384},{384,0},{1,129},{129,257},{257,385},{3... | collective-permute-start | bytes 393224 | tf_op jit(solution)/shard_map/spread_weight/ppermute | solution.py:19
  153.1 3.7 %collective-permute-start.22 = (bf16[2,64,512]{2,1,0:T(8,128)(2,1)S(1)}, bf16[2,64,512]{2,1,0:T(8,128)(2,1)S(1)}, u32[]{:S(2)}, u32[]{:S(2)}) collective-permute-start(bf16[2,64,512]{2,1,0:T(8,128)(2,1)S(1)} %collective-permute-done.20.refs_2_), channel_id=1, source_target_pairs={{0,128},{128,256},{256,384},{384,0},{1,129},{129,257},{257,385},{3... | collective-permute-start | bytes 393224 | tf_op jit(solution)/shard_map/spread_weight/ppermute | solution.py:19
  156.8 6.4 %collective-permute-done.23.refs_7_ = bf16[2,64,512]{2,1,0:T(8,128)(2,1)S(1)} collective-permute-done((bf16[2,64,512]{2,1,0:T(8,128)(2,1)S(1)}, bf16[2,64,512]{2,1,0:T(8,128)(2,1)S(1)}, u32[]{:S(2)}, u32[]{:S(2)}) %collective-permute-start.23) | collective-permute-done | bytes 131104 | tf_op jit(solution)/shard_map/spread_weight/ppermute | solution.py:19
  163.3 6.2 %collective-permute-start.24 = (bf16[2,64,512]{2,1,0:T(8,128)(2,1)S(1)}, bf16[2,64,512]{2,1,0:T(8,128)(2,1)S(1)}, u32[]{:S(2)}, u32[]{:S(2)}) collective-permute-start(bf16[2,64,512]{2,1,0:T(8,128)(2,1)S(1)} %collective-permute-done.23.refs_7_), channel_id=1, source_target_pairs={{0,384},{128,0},{256,128},{384,256},{1,385},{129,1},{257,129},{385... | collective-permute-start | bytes 393224 | tf_op jit(solution)/shard_map/spread_weight/ppermute | solution.py:19
  172.6 8.0 %collective-permute-done.24.refs_5_ = bf16[2,64,512]{2,1,0:T(8,128)(2,1)S(1)} collective-permute-done((bf16[2,64,512]{2,1,0:T(8,128)(2,1)S(1)}, bf16[2,64,512]{2,1,0:T(8,128)(2,1)S(1)}, u32[]{:S(2)}, u32[]{:S(2)}) %collective-permute-start.24) | collective-permute-done | bytes 131104 | tf_op jit(solution)/shard_map/spread_weight/ppermute | solution.py:19
  (62 shorter events, 33.0 us)
Async XLA Ops:
  1.9 10.7 %collective-permute-start = (bf16[4,2,96,512]{3,2,1,0:T(8,128)(2,1)S(1)}, bf16[4,2,96,512]{3,2,1,0:T(8,128)(2,1)S(1)}, u32[]{:S(2)}, u32[]{:S(2)}) collective-permute-start(bf16[4,2,96,512]{3,2,1,0:T(8,128)(2,1)S(1)} %pad_maximum_fusion.1), channel_id=1, source_target_pairs={{0,4},{4,0},{8,12},{12,8},{16,20},{20,16},{24,28},{28,24},{32,36},... | collective-permute-start | bytes 2359304 | tf_op jit(solution)/shard_map/swap_modes/ppermute | solution.py:23
  20.1 16.8 %collective-permute-start.2 = (bf16[2,2,4,2,16,512]{5,4,3,2,1,0:T(8,128)(2,1)S(1)}, bf16[2,2,4,2,16,512]{5,4,3,2,1,0:T(8,128)(2,1)S(1)}, u32[]{:S(2)}, u32[]{:S(2)}) collective-permute-start(bf16[2,2,4,2,16,512]{5,4,3,2,1,0:T(8,128)(2,1)S(1)} %pad_maximum_fusion.3), channel_id=1, source_target_pairs={{0,24},{4,100},{8,16},{12,108},{16,8},{20,116},{24,0},{28,124},{32... | collective-permute-start | bytes 1572872 | tf_op jit(solution)/shard_map/gather_grad/ppermute | solution.py:39
  22.2 25.5 %collective-permute-start.8 = (bf16[2,2,2,16,512]{4,3,2,1,0:T(8,128)(2,1)S(1)}, bf16[2,2,2,16,512]{4,3,2,1,0:T(8,128)(2,1)S(1)}, u32[]{:S(2)}, u32[]{:S(2)}) collective-permute-start(bf16[2,2,2,16,512]{4,3,2,1,0:T(8,128)(2,1)S(1)} %pad_maximum_fusion.11), channel_id=1, source_target_pairs={{0,384},{128,0},{256,128},{384,256},{1,385},{129,1},{257,129},{385... | collective-permute-start | bytes 393224 | tf_op jit(solution)/shard_map/exchange_modes/ppermute | solution.py:19
  32.0 23.1 %collective-permute-start.7 = (bf16[2,2,2,16,512]{4,3,2,1,0:T(8,128)(2,1)S(1)}, bf16[2,2,2,16,512]{4,3,2,1,0:T(8,128)(2,1)S(1)}, u32[]{:S(2)}, u32[]{:S(2)}) collective-permute-start(bf16[2,2,2,16,512]{4,3,2,1,0:T(8,128)(2,1)S(1)} %pad_maximum_fusion.10), channel_id=1, source_target_pairs={{0,256},{128,384},{256,0},{384,128},{1,257},{129,385},{257,1},{385... | collective-permute-start | bytes 393224 | tf_op jit(solution)/shard_map/exchange_modes/ppermute | solution.py:19
  37.1 36.1 %collective-permute-start.3 = (bf16[4,2,4,2,16,512]{5,4,3,2,1,0:T(8,128)(2,1)S(1)}, bf16[4,2,4,2,16,512]{5,4,3,2,1,0:T(8,128)(2,1)S(1)}, u32[]{:S(2)}, u32[]{:S(2)}) collective-permute-start(bf16[4,2,4,2,16,512]{5,4,3,2,1,0:T(8,128)(2,1)S(1)} %pad_maximum_fusion.refs_0_), channel_id=1, source_target_pairs={{0,32},{4,12},{8,40},{12,20},{16,48},{20,28},{24,56},{28,4},{32,64... | collective-permute-start | bytes 3145736 | tf_op jit(solution)/shard_map/gather_grad/ppermute | solution.py:39
  40.2 32.9 %collective-permute-start.4 = (bf16[4,2,4,2,16,512]{5,4,3,2,1,0:T(8,128)(2,1)S(1)}, bf16[4,2,4,2,16,512]{5,4,3,2,1,0:T(8,128)(2,1)S(1)}, u32[]{:S(2)}, u32[]{:S(2)}) collective-permute-start(bf16[4,2,4,2,16,512]{5,4,3,2,1,0:T(8,128)(2,1)S(1)} %pad_maximum_fusion.refs_0_), channel_id=1, source_target_pairs={{0,64},{4,20},{8,72},{12,28},{16,80},{20,4},{24,88},{28,12},{32,96... | collective-permute-start | bytes 3145736 | tf_op jit(solution)/shard_map/gather_grad/ppermute | solution.py:39
  44.6 28.6 %collective-permute-start.5 = (bf16[4,2,4,2,16,512]{5,4,3,2,1,0:T(8,128)(2,1)S(1)}, bf16[4,2,4,2,16,512]{5,4,3,2,1,0:T(8,128)(2,1)S(1)}, u32[]{:S(2)}, u32[]{:S(2)}) collective-permute-start(bf16[4,2,4,2,16,512]{5,4,3,2,1,0:T(8,128)(2,1)S(1)} %pad_maximum_fusion.refs_0_), channel_id=1, source_target_pairs={{0,96},{4,28},{8,104},{12,4},{16,112},{20,12},{24,120},{28,20},{32... | collective-permute-start | bytes 3145736 | tf_op jit(solution)/shard_map/gather_grad/ppermute | solution.py:39
  47.7 11.4 %collective-permute-start.6 = (bf16[2,2,2,16,512]{4,3,2,1,0:T(8,128)(2,1)S(1)}, bf16[2,2,2,16,512]{4,3,2,1,0:T(8,128)(2,1)S(1)}, u32[]{:S(2)}, u32[]{:S(2)}) collective-permute-start(bf16[2,2,2,16,512]{4,3,2,1,0:T(8,128)(2,1)S(1)} %pad_maximum_fusion.9), channel_id=1, source_target_pairs={{0,128},{128,256},{256,384},{384,0},{1,129},{129,257},{257,385},{3... | collective-permute-start | bytes 393224 | tf_op jit(solution)/shard_map/exchange_modes/ppermute | solution.py:19
  59.1 22.1 %collective-permute-start.9 = (bf16[2,4,2,16,512]{4,3,2,1,0:T(8,128)(2,1)S(1)}, bf16[2,4,2,16,512]{4,3,2,1,0:T(8,128)(2,1)S(1)}, u32[]{:S(2)}, u32[]{:S(2)}) collective-permute-start(bf16[2,4,2,16,512]{4,3,2,1,0:T(8,128)(2,1)S(1)} %get-tuple-element.15.refs_8_), channel_id=1, source_target_pairs={{0,2},{1,3},{2,0},{3,1},{4,6},{5,7},{6,4},{7,5},{8,10},{9,11},{10,... | collective-permute-start | bytes 786440 | tf_op jit(solution)/shard_map/gather_rows/ppermute | solution.py:23
  71.1 12.0 %collective-permute-start.13 = (bf16[3,2,2,16,512]{4,3,2,1,0:T(8,128)(2,1)S(1)}, bf16[3,2,2,16,512]{4,3,2,1,0:T(8,128)(2,1)S(1)}, u32[]{:S(2)}, u32[]{:S(2)}) collective-permute-start(bf16[3,2,2,16,512]{4,3,2,1,0:T(8,128)(2,1)S(1)} %get-tuple-element.32), channel_id=1, source_target_pairs={{0,8},{4,36},{8,0},{12,44},{16,24},{20,52},{24,16},{28,60},{32,40}... | collective-permute-start | bytes 589832 | tf_op jit(solution)/shard_map/gather_late_grad/ppermute | solution.py:39
  81.2 26.2 %collective-permute-start.10 = (f32[2,4,2,2,16,512]{5,4,3,2,1,0:T(8,128)S(1)}, f32[2,4,2,2,16,512]{5,4,3,2,1,0:T(8,128)S(1)}, u32[]{:S(2)}, u32[]{:S(2)}) collective-permute-start(f32[2,4,2,2,16,512]{5,4,3,2,1,0:T(8,128)S(1)} %get-tuple-element.9), channel_id=1, source_target_pairs={{0,1},{1,0},{2,3},{3,2},{4,5},{5,4},{6,7},{7,6},{8,9},{9,8},{10,11... | collective-permute-start | bytes 3145736 | tf_op jit(solution)/shard_map/sum_input/ppermute | solution.py:23
  83.1 10.0 %collective-permute-start.14 = (bf16[2,3,2,2,16,512]{5,4,3,2,1,0:T(8,128)(2,1)S(1)}, bf16[2,3,2,2,16,512]{5,4,3,2,1,0:T(8,128)(2,1)S(1)}, u32[]{:S(2)}, u32[]{:S(2)}) collective-permute-start(bf16[2,3,2,2,16,512]{5,4,3,2,1,0:T(8,128)(2,1)S(1)} %pad_maximum_fusion.5), channel_id=1, source_target_pairs={{0,24},{4,100},{8,16},{12,108},{16,8},{20,116},{24,0},{28,124},{32... | collective-permute-start | bytes 1179656 | tf_op jit(solution)/shard_map/gather_late_grad/ppermute | solution.py:39
  93.2 34.2 %collective-permute-start.15 = (bf16[4,3,2,2,16,512]{5,4,3,2,1,0:T(8,128)(2,1)S(1)}, bf16[4,3,2,2,16,512]{5,4,3,2,1,0:T(8,128)(2,1)S(1)}, u32[]{:S(2)}, u32[]{:S(2)}) collective-permute-start(bf16[4,3,2,2,16,512]{5,4,3,2,1,0:T(8,128)(2,1)S(1)} %pad_maximum_fusion.2.refs_4_), channel_id=1, source_target_pairs={{0,32},{4,12},{8,40},{12,20},{16,48},{20,28},{24,56},{28,4},{32,64... | collective-permute-start | bytes 2359304 | tf_op jit(solution)/shard_map/gather_late_grad/ppermute | solution.py:39
  95.2 32.3 %collective-permute-start.16 = (bf16[4,3,2,2,16,512]{5,4,3,2,1,0:T(8,128)(2,1)S(1)}, bf16[4,3,2,2,16,512]{5,4,3,2,1,0:T(8,128)(2,1)S(1)}, u32[]{:S(2)}, u32[]{:S(2)}) collective-permute-start(bf16[4,3,2,2,16,512]{5,4,3,2,1,0:T(8,128)(2,1)S(1)} %pad_maximum_fusion.2.refs_4_), channel_id=1, source_target_pairs={{0,64},{4,20},{8,72},{12,28},{16,80},{20,4},{24,88},{28,12},{32,96... | collective-permute-start | bytes 2359304 | tf_op jit(solution)/shard_map/gather_late_grad/ppermute | solution.py:39
  101.6 25.9 %collective-permute-start.17 = (bf16[4,3,2,2,16,512]{5,4,3,2,1,0:T(8,128)(2,1)S(1)}, bf16[4,3,2,2,16,512]{5,4,3,2,1,0:T(8,128)(2,1)S(1)}, u32[]{:S(2)}, u32[]{:S(2)}) collective-permute-start(bf16[4,3,2,2,16,512]{5,4,3,2,1,0:T(8,128)(2,1)S(1)} %pad_maximum_fusion.2.refs_4_), channel_id=1, source_target_pairs={{0,96},{4,28},{8,104},{12,4},{16,112},{20,12},{24,120},{28,20},{32... | collective-permute-start | bytes 2359304 | tf_op jit(solution)/shard_map/gather_late_grad/ppermute | solution.py:39
  103.6 23.9 %collective-permute-start.18 = (bf16[2,2,4,2,16,512]{5,4,3,2,1,0:T(8,128)(2,1)S(1)}, bf16[2,2,4,2,16,512]{5,4,3,2,1,0:T(8,128)(2,1)S(1)}, u32[]{:S(2)}, u32[]{:S(2)}) collective-permute-start(bf16[2,2,4,2,16,512]{5,4,3,2,1,0:T(8,128)(2,1)S(1)} %pad_maximum_fusion.4), channel_id=1, source_target_pairs={{0,1},{1,0},{2,3},{3,2},{4,5},{5,4},{6,7},{7,6},{8,9},{9,8},{10,11... | collective-permute-start | bytes 1572872 | tf_op jit(solution)/shard_map/gather_rows/ppermute | solution.py:23
  107.4 62.1 %collective-permute-start.11 = (f32[4,2,2,16,512]{4,3,2,1,0:T(8,128)S(1)}, f32[4,2,2,16,512]{4,3,2,1,0:T(8,128)S(1)}, u32[]{:S(2)}, u32[]{:S(2)}) collective-permute-start(f32[4,2,2,16,512]{4,3,2,1,0:T(8,128)S(1)} %fusion), channel_id=1, source_target_pairs={{0,2},{1,3},{2,0},{3,1},{4,6},{5,7},{6,4},{7,5},{8,10},{9,11},{10,... | collective-permute-start | bytes 1572872 | tf_op jit(solution)/shard_map/sum_input/ppermute | solution.py:23
  134.7 18.4 %collective-permute-start.20 = (bf16[2,64,512]{2,1,0:T(8,128)(2,1)S(1)}, bf16[2,64,512]{2,1,0:T(8,128)(2,1)S(1)}, u32[]{:S(2)}, u32[]{:S(2)}) collective-permute-start(bf16[2,64,512]{2,1,0:T(8,128)(2,1)S(1)} %get-tuple-element.10.refs_0_), channel_id=1, source_target_pairs={{0,128},{128,256},{256,384},{384,0},{1,129},{129,257},{257,385},{3... | collective-permute-start | bytes 393224 | tf_op jit(solution)/shard_map/spread_weight/ppermute | solution.py:19
  138.4 24.9 %collective-permute-start.23 = (bf16[2,64,512]{2,1,0:T(8,128)(2,1)S(1)}, bf16[2,64,512]{2,1,0:T(8,128)(2,1)S(1)}, u32[]{:S(2)}, u32[]{:S(2)}) collective-permute-start(bf16[2,64,512]{2,1,0:T(8,128)(2,1)S(1)} %collective-permute-done.19.refs_1_), channel_id=1, source_target_pairs={{0,384},{128,0},{256,128},{384,256},{1,385},{129,1},{257,129},{385... | collective-permute-start | bytes 393224 | tf_op jit(solution)/shard_map/spread_weight/ppermute | solution.py:19
  143.9 28.7 %collective-permute-start.25 = (bf16[2,64,512]{2,1,0:T(8,128)(2,1)S(1)}, bf16[2,64,512]{2,1,0:T(8,128)(2,1)S(1)}, u32[]{:S(2)}, u32[]{:S(2)}) collective-permute-start(bf16[2,64,512]{2,1,0:T(8,128)(2,1)S(1)} %get-tuple-element.10.refs_0_), channel_id=1, source_target_pairs={{0,384},{128,0},{256,128},{384,256},{1,385},{129,1},{257,129},{385... | collective-permute-start | bytes 393224 | tf_op jit(solution)/shard_map/spread_weight/ppermute | solution.py:19
  147.8 24.8 %collective-permute-start.21 = (bf16[2,64,512]{2,1,0:T(8,128)(2,1)S(1)}, bf16[2,64,512]{2,1,0:T(8,128)(2,1)S(1)}, u32[]{:S(2)}, u32[]{:S(2)}) collective-permute-start(bf16[2,64,512]{2,1,0:T(8,128)(2,1)S(1)} %collective-permute-done.19.refs_1_), channel_id=1, source_target_pairs={{0,128},{128,256},{256,384},{384,0},{1,129},{129,257},{257,385},{3... | collective-permute-start | bytes 393224 | tf_op jit(solution)/shard_map/spread_weight/ppermute | solution.py:19
  153.1 19.5 %collective-permute-start.22 = (bf16[2,64,512]{2,1,0:T(8,128)(2,1)S(1)}, bf16[2,64,512]{2,1,0:T(8,128)(2,1)S(1)}, u32[]{:S(2)}, u32[]{:S(2)}) collective-permute-start(bf16[2,64,512]{2,1,0:T(8,128)(2,1)S(1)} %collective-permute-done.20.refs_2_), channel_id=1, source_target_pairs={{0,128},{128,256},{256,384},{384,0},{1,129},{129,257},{257,385},{3... | collective-permute-start | bytes 393224 | tf_op jit(solution)/shard_map/spread_weight/ppermute | solution.py:19
  163.3 17.4 %collective-permute-start.24 = (bf16[2,64,512]{2,1,0:T(8,128)(2,1)S(1)}, bf16[2,64,512]{2,1,0:T(8,128)(2,1)S(1)}, u32[]{:S(2)}, u32[]{:S(2)}) collective-permute-start(bf16[2,64,512]{2,1,0:T(8,128)(2,1)S(1)} %collective-permute-done.23.refs_7_), channel_id=1, source_target_pairs={{0,384},{128,0},{256,128},{384,256},{1,385},{129,1},{257,129},{385... | collective-permute-start | bytes 393224 | tf_op jit(solution)/shard_map/spread_weight/ppermute | solution.py:19
  169.7 13.8 %collective-permute-start.12 = (bf16[4,2,16,512]{3,2,1,0:T(8,128)(2,1)S(1)}, bf16[4,2,16,512]{3,2,1,0:T(8,128)(2,1)S(1)}, u32[]{:S(2)}, u32[]{:S(2)}) collective-permute-start(bf16[4,2,16,512]{3,2,1,0:T(8,128)(2,1)S(1)} %get-tuple-element.17), channel_id=1, source_target_pairs={{0,4},{4,0},{8,12},{12,8},{16,20},{20,16},{24,28},{28,24},{32,36},... | collective-permute-start | bytes 393224 | tf_op jit(solution)/shard_map/sum_input/ppermute | solution.py:23
  (5 other events, 42.0 us)

commit v5 on v4

--- a/solution.py
+++ b/solution.py
@@ -1,3 +1,5 @@
+import functools
+
 import jax
 import jax.numpy as jnp
 from jax import lax
@@ -7,6 +9,7 @@
 
 HEARD = (0, 3, 2, 1)
 SHIFTS = (1, 2, 3)
+ARRIVAL = (0, 3, 1, 2)
 PAIRED = (0, 1, 3, 2)
 TREE = (0, 2, 1, 3)
 MIB = 1 << 20
@@ -108,32 +111,34 @@
 
 
 def weight_terms(position, *refs):
-    pieces, late, (x0, x1, x2, here, there, grads, rows, sem) = refs[:4], refs[4:8], refs[8:]
+    pieces, late, (x0, x1, x2, here, there, grads, rows, sems) = refs[:4], refs[4:8], refs[8:]
     mode = position[0]
     fetch_plane(
         position,
         pieces,
         lambda piece, source: piece.at[source, mode],
         lambda place: grads.at[0, :, place, :],
-        sem,
+        sems.at[0],
     )
     for index, piece in enumerate((x0, x1, x2.at[0], x2.at[1])):
         for source in range(2):
             row = pl.multiple_of(tree_row(position, index) + 64 * source, 16)
-            pltpu.make_async_copy(piece.at[source], rows.at[:, :, pl.ds(row, 16), :], sem).start()
+            pltpu.make_async_copy(piece.at[source], rows.at[:, :, pl.ds(row, 16), :], sems.at[0]).start()
     fetch_plane(
         position,
         late,
         lambda piece, source: piece.at[:, source],
         lambda place: grads.at[pl.ds(1, 3), :, place, :],
-        sem,
-    )
-    pltpu.make_async_copy(grads, grads, sem).wait()
-    pltpu.make_async_copy(rows, rows, sem).wait()
+        sems.at[1],
+    )
+    pltpu.make_async_copy(grads.at[0], grads.at[0], sems.at[0]).wait()
+    pltpu.make_async_copy(rows, rows, sems.at[0]).wait()
 
     total = jnp.zeros((256, 512), jnp.float32)
     contract = (((1,), (1,)), ((), ()))
     for block in range(4):
+        if block == 1:
+            pltpu.make_async_copy(grads.at[pl.ds(1, 3)], grads.at[pl.ds(1, 3)], sems.at[1]).wait()
         real = rows[block, 0]
         imag = rows[block, 1]
         total += lax.dot_general(
@@ -148,13 +153,43 @@
             out[part] = total[start : start + 64].astype(jnp.bfloat16)
 
 
-def place_modes(position, *refs):
-    pieces, (out, sem) = refs[:8], refs[8:]
-    for step in range(4):
-        for slot in range(2):
-            mode = ((position[1] & 1) ^ slot) * 4 + ((position[0] + HEARD[step]) & 3)
-            pltpu.make_async_copy(pieces[2 * step + slot], out.at[mode], sem).start()
-    pltpu.make_async_copy(out, out, sem).wait()
+def place_modes(first, position, *refs):
+    pieces, (out, staged, read, written) = refs[:-4], refs[-4:]
+    reads = [
+        pltpu.make_async_copy(piece, staged.at[index], read.at[index]) for index, piece in enumerate(pieces)
+    ]
+    for copy in reads:
+        copy.start()
+    for index, copy in enumerate(reads):
+        slot, step = (first + index) % 2, (first + index) // 2
+        mode = ((position[1] & 1) ^ slot) * 4 + ((position[0] + ARRIVAL[step]) & 3)
+        copy.wait()
+        pltpu.make_async_copy(staged.at[index], out.at[mode], written).start()
+    pltpu.make_async_copy(staged, staged, written).wait()
+
+
+def place_last(position, piece, placed, out, staged, read, written):
+    del placed
+    place_modes(7, position, piece, out, staged, read, written)
+
+
+def place_call(body, name, pieces, position, placed=None):
+    held = [] if placed is None else [placed]
+    return pl.pallas_call(
+        body,
+        out_shape=jax.ShapeDtypeStruct((8, 2, 64, 512), jnp.bfloat16),
+        in_specs=[SMEM] + [ANY] * (len(pieces) + len(held)),
+        out_specs=ANY,
+        input_output_aliases={1 + len(pieces): 0} if held else {},
+        scratch_shapes=[
+            pltpu.VMEM((len(pieces), 2, 64, 512), jnp.bfloat16),
+            pltpu.SemaphoreType.DMA((len(pieces),)),
+            pltpu.SemaphoreType.DMA,
+        ],
+        compiler_params=pltpu.CompilerParams(vmem_limit_bytes=8 * MIB),
+        cost_estimate=pl.CostEstimate(flops=0, bytes_accessed=2 * MIB, transcendentals=0),
+        name=name,
+    )(position, *pieces, *held)
 
 
 def on_device(weight, spectrum, out_grad):
@@ -225,7 +260,7 @@
         scratch_shapes=[
             pltpu.VMEM((4, 2, 512, 512), jnp.bfloat16),
             pltpu.VMEM((4, 2, 128, 512), jnp.bfloat16),
-            pltpu.SemaphoreType.DMA,
+            pltpu.SemaphoreType.DMA((2,)),
         ],
         compiler_params=pltpu.CompilerParams(vmem_limit_bytes=24 * MIB),
         cost_estimate=pl.CostEstimate(flops=1 << 30, bytes_accessed=5 * MIB, transcendentals=0),
@@ -237,16 +272,13 @@
         other = swap_cores(there)
         back_1, ahead_1 = ring(other, "dp", 1), ring(other, "dp", 3)
         far_0, far_1 = ring(back_0, "dp", 1), ring(ahead_1, "dp", 3)
-    weight_grad = pl.pallas_call(
-        place_modes,
-        out_shape=jax.ShapeDtypeStruct(weight.shape, jnp.bfloat16),
-        in_specs=[SMEM] + [ANY] * 8,
-        out_specs=VMEM,
-        scratch_shapes=[pltpu.SemaphoreType.DMA],
-        compiler_params=pltpu.CompilerParams(vmem_limit_bytes=8 * MIB),
-        cost_estimate=pl.CostEstimate(flops=0, bytes_accessed=2 * MIB, transcendentals=0),
-        name="place_modes",
-    )(position, here, other, back_0, back_1, far_0, far_1, ahead_0, ahead_1)
+    placed = place_call(
+        functools.partial(place_modes, 0),
+        "place_modes",
+        [here, other, back_0, back_1, ahead_0, ahead_1, far_0],
+        position,
+    )
+    weight_grad = place_call(place_last, "place_last", [far_1], position, placed)
     return (spectrum_grad, weight_grad)
 
 

time: 185 us -> 184 us (level)
  waiting for transfers between devices: 56.9 us -> 54 us
    ppermute x9, waiting for transfers between devices: 18.4 us -> 15.5 us  [ring(): return lax.ppermute(value, axis, [(i, (i + shift) % 4) for i in range(4)])]
    pallas_call x1 -> x2, Pallas kernels: 2.91 us -> 4.1 us  [place_call(): pl.pallas_call(body, out_shape=jax.ShapeDtypeStruct((8, 2, 64, 512), jnp....]
  transfers between devices with their start and end apart: 26 -> 26, of which waited for: 9 -> 9; matrix products, arithmetic and copies ran while one was open for 0% -> 0% of each run, Pallas kernels for 5% -> 6%
where the time goes in v5:
time: 184 us; the launch traced here: 183 us
  starting transfers between devices  113 us (61%)
  waiting for transfers between devices  54 us (29%)
  Pallas kernels  11.2 us (6%)
    ppermute x9, starting transfers between devices, ring(): return lax.ppermute(value, axis, [(i, (i + shift) % 4) for i in range(4)])  50.4 us
    ppermute x7, starting transfers between devices, flip(): return lax.ppermute(value, axis, [(i, i ^ bits) for i in range(size)])  34.5 us
    ppermute x10, starting transfers between devices, hop(): return lax.ppermute(value, 'cin', pairs)  28.5 us
    ppermute x7, waiting for transfers between devices, flip(): return lax.ppermute(value, axis, [(i, i ^ bits) for i in range(size)])  24.9 us
    ppermute x9, waiting for transfers between devices, ring(): return lax.ppermute(value, axis, [(i, (i + shift) % 4) for i in range(4)])  15.5 us
    ppermute x10, waiting for transfers between devices, hop(): return lax.ppermute(value, 'cin', pairs)  13.6 us
    pallas_call x1, Pallas kernels, on_device(): pl.pallas_call(weight_terms, out_shape=[jax.ShapeDtypeStruct((2, 64, 512)...  4.24 us
    pallas_call x2, Pallas kernels, place_call(): pl.pallas_call(body, out_shape=jax.ShapeDtypeStruct((8, 2, 64, 512), jnp....  4.1 us
  transfers between devices with their start and end apart: 26, of which 9 were waited for; matrix products, arithmetic and copies ran while one was open for 0% of the time, Pallas kernels for 6%

profile of v5, /device:TPU:1, one launch (start us, length us, event | category | flops | bytes accessed | tf_op | source)
XLA Modules:
  0.0 182.7 jit_solution(4238413289489739332)
XLA Ops:
  1.9 8.8 %collective-permute-start = (bf16[4,2,96,512]{3,2,1,0:T(8,128)(2,1)S(1)}, bf16[4,2,96,512]{3,2,1,0:T(8,128)(2,1)S(1)}, u32[]{:S(2)}, u32[]{:S(2)}) collective-permute-start(bf16[4,2,96,512]{3,2,1,0:T(8,128)(2,1)S(1)} %pad_maximum_fusion.1), channel_id=1, source_target_pairs={{0,4},{4,0},{8,12},{12,8},{16,20},{20,16},{24,28},{28,24},{32,36},... | collective-permute-start | bytes 2359304 | tf_op jit(solution)/shard_map/swap_modes/ppermute | solution.py:26
  14.6 5.5 %collective-permute-done.1 = bf16[2,4,2,16,512]{4,3,2,1,0:T(8,128)(2,1)S(1)} collective-permute-done((bf16[2,4,2,16,512]{4,3,2,1,0:T(8,128)(2,1)S(1)}, bf16[2,4,2,16,512]{4,3,2,1,0:T(8,128)(2,1)S(1)}, u32[]{:S(2)}, u32[]{:S(2)}) %collective-permute-start.1) | collective-permute-done | bytes 262176 | tf_op jit(solution)/shard_map/gather_grad/ppermute | solution.py:42
  22.2 9.8 %collective-permute-start.8 = (bf16[2,2,2,16,512]{4,3,2,1,0:T(8,128)(2,1)S(1)}, bf16[2,2,2,16,512]{4,3,2,1,0:T(8,128)(2,1)S(1)}, u32[]{:S(2)}, u32[]{:S(2)}) collective-permute-start(bf16[2,2,2,16,512]{4,3,2,1,0:T(8,128)(2,1)S(1)} %pad_maximum_fusion.11), channel_id=1, source_target_pairs={{0,384},{128,0},{256,128},{384,256},{1,385},{129,1},{257,129},{385... | collective-permute-start | bytes 393224 | tf_op jit(solution)/shard_map/exchange_modes/ppermute | solution.py:22
  32.0 4.9 %collective-permute-start.7 = (bf16[2,2,2,16,512]{4,3,2,1,0:T(8,128)(2,1)S(1)}, bf16[2,2,2,16,512]{4,3,2,1,0:T(8,128)(2,1)S(1)}, u32[]{:S(2)}, u32[]{:S(2)}) collective-permute-start(bf16[2,2,2,16,512]{4,3,2,1,0:T(8,128)(2,1)S(1)} %pad_maximum_fusion.10), channel_id=1, source_target_pairs={{0,256},{128,384},{256,0},{384,128},{1,257},{129,385},{257,1},{385... | collective-permute-start | bytes 393224 | tf_op jit(solution)/shard_map/exchange_modes/ppermute | solution.py:22
  37.1 3.1 %collective-permute-start.3 = (bf16[4,2,4,2,16,512]{5,4,3,2,1,0:T(8,128)(2,1)S(1)}, bf16[4,2,4,2,16,512]{5,4,3,2,1,0:T(8,128)(2,1)S(1)}, u32[]{:S(2)}, u32[]{:S(2)}) collective-permute-start(bf16[4,2,4,2,16,512]{5,4,3,2,1,0:T(8,128)(2,1)S(1)} %pad_maximum_fusion.refs_0_), channel_id=1, source_target_pairs={{0,32},{4,12},{8,40},{12,20},{16,48},{20,28},{24,56},{28,4},{32,64... | collective-permute-start | bytes 3145736 | tf_op jit(solution)/shard_map/gather_grad/ppermute | solution.py:42
  40.2 4.4 %collective-permute-start.4 = (bf16[4,2,4,2,16,512]{5,4,3,2,1,0:T(8,128)(2,1)S(1)}, bf16[4,2,4,2,16,512]{5,4,3,2,1,0:T(8,128)(2,1)S(1)}, u32[]{:S(2)}, u32[]{:S(2)}) collective-permute-start(bf16[4,2,4,2,16,512]{5,4,3,2,1,0:T(8,128)(2,1)S(1)} %pad_maximum_fusion.refs_0_), channel_id=1, source_target_pairs={{0,64},{4,20},{8,72},{12,28},{16,80},{20,4},{24,88},{28,12},{32,96... | collective-permute-start | bytes 3145736 | tf_op jit(solution)/shard_map/gather_grad/ppermute | solution.py:42
  44.6 3.1 %collective-permute-start.5 = (bf16[4,2,4,2,16,512]{5,4,3,2,1,0:T(8,128)(2,1)S(1)}, bf16[4,2,4,2,16,512]{5,4,3,2,1,0:T(8,128)(2,1)S(1)}, u32[]{:S(2)}, u32[]{:S(2)}) collective-permute-start(bf16[4,2,4,2,16,512]{5,4,3,2,1,0:T(8,128)(2,1)S(1)} %pad_maximum_fusion.refs_0_), channel_id=1, source_target_pairs={{0,96},{4,28},{8,104},{12,4},{16,112},{20,12},{24,120},{28,20},{32... | collective-permute-start | bytes 3145736 | tf_op jit(solution)/shard_map/gather_grad/ppermute | solution.py:42
  47.7 7.4 %collective-permute-start.6 = (bf16[2,2,2,16,512]{4,3,2,1,0:T(8,128)(2,1)S(1)}, bf16[2,2,2,16,512]{4,3,2,1,0:T(8,128)(2,1)S(1)}, u32[]{:S(2)}, u32[]{:S(2)}) collective-permute-start(bf16[2,2,2,16,512]{4,3,2,1,0:T(8,128)(2,1)S(1)} %pad_maximum_fusion.9), channel_id=1, source_target_pairs={{0,128},{128,256},{256,384},{384,0},{1,129},{129,257},{257,385},{3... | collective-permute-start | bytes 393224 | tf_op jit(solution)/shard_map/exchange_modes/ppermute | solution.py:22
  55.1 3.9 %collective-permute-done.6 = bf16[2,2,2,16,512]{4,3,2,1,0:T(8,128)(2,1)S(1)} collective-permute-done((bf16[2,2,2,16,512]{4,3,2,1,0:T(8,128)(2,1)S(1)}, bf16[2,2,2,16,512]{4,3,2,1,0:T(8,128)(2,1)S(1)}, u32[]{:S(2)}, u32[]{:S(2)}) %collective-permute-start.6) | collective-permute-done | bytes 131104 | tf_op jit(solution)/shard_map/exchange_modes/ppermute | solution.py:22
  59.1 12.0 %collective-permute-start.9 = (bf16[2,4,2,16,512]{4,3,2,1,0:T(8,128)(2,1)S(1)}, bf16[2,4,2,16,512]{4,3,2,1,0:T(8,128)(2,1)S(1)}, u32[]{:S(2)}, u32[]{:S(2)}) collective-permute-start(bf16[2,4,2,16,512]{4,3,2,1,0:T(8,128)(2,1)S(1)} %get-tuple-element.15.refs_8_), channel_id=1, source_target_pairs={{0,2},{1,3},{2,0},{3,1},{4,6},{5,7},{6,4},{7,5},{8,10},{9,11},{10,... | collective-permute-start | bytes 786440 | tf_op jit(solution)/shard_map/gather_rows/ppermute | solution.py:26
  76.0 5.1 %collective-permute-done.9.refs_9_ = bf16[2,4,2,16,512]{4,3,2,1,0:T(8,128)(2,1)S(1)} collective-permute-done((bf16[2,4,2,16,512]{4,3,2,1,0:T(8,128)(2,1)S(1)}, bf16[2,4,2,16,512]{4,3,2,1,0:T(8,128)(2,1)S(1)}, u32[]{:S(2)}, u32[]{:S(2)}) %collective-permute-start.9) | collective-permute-done | bytes 262176 | tf_op jit(solution)/shard_map/gather_rows/ppermute | solution.py:26
  85.1 8.1 %collective-permute-done.14 = bf16[2,3,2,2,16,512]{5,4,3,2,1,0:T(8,128)(2,1)S(1)} collective-permute-done((bf16[2,3,2,2,16,512]{5,4,3,2,1,0:T(8,128)(2,1)S(1)}, bf16[2,3,2,2,16,512]{5,4,3,2,1,0:T(8,128)(2,1)S(1)}, u32[]{:S(2)}, u32[]{:S(2)}) %collective-permute-start.14) | collective-permute-done | bytes 393248 | tf_op jit(solution)/shard_map/gather_late_grad/ppermute | solution.py:42
  95.2 6.4 %collective-permute-start.16 = (bf16[4,3,2,2,16,512]{5,4,3,2,1,0:T(8,128)(2,1)S(1)}, bf16[4,3,2,2,16,512]{5,4,3,2,1,0:T(8,128)(2,1)S(1)}, u32[]{:S(2)}, u32[]{:S(2)}) collective-permute-start(bf16[4,3,2,2,16,512]{5,4,3,2,1,0:T(8,128)(2,1)S(1)} %pad_maximum_fusion.2.refs_4_), channel_id=1, source_target_pairs={{0,64},{4,20},{8,72},{12,28},{16,80},{20,4},{24,88},{28,12},{32,96... | collective-permute-start | bytes 2359304 | tf_op jit(solution)/shard_map/gather_late_grad/ppermute | solution.py:42
  103.6 3.4 %collective-permute-start.18 = (bf16[2,2,4,2,16,512]{5,4,3,2,1,0:T(8,128)(2,1)S(1)}, bf16[2,2,4,2,16,512]{5,4,3,2,1,0:T(8,128)(2,1)S(1)}, u32[]{:S(2)}, u32[]{:S(2)}) collective-permute-start(bf16[2,2,4,2,16,512]{5,4,3,2,1,0:T(8,128)(2,1)S(1)} %pad_maximum_fusion.4), channel_id=1, source_target_pairs={{0,1},{1,0},{2,3},{3,2},{4,5},{5,4},{6,7},{7,6},{8,9},{9,8},{10,11... | collective-permute-start | bytes 1572872 | tf_op jit(solution)/shard_map/gather_rows/ppermute | solution.py:26
  110.0 17.5 %collective-permute-done.18.refs_10_ = bf16[2,2,4,2,16,512]{5,4,3,2,1,0:T(8,128)(2,1)S(1)} collective-permute-done((bf16[2,2,4,2,16,512]{5,4,3,2,1,0:T(8,128)(2,1)S(1)}, bf16[2,2,4,2,16,512]{5,4,3,2,1,0:T(8,128)(2,1)S(1)}, u32[]{:S(2)}, u32[]{:S(2)}) %collective-permute-start.18) | collective-permute-done | bytes 524320 | tf_op jit(solution)/shard_map/gather_rows/ppermute | solution.py:26
  127.5 4.2 %weight_terms.1 = (bf16[2,64,512]{2,1,0:T(8,128)(2,1)S(1)}, bf16[2,64,512]{2,1,0:T(8,128)(2,1)S(1)}) custom-call(s32[3]{0:T(128)S(1)} %pad_add_fusion.position, bf16[4,2,4,2,16,512]{5,4,3,2,1,0:T(8,128)(2,1)S(1)} %pad_maximum_fusion.refs_0_, bf16[4,2,4,2,16,512]{5,4,3,2,1,0:T(8,128)(2,1)S(1)} %collective-permute-done.3.refs_1_, ...), custom_call_target="tpu_custom_call" | custom-call | flops 1073741824 | bytes 5242880 | tf_op jit(solution)/shard_map/weight_terms/pallas_call | solution.py:255
  134.8 3.7 %collective-permute-start.22 = (bf16[2,64,512]{2,1,0:T(8,128)(2,1)S(1)}, bf16[2,64,512]{2,1,0:T(8,128)(2,1)S(1)}, u32[]{:S(2)}, u32[]{:S(2)}) collective-permute-start(bf16[2,64,512]{2,1,0:T(8,128)(2,1)S(1)} %get-tuple-element.11.refs_0_), channel_id=1, source_target_pairs={{0,128},{128,256},{256,384},{384,0},{1,129},{129,257},{257,385},{3... | collective-permute-start | bytes 393224 | tf_op jit(solution)/shard_map/spread_weight/ppermute | solution.py:22
  138.5 5.5 %collective-permute-start.20 = (bf16[2,64,512]{2,1,0:T(8,128)(2,1)S(1)}, bf16[2,64,512]{2,1,0:T(8,128)(2,1)S(1)}, u32[]{:S(2)}, u32[]{:S(2)}) collective-permute-start(bf16[2,64,512]{2,1,0:T(8,128)(2,1)S(1)} %collective-permute-done.19.refs_1_), channel_id=1, source_target_pairs={{0,384},{128,0},{256,128},{384,256},{1,385},{129,1},{257,129},{385... | collective-permute-start | bytes 393224 | tf_op jit(solution)/shard_map/spread_weight/ppermute | solution.py:22
  144.0 3.9 %collective-permute-start.24 = (bf16[2,64,512]{2,1,0:T(8,128)(2,1)S(1)}, bf16[2,64,512]{2,1,0:T(8,128)(2,1)S(1)}, u32[]{:S(2)}, u32[]{:S(2)}) collective-permute-start(bf16[2,64,512]{2,1,0:T(8,128)(2,1)S(1)} %get-tuple-element.11.refs_0_), channel_id=1, source_target_pairs={{0,384},{128,0},{256,128},{384,256},{1,385},{129,1},{257,129},{385... | collective-permute-start | bytes 393224 | tf_op jit(solution)/shard_map/spread_weight/ppermute | solution.py:22
  147.9 5.3 %collective-permute-start.23 = (bf16[2,64,512]{2,1,0:T(8,128)(2,1)S(1)}, bf16[2,64,512]{2,1,0:T(8,128)(2,1)S(1)}, u32[]{:S(2)}, u32[]{:S(2)}) collective-permute-start(bf16[2,64,512]{2,1,0:T(8,128)(2,1)S(1)} %collective-permute-done.19.refs_1_), channel_id=1, source_target_pairs={{0,128},{128,256},{256,384},{384,0},{1,129},{129,257},{257,385},{3... | collective-permute-start | bytes 393224 | tf_op jit(solution)/shard_map/spread_weight/ppermute | solution.py:22
  153.2 3.7 %collective-permute-start.25 = (bf16[2,64,512]{2,1,0:T(8,128)(2,1)S(1)}, bf16[2,64,512]{2,1,0:T(8,128)(2,1)S(1)}, u32[]{:S(2)}, u32[]{:S(2)}) collective-permute-start(bf16[2,64,512]{2,1,0:T(8,128)(2,1)S(1)} %collective-permute-done.22.refs_2_), channel_id=1, source_target_pairs={{0,128},{128,256},{256,384},{384,0},{1,129},{129,257},{257,385},{3... | collective-permute-start | bytes 393224 | tf_op jit(solution)/shard_map/spread_weight/ppermute | solution.py:22
  156.9 6.4 %collective-permute-done.20.refs_5_ = bf16[2,64,512]{2,1,0:T(8,128)(2,1)S(1)} collective-permute-done((bf16[2,64,512]{2,1,0:T(8,128)(2,1)S(1)}, bf16[2,64,512]{2,1,0:T(8,128)(2,1)S(1)}, u32[]{:S(2)}, u32[]{:S(2)}) %collective-permute-start.20) | collective-permute-done | bytes 131104 | tf_op jit(solution)/shard_map/spread_weight/ppermute | solution.py:22
  163.4 6.2 %collective-permute-start.21 = (bf16[2,64,512]{2,1,0:T(8,128)(2,1)S(1)}, bf16[2,64,512]{2,1,0:T(8,128)(2,1)S(1)}, u32[]{:S(2)}, u32[]{:S(2)}) collective-permute-start(bf16[2,64,512]{2,1,0:T(8,128)(2,1)S(1)} %collective-permute-done.20.refs_5_), channel_id=1, source_target_pairs={{0,384},{128,0},{256,128},{384,256},{1,385},{129,1},{257,129},{385... | collective-permute-start | bytes 393224 | tf_op jit(solution)/shard_map/spread_weight/ppermute | solution.py:22
  175.4 5.2 %collective-permute-done.21.piece = bf16[2,64,512]{2,1,0:T(8,128)(2,1)S(1)} collective-permute-done((bf16[2,64,512]{2,1,0:T(8,128)(2,1)S(1)}, bf16[2,64,512]{2,1,0:T(8,128)(2,1)S(1)}, u32[]{:S(2)}, u32[]{:S(2)}) %collective-permute-start.21) | collective-permute-done | bytes 131104 | tf_op jit(solution)/shard_map/spread_weight/ppermute | solution.py:22
  (63 shorter events, 34.1 us)
Async XLA Ops:
  1.9 10.7 %collective-permute-start = (bf16[4,2,96,512]{3,2,1,0:T(8,128)(2,1)S(1)}, bf16[4,2,96,512]{3,2,1,0:T(8,128)(2,1)S(1)}, u32[]{:S(2)}, u32[]{:S(2)}) collective-permute-start(bf16[4,2,96,512]{3,2,1,0:T(8,128)(2,1)S(1)} %pad_maximum_fusion.1), channel_id=1, source_target_pairs={{0,4},{4,0},{8,12},{12,8},{16,20},{20,16},{24,28},{28,24},{32,36},... | collective-permute-start | bytes 2359304 | tf_op jit(solution)/shard_map/swap_modes/ppermute | solution.py:26
  20.1 16.8 %collective-permute-start.2 = (bf16[2,2,4,2,16,512]{5,4,3,2,1,0:T(8,128)(2,1)S(1)}, bf16[2,2,4,2,16,512]{5,4,3,2,1,0:T(8,128)(2,1)S(1)}, u32[]{:S(2)}, u32[]{:S(2)}) collective-permute-start(bf16[2,2,4,2,16,512]{5,4,3,2,1,0:T(8,128)(2,1)S(1)} %pad_maximum_fusion.3), channel_id=1, source_target_pairs={{0,24},{4,100},{8,16},{12,108},{16,8},{20,116},{24,0},{28,124},{32... | collective-permute-start | bytes 1572872 | tf_op jit(solution)/shard_map/gather_grad/ppermute | solution.py:42
  22.2 25.5 %collective-permute-start.8 = (bf16[2,2,2,16,512]{4,3,2,1,0:T(8,128)(2,1)S(1)}, bf16[2,2,2,16,512]{4,3,2,1,0:T(8,128)(2,1)S(1)}, u32[]{:S(2)}, u32[]{:S(2)}) collective-permute-start(bf16[2,2,2,16,512]{4,3,2,1,0:T(8,128)(2,1)S(1)} %pad_maximum_fusion.11), channel_id=1, source_target_pairs={{0,384},{128,0},{256,128},{384,256},{1,385},{129,1},{257,129},{385... | collective-permute-start | bytes 393224 | tf_op jit(solution)/shard_map/exchange_modes/ppermute | solution.py:22
  32.0 23.1 %collective-permute-start.7 = (bf16[2,2,2,16,512]{4,3,2,1,0:T(8,128)(2,1)S(1)}, bf16[2,2,2,16,512]{4,3,2,1,0:T(8,128)(2,1)S(1)}, u32[]{:S(2)}, u32[]{:S(2)}) collective-permute-start(bf16[2,2,2,16,512]{4,3,2,1,0:T(8,128)(2,1)S(1)} %pad_maximum_fusion.10), channel_id=1, source_target_pairs={{0,256},{128,384},{256,0},{384,128},{1,257},{129,385},{257,1},{385... | collective-permute-start | bytes 393224 | tf_op jit(solution)/shard_map/exchange_modes/ppermute | solution.py:22
  37.1 36.1 %collective-permute-start.3 = (bf16[4,2,4,2,16,512]{5,4,3,2,1,0:T(8,128)(2,1)S(1)}, bf16[4,2,4,2,16,512]{5,4,3,2,1,0:T(8,128)(2,1)S(1)}, u32[]{:S(2)}, u32[]{:S(2)}) collective-permute-start(bf16[4,2,4,2,16,512]{5,4,3,2,1,0:T(8,128)(2,1)S(1)} %pad_maximum_fusion.refs_0_), channel_id=1, source_target_pairs={{0,32},{4,12},{8,40},{12,20},{16,48},{20,28},{24,56},{28,4},{32,64... | collective-permute-start | bytes 3145736 | tf_op jit(solution)/shard_map/gather_grad/ppermute | solution.py:42
  40.2 32.9 %collective-permute-start.4 = (bf16[4,2,4,2,16,512]{5,4,3,2,1,0:T(8,128)(2,1)S(1)}, bf16[4,2,4,2,16,512]{5,4,3,2,1,0:T(8,128)(2,1)S(1)}, u32[]{:S(2)}, u32[]{:S(2)}) collective-permute-start(bf16[4,2,4,2,16,512]{5,4,3,2,1,0:T(8,128)(2,1)S(1)} %pad_maximum_fusion.refs_0_), channel_id=1, source_target_pairs={{0,64},{4,20},{8,72},{12,28},{16,80},{20,4},{24,88},{28,12},{32,96... | collective-permute-start | bytes 3145736 | tf_op jit(solution)/shard_map/gather_grad/ppermute | solution.py:42
  44.6 28.6 %collective-permute-start.5 = (bf16[4,2,4,2,16,512]{5,4,3,2,1,0:T(8,128)(2,1)S(1)}, bf16[4,2,4,2,16,512]{5,4,3,2,1,0:T(8,128)(2,1)S(1)}, u32[]{:S(2)}, u32[]{:S(2)}) collective-permute-start(bf16[4,2,4,2,16,512]{5,4,3,2,1,0:T(8,128)(2,1)S(1)} %pad_maximum_fusion.refs_0_), channel_id=1, source_target_pairs={{0,96},{4,28},{8,104},{12,4},{16,112},{20,12},{24,120},{28,20},{32... | collective-permute-start | bytes 3145736 | tf_op jit(solution)/shard_map/gather_grad/ppermute | solution.py:42
  47.7 11.4 %collective-permute-start.6 = (bf16[2,2,2,16,512]{4,3,2,1,0:T(8,128)(2,1)S(1)}, bf16[2,2,2,16,512]{4,3,2,1,0:T(8,128)(2,1)S(1)}, u32[]{:S(2)}, u32[]{:S(2)}) collective-permute-start(bf16[2,2,2,16,512]{4,3,2,1,0:T(8,128)(2,1)S(1)} %pad_maximum_fusion.9), channel_id=1, source_target_pairs={{0,128},{128,256},{256,384},{384,0},{1,129},{129,257},{257,385},{3... | collective-permute-start | bytes 393224 | tf_op jit(solution)/shard_map/exchange_modes/ppermute | solution.py:22
  59.1 22.1 %collective-permute-start.9 = (bf16[2,4,2,16,512]{4,3,2,1,0:T(8,128)(2,1)S(1)}, bf16[2,4,2,16,512]{4,3,2,1,0:T(8,128)(2,1)S(1)}, u32[]{:S(2)}, u32[]{:S(2)}) collective-permute-start(bf16[2,4,2,16,512]{4,3,2,1,0:T(8,128)(2,1)S(1)} %get-tuple-element.15.refs_8_), channel_id=1, source_target_pairs={{0,2},{1,3},{2,0},{3,1},{4,6},{5,7},{6,4},{7,5},{8,10},{9,11},{10,... | collective-permute-start | bytes 786440 | tf_op jit(solution)/shard_map/gather_rows/ppermute | solution.py:26
  71.1 12.0 %collective-permute-start.13 = (bf16[3,2,2,16,512]{4,3,2,1,0:T(8,128)(2,1)S(1)}, bf16[3,2,2,16,512]{4,3,2,1,0:T(8,128)(2,1)S(1)}, u32[]{:S(2)}, u32[]{:S(2)}) collective-permute-start(bf16[3,2,2,16,512]{4,3,2,1,0:T(8,128)(2,1)S(1)} %get-tuple-element.32), channel_id=1, source_target_pairs={{0,8},{4,36},{8,0},{12,44},{16,24},{20,52},{24,16},{28,60},{32,40}... | collective-permute-start | bytes 589832 | tf_op jit(solution)/shard_map/gather_late_grad/ppermute | solution.py:42
  81.2 26.2 %collective-permute-start.10 = (f32[2,4,2,2,16,512]{5,4,3,2,1,0:T(8,128)S(1)}, f32[2,4,2,2,16,512]{5,4,3,2,1,0:T(8,128)S(1)}, u32[]{:S(2)}, u32[]{:S(2)}) collective-permute-start(f32[2,4,2,2,16,512]{5,4,3,2,1,0:T(8,128)S(1)} %get-tuple-element.9), channel_id=1, source_target_pairs={{0,1},{1,0},{2,3},{3,2},{4,5},{5,4},{6,7},{7,6},{8,9},{9,8},{10,11... | collective-permute-start | bytes 3145736 | tf_op jit(solution)/shard_map/sum_input/ppermute | solution.py:26
  83.1 10.0 %collective-permute-start.14 = (bf16[2,3,2,2,16,512]{5,4,3,2,1,0:T(8,128)(2,1)S(1)}, bf16[2,3,2,2,16,512]{5,4,3,2,1,0:T(8,128)(2,1)S(1)}, u32[]{:S(2)}, u32[]{:S(2)}) collective-permute-start(bf16[2,3,2,2,16,512]{5,4,3,2,1,0:T(8,128)(2,1)S(1)} %pad_maximum_fusion.5), channel_id=1, source_target_pairs={{0,24},{4,100},{8,16},{12,108},{16,8},{20,116},{24,0},{28,124},{32... | collective-permute-start | bytes 1179656 | tf_op jit(solution)/shard_map/gather_late_grad/ppermute | solution.py:42
  93.2 34.2 %collective-permute-start.15 = (bf16[4,3,2,2,16,512]{5,4,3,2,1,0:T(8,128)(2,1)S(1)}, bf16[4,3,2,2,16,512]{5,4,3,2,1,0:T(8,128)(2,1)S(1)}, u32[]{:S(2)}, u32[]{:S(2)}) collective-permute-start(bf16[4,3,2,2,16,512]{5,4,3,2,1,0:T(8,128)(2,1)S(1)} %pad_maximum_fusion.2.refs_4_), channel_id=1, source_target_pairs={{0,32},{4,12},{8,40},{12,20},{16,48},{20,28},{24,56},{28,4},{32,64... | collective-permute-start | bytes 2359304 | tf_op jit(solution)/shard_map/gather_late_grad/ppermute | solution.py:42
  95.2 32.3 %collective-permute-start.16 = (bf16[4,3,2,2,16,512]{5,4,3,2,1,0:T(8,128)(2,1)S(1)}, bf16[4,3,2,2,16,512]{5,4,3,2,1,0:T(8,128)(2,1)S(1)}, u32[]{:S(2)}, u32[]{:S(2)}) collective-permute-start(bf16[4,3,2,2,16,512]{5,4,3,2,1,0:T(8,128)(2,1)S(1)} %pad_maximum_fusion.2.refs_4_), channel_id=1, source_target_pairs={{0,64},{4,20},{8,72},{12,28},{16,80},{20,4},{24,88},{28,12},{32,96... | collective-permute-start | bytes 2359304 | tf_op jit(solution)/shard_map/gather_late_grad/ppermute | solution.py:42
  101.6 25.9 %collective-permute-start.17 = (bf16[4,3,2,2,16,512]{5,4,3,2,1,0:T(8,128)(2,1)S(1)}, bf16[4,3,2,2,16,512]{5,4,3,2,1,0:T(8,128)(2,1)S(1)}, u32[]{:S(2)}, u32[]{:S(2)}) collective-permute-start(bf16[4,3,2,2,16,512]{5,4,3,2,1,0:T(8,128)(2,1)S(1)} %pad_maximum_fusion.2.refs_4_), channel_id=1, source_target_pairs={{0,96},{4,28},{8,104},{12,4},{16,112},{20,12},{24,120},{28,20},{32... | collective-permute-start | bytes 2359304 | tf_op jit(solution)/shard_map/gather_late_grad/ppermute | solution.py:42
  103.6 23.9 %collective-permute-start.18 = (bf16[2,2,4,2,16,512]{5,4,3,2,1,0:T(8,128)(2,1)S(1)}, bf16[2,2,4,2,16,512]{5,4,3,2,1,0:T(8,128)(2,1)S(1)}, u32[]{:S(2)}, u32[]{:S(2)}) collective-permute-start(bf16[2,2,4,2,16,512]{5,4,3,2,1,0:T(8,128)(2,1)S(1)} %pad_maximum_fusion.4), channel_id=1, source_target_pairs={{0,1},{1,0},{2,3},{3,2},{4,5},{5,4},{6,7},{7,6},{8,9},{9,8},{10,11... | collective-permute-start | bytes 1572872 | tf_op jit(solution)/shard_map/gather_rows/ppermute | solution.py:26
  107.4 62.2 %collective-permute-start.11 = (f32[4,2,2,16,512]{4,3,2,1,0:T(8,128)S(1)}, f32[4,2,2,16,512]{4,3,2,1,0:T(8,128)S(1)}, u32[]{:S(2)}, u32[]{:S(2)}) collective-permute-start(f32[4,2,2,16,512]{4,3,2,1,0:T(8,128)S(1)} %fusion), channel_id=1, source_target_pairs={{0,2},{1,3},{2,0},{3,1},{4,6},{5,7},{6,4},{7,5},{8,10},{9,11},{10,... | collective-permute-start | bytes 1572872 | tf_op jit(solution)/shard_map/sum_input/ppermute | solution.py:26
  134.8 18.4 %collective-permute-start.22 = (bf16[2,64,512]{2,1,0:T(8,128)(2,1)S(1)}, bf16[2,64,512]{2,1,0:T(8,128)(2,1)S(1)}, u32[]{:S(2)}, u32[]{:S(2)}) collective-permute-start(bf16[2,64,512]{2,1,0:T(8,128)(2,1)S(1)} %get-tuple-element.11.refs_0_), channel_id=1, source_target_pairs={{0,128},{128,256},{256,384},{384,0},{1,129},{129,257},{257,385},{3... | collective-permute-start | bytes 393224 | tf_op jit(solution)/shard_map/spread_weight/ppermute | solution.py:22
  138.5 24.9 %collective-permute-start.20 = (bf16[2,64,512]{2,1,0:T(8,128)(2,1)S(1)}, bf16[2,64,512]{2,1,0:T(8,128)(2,1)S(1)}, u32[]{:S(2)}, u32[]{:S(2)}) collective-permute-start(bf16[2,64,512]{2,1,0:T(8,128)(2,1)S(1)} %collective-permute-done.19.refs_1_), channel_id=1, source_target_pairs={{0,384},{128,0},{256,128},{384,256},{1,385},{129,1},{257,129},{385... | collective-permute-start | bytes 393224 | tf_op jit(solution)/shard_map/spread_weight/ppermute | solution.py:22
  144.0 28.7 %collective-permute-start.24 = (bf16[2,64,512]{2,1,0:T(8,128)(2,1)S(1)}, bf16[2,64,512]{2,1,0:T(8,128)(2,1)S(1)}, u32[]{:S(2)}, u32[]{:S(2)}) collective-permute-start(bf16[2,64,512]{2,1,0:T(8,128)(2,1)S(1)} %get-tuple-element.11.refs_0_), channel_id=1, source_target_pairs={{0,384},{128,0},{256,128},{384,256},{1,385},{129,1},{257,129},{385... | collective-permute-start | bytes 393224 | tf_op jit(solution)/shard_map/spread_weight/ppermute | solution.py:22
  147.9 24.8 %collective-permute-start.23 = (bf16[2,64,512]{2,1,0:T(8,128)(2,1)S(1)}, bf16[2,64,512]{2,1,0:T(8,128)(2,1)S(1)}, u32[]{:S(2)}, u32[]{:S(2)}) collective-permute-start(bf16[2,64,512]{2,1,0:T(8,128)(2,1)S(1)} %collective-permute-done.19.refs_1_), channel_id=1, source_target_pairs={{0,128},{128,256},{256,384},{384,0},{1,129},{129,257},{257,385},{3... | collective-permute-start | bytes 393224 | tf_op jit(solution)/shard_map/spread_weight/ppermute | solution.py:22
  153.2 19.5 %collective-permute-start.25 = (bf16[2,64,512]{2,1,0:T(8,128)(2,1)S(1)}, bf16[2,64,512]{2,1,0:T(8,128)(2,1)S(1)}, u32[]{:S(2)}, u32[]{:S(2)}) collective-permute-start(bf16[2,64,512]{2,1,0:T(8,128)(2,1)S(1)} %collective-permute-done.22.refs_2_), channel_id=1, source_target_pairs={{0,128},{128,256},{256,384},{384,0},{1,129},{129,257},{257,385},{3... | collective-permute-start | bytes 393224 | tf_op jit(solution)/shard_map/spread_weight/ppermute | solution.py:22
  163.4 17.2 %collective-permute-start.21 = (bf16[2,64,512]{2,1,0:T(8,128)(2,1)S(1)}, bf16[2,64,512]{2,1,0:T(8,128)(2,1)S(1)}, u32[]{:S(2)}, u32[]{:S(2)}) collective-permute-start(bf16[2,64,512]{2,1,0:T(8,128)(2,1)S(1)} %collective-permute-done.20.refs_5_), channel_id=1, source_target_pairs={{0,384},{128,0},{256,128},{384,256},{1,385},{129,1},{257,129},{385... | collective-permute-start | bytes 393224 | tf_op jit(solution)/shard_map/spread_weight/ppermute | solution.py:22
  169.8 12.2 %collective-permute-start.12 = (bf16[4,2,16,512]{3,2,1,0:T(8,128)(2,1)S(1)}, bf16[4,2,16,512]{3,2,1,0:T(8,128)(2,1)S(1)}, u32[]{:S(2)}, u32[]{:S(2)}) collective-permute-start(bf16[4,2,16,512]{3,2,1,0:T(8,128)(2,1)S(1)} %get-tuple-element.17), channel_id=1, source_target_pairs={{0,4},{4,0},{8,12},{12,8},{16,20},{20,16},{24,28},{28,24},{32,36},... | collective-permute-start | bytes 393224 | tf_op jit(solution)/shard_map/sum_input/ppermute | solution.py:26
  (5 other events, 42.0 us)

commit v6 on v5

--- a/solution.py
+++ b/solution.py
@@ -79,18 +79,22 @@
 
 
 def input_terms(position, w, w_other, *refs):
-    pieces, (keep, send, grads, sem) = refs[:4], refs[4:]
-    fetch_plane(
-        position,
-        pieces,
-        lambda piece, source: piece.at[source],
-        lambda rows: grads.at[:, :, rows, :],
-        sem,
-    )
+    pieces, (keep, send, grads, sems) = refs[:4], refs[4:]
+    for half in range(2):
+        modes = pl.ds(2 * half, 2)
+        fetch_plane(
+            position,
+            pieces,
+            lambda piece, source, modes=modes: piece.at[source, modes],
+            lambda rows, modes=modes: grads.at[modes, :, rows, :],
+            sems.at[half],
+        )
     base = (position[1] & 1) * 4
     rows = [pl.ds(tree_row(position, r), 16) for r in range(4)]
-    pltpu.make_async_copy(grads, grads, sem).wait()
     for mode in range(4):
+        if mode % 2 == 0:
+            arrived = grads.at[pl.ds(mode, 2)]
+            pltpu.make_async_copy(arrived, arrived, sems.at[mode // 2]).wait()
         real, imag = (
             jnp.concatenate(
                 [block for row in rows for block in (w[base + mode, part, row, :], w_other[mode, part, row, :])],
@@ -236,7 +240,7 @@
         out_shape=(tree, tree),
         in_specs=[SMEM, VMEM, VMEM] + [ANY] * 4,
         out_specs=(VMEM, VMEM),
-        scratch_shapes=[pltpu.VMEM((4, 2, 512, 512), jnp.bfloat16), pltpu.SemaphoreType.DMA],
+        scratch_shapes=[pltpu.VMEM((4, 2, 512, 512), jnp.bfloat16), pltpu.SemaphoreType.DMA((2,))],
         compiler_params=pltpu.CompilerParams(vmem_limit_bytes=24 * MIB),
         cost_estimate=pl.CostEstimate(flops=1 << 30, bytes_accessed=8 * MIB, transcendentals=0),
         name="input_terms",

time: 184 us -> 183 us (level)
  transfers between devices with their start and end apart: 26 -> 26, of which waited for: 9 -> 9; matrix products, arithmetic and copies ran while one was open for 0% -> 0% of each run, Pallas kernels for 6% -> 7%
where the time goes in v6:
time: 183 us
  starting transfers between devices  113 us (62%)
  waiting for transfers between devices  52.8 us (29%)
  Pallas kernels  12.3 us (7%)
    ppermute x9, starting transfers between devices, ring(): return lax.ppermute(value, axis, [(i, (i + shift) % 4) for i in range(4)])  50.4 us
    ppermute x7, starting transfers between devices, flip(): return lax.ppermute(value, axis, [(i, i ^ bits) for i in range(size)])  34.5 us
    ppermute x10, starting transfers between devices, hop(): return lax.ppermute(value, 'cin', pairs)  28.5 us
    ppermute x7, waiting for transfers between devices, flip(): return lax.ppermute(value, axis, [(i, i ^ bits) for i in range(size)])  23.8 us
    ppermute x9, waiting for transfers between devices, ring(): return lax.ppermute(value, axis, [(i, (i + shift) % 4) for i in range(4)])  15.4 us
    ppermute x10, waiting for transfers between devices, hop(): return lax.ppermute(value, 'cin', pairs)  13.6 us
    pallas_call x1, Pallas kernels, on_device(): pl.pallas_call(weight_terms, out_shape=[jax.ShapeDtypeStruct((2, 64, 512)...  4.24 us
    pallas_call x2, Pallas kernels, place_call(): pl.pallas_call(body, out_shape=jax.ShapeDtypeStruct((8, 2, 64, 512), jnp....  4.1 us
  transfers between devices with their start and end apart: 26, of which 9 were waited for; matrix products, arithmetic and copies ran while one was open for 0% of the time, Pallas kernels for 7%

profile of v6, /device:TPU:1, one launch (start us, length us, event | category | flops | bytes accessed | tf_op | source)
XLA Modules:
  0.0 182.6 jit_solution(17906919482596145979)
XLA Ops:
  1.9 8.8 %collective-permute-start = (bf16[4,2,96,512]{3,2,1,0:T(8,128)(2,1)S(1)}, bf16[4,2,96,512]{3,2,1,0:T(8,128)(2,1)S(1)}, u32[]{:S(2)}, u32[]{:S(2)}) collective-permute-start(bf16[4,2,96,512]{3,2,1,0:T(8,128)(2,1)S(1)} %pad_maximum_fusion.1), channel_id=1, source_target_pairs={{0,4},{4,0},{8,12},{12,8},{16,20},{20,16},{24,28},{28,24},{32,36},... | collective-permute-start | bytes 2359304 | tf_op jit(solution)/shard_map/swap_modes/ppermute | solution.py:26
  14.6 5.5 %collective-permute-done.1 = bf16[2,4,2,16,512]{4,3,2,1,0:T(8,128)(2,1)S(1)} collective-permute-done((bf16[2,4,2,16,512]{4,3,2,1,0:T(8,128)(2,1)S(1)}, bf16[2,4,2,16,512]{4,3,2,1,0:T(8,128)(2,1)S(1)}, u32[]{:S(2)}, u32[]{:S(2)}) %collective-permute-start.1) | collective-permute-done | bytes 262176 | tf_op jit(solution)/shard_map/gather_grad/ppermute | solution.py:42
  22.2 9.8 %collective-permute-start.8 = (bf16[2,2,2,16,512]{4,3,2,1,0:T(8,128)(2,1)S(1)}, bf16[2,2,2,16,512]{4,3,2,1,0:T(8,128)(2,1)S(1)}, u32[]{:S(2)}, u32[]{:S(2)}) collective-permute-start(bf16[2,2,2,16,512]{4,3,2,1,0:T(8,128)(2,1)S(1)} %pad_maximum_fusion.11), channel_id=1, source_target_pairs={{0,384},{128,0},{256,128},{384,256},{1,385},{129,1},{257,129},{385... | collective-permute-start | bytes 393224 | tf_op jit(solution)/shard_map/exchange_modes/ppermute | solution.py:22
  32.0 4.9 %collective-permute-start.7 = (bf16[2,2,2,16,512]{4,3,2,1,0:T(8,128)(2,1)S(1)}, bf16[2,2,2,16,512]{4,3,2,1,0:T(8,128)(2,1)S(1)}, u32[]{:S(2)}, u32[]{:S(2)}) collective-permute-start(bf16[2,2,2,16,512]{4,3,2,1,0:T(8,128)(2,1)S(1)} %pad_maximum_fusion.10), channel_id=1, source_target_pairs={{0,256},{128,384},{256,0},{384,128},{1,257},{129,385},{257,1},{385... | collective-permute-start | bytes 393224 | tf_op jit(solution)/shard_map/exchange_modes/ppermute | solution.py:22
  37.1 3.1 %collective-permute-start.3 = (bf16[4,2,4,2,16,512]{5,4,3,2,1,0:T(8,128)(2,1)S(1)}, bf16[4,2,4,2,16,512]{5,4,3,2,1,0:T(8,128)(2,1)S(1)}, u32[]{:S(2)}, u32[]{:S(2)}) collective-permute-start(bf16[4,2,4,2,16,512]{5,4,3,2,1,0:T(8,128)(2,1)S(1)} %pad_maximum_fusion.refs_0_), channel_id=1, source_target_pairs={{0,32},{4,12},{8,40},{12,20},{16,48},{20,28},{24,56},{28,4},{32,64... | collective-permute-start | bytes 3145736 | tf_op jit(solution)/shard_map/gather_grad/ppermute | solution.py:42
  40.2 4.4 %collective-permute-start.4 = (bf16[4,2,4,2,16,512]{5,4,3,2,1,0:T(8,128)(2,1)S(1)}, bf16[4,2,4,2,16,512]{5,4,3,2,1,0:T(8,128)(2,1)S(1)}, u32[]{:S(2)}, u32[]{:S(2)}) collective-permute-start(bf16[4,2,4,2,16,512]{5,4,3,2,1,0:T(8,128)(2,1)S(1)} %pad_maximum_fusion.refs_0_), channel_id=1, source_target_pairs={{0,64},{4,20},{8,72},{12,28},{16,80},{20,4},{24,88},{28,12},{32,96... | collective-permute-start | bytes 3145736 | tf_op jit(solution)/shard_map/gather_grad/ppermute | solution.py:42
  47.7 7.4 %collective-permute-start.6 = (bf16[2,2,2,16,512]{4,3,2,1,0:T(8,128)(2,1)S(1)}, bf16[2,2,2,16,512]{4,3,2,1,0:T(8,128)(2,1)S(1)}, u32[]{:S(2)}, u32[]{:S(2)}) collective-permute-start(bf16[2,2,2,16,512]{4,3,2,1,0:T(8,128)(2,1)S(1)} %pad_maximum_fusion.9), channel_id=1, source_target_pairs={{0,128},{128,256},{256,384},{384,0},{1,129},{129,257},{257,385},{3... | collective-permute-start | bytes 393224 | tf_op jit(solution)/shard_map/exchange_modes/ppermute | solution.py:22
  55.1 3.9 %collective-permute-done.6 = bf16[2,2,2,16,512]{4,3,2,1,0:T(8,128)(2,1)S(1)} collective-permute-done((bf16[2,2,2,16,512]{4,3,2,1,0:T(8,128)(2,1)S(1)}, bf16[2,2,2,16,512]{4,3,2,1,0:T(8,128)(2,1)S(1)}, u32[]{:S(2)}, u32[]{:S(2)}) %collective-permute-start.6) | collective-permute-done | bytes 131104 | tf_op jit(solution)/shard_map/exchange_modes/ppermute | solution.py:22
  59.1 12.0 %collective-permute-start.9 = (bf16[2,4,2,16,512]{4,3,2,1,0:T(8,128)(2,1)S(1)}, bf16[2,4,2,16,512]{4,3,2,1,0:T(8,128)(2,1)S(1)}, u32[]{:S(2)}, u32[]{:S(2)}) collective-permute-start(bf16[2,4,2,16,512]{4,3,2,1,0:T(8,128)(2,1)S(1)} %get-tuple-element.15.refs_8_), channel_id=1, source_target_pairs={{0,2},{1,3},{2,0},{3,1},{4,6},{5,7},{6,4},{7,5},{8,10},{9,11},{10,... | collective-permute-start | bytes 786440 | tf_op jit(solution)/shard_map/gather_rows/ppermute | solution.py:26
  73.1 4.0 %input_terms.1 = (f32[2,4,2,2,16,512]{5,4,3,2,1,0:T(8,128)S(1)}, f32[2,4,2,2,16,512]{5,4,3,2,1,0:T(8,128)S(1)}) custom-call(s32[3]{0:T(128)S(1)} %pad_add_fusion.position, bf16[8,2,64,512]{3,2,1,0:T(8,128)(2,1)S(1)} %copy-done, bf16[4,2,96,512]{3,2,1,0:T(8,128)(2,1)S(1)} %collective-permute-done.w_other, ...), custom_call_target="tpu_custom_call" | custom-call | flops 1073741824 | bytes 8388608 | tf_op jit(solution)/shard_map/input_terms/pallas_call | solution.py:238
  77.1 4.0 %collective-permute-done.9.refs_9_ = bf16[2,4,2,16,512]{4,3,2,1,0:T(8,128)(2,1)S(1)} collective-permute-done((bf16[2,4,2,16,512]{4,3,2,1,0:T(8,128)(2,1)S(1)}, bf16[2,4,2,16,512]{4,3,2,1,0:T(8,128)(2,1)S(1)}, u32[]{:S(2)}, u32[]{:S(2)}) %collective-permute-start.9) | collective-permute-done | bytes 262176 | tf_op jit(solution)/shard_map/gather_rows/ppermute | solution.py:26
  85.1 8.1 %collective-permute-done.14 = bf16[2,3,2,2,16,512]{5,4,3,2,1,0:T(8,128)(2,1)S(1)} collective-permute-done((bf16[2,3,2,2,16,512]{5,4,3,2,1,0:T(8,128)(2,1)S(1)}, bf16[2,3,2,2,16,512]{5,4,3,2,1,0:T(8,128)(2,1)S(1)}, u32[]{:S(2)}, u32[]{:S(2)}) %collective-permute-start.14) | collective-permute-done | bytes 393248 | tf_op jit(solution)/shard_map/gather_late_grad/ppermute | solution.py:42
  95.2 6.4 %collective-permute-start.16 = (bf16[4,3,2,2,16,512]{5,4,3,2,1,0:T(8,128)(2,1)S(1)}, bf16[4,3,2,2,16,512]{5,4,3,2,1,0:T(8,128)(2,1)S(1)}, u32[]{:S(2)}, u32[]{:S(2)}) collective-permute-start(bf16[4,3,2,2,16,512]{5,4,3,2,1,0:T(8,128)(2,1)S(1)} %pad_maximum_fusion.2.refs_4_), channel_id=1, source_target_pairs={{0,64},{4,20},{8,72},{12,28},{16,80},{20,4},{24,88},{28,12},{32,96... | collective-permute-start | bytes 2359304 | tf_op jit(solution)/shard_map/gather_late_grad/ppermute | solution.py:42
  103.6 3.4 %collective-permute-start.18 = (bf16[2,2,4,2,16,512]{5,4,3,2,1,0:T(8,128)(2,1)S(1)}, bf16[2,2,4,2,16,512]{5,4,3,2,1,0:T(8,128)(2,1)S(1)}, u32[]{:S(2)}, u32[]{:S(2)}) collective-permute-start(bf16[2,2,4,2,16,512]{5,4,3,2,1,0:T(8,128)(2,1)S(1)} %pad_maximum_fusion.4), channel_id=1, source_target_pairs={{0,1},{1,0},{2,3},{3,2},{4,5},{5,4},{6,7},{7,6},{8,9},{9,8},{10,11... | collective-permute-start | bytes 1572872 | tf_op jit(solution)/shard_map/gather_rows/ppermute | solution.py:26
  110.0 17.5 %collective-permute-done.18.refs_10_ = bf16[2,2,4,2,16,512]{5,4,3,2,1,0:T(8,128)(2,1)S(1)} collective-permute-done((bf16[2,2,4,2,16,512]{5,4,3,2,1,0:T(8,128)(2,1)S(1)}, bf16[2,2,4,2,16,512]{5,4,3,2,1,0:T(8,128)(2,1)S(1)}, u32[]{:S(2)}, u32[]{:S(2)}) %collective-permute-start.18) | collective-permute-done | bytes 524320 | tf_op jit(solution)/shard_map/gather_rows/ppermute | solution.py:26
  127.5 4.2 %weight_terms.1 = (bf16[2,64,512]{2,1,0:T(8,128)(2,1)S(1)}, bf16[2,64,512]{2,1,0:T(8,128)(2,1)S(1)}) custom-call(s32[3]{0:T(128)S(1)} %pad_add_fusion.position, bf16[4,2,4,2,16,512]{5,4,3,2,1,0:T(8,128)(2,1)S(1)} %pad_maximum_fusion.refs_0_, bf16[4,2,4,2,16,512]{5,4,3,2,1,0:T(8,128)(2,1)S(1)} %collective-permute-done.3.refs_1_, ...), custom_call_target="tpu_custom_call" | custom-call | flops 1073741824 | bytes 5242880 | tf_op jit(solution)/shard_map/weight_terms/pallas_call | solution.py:259
  134.8 3.7 %collective-permute-start.22 = (bf16[2,64,512]{2,1,0:T(8,128)(2,1)S(1)}, bf16[2,64,512]{2,1,0:T(8,128)(2,1)S(1)}, u32[]{:S(2)}, u32[]{:S(2)}) collective-permute-start(bf16[2,64,512]{2,1,0:T(8,128)(2,1)S(1)} %get-tuple-element.11.refs_0_), channel_id=1, source_target_pairs={{0,128},{128,256},{256,384},{384,0},{1,129},{129,257},{257,385},{3... | collective-permute-start | bytes 393224 | tf_op jit(solution)/shard_map/spread_weight/ppermute | solution.py:22
  138.5 5.5 %collective-permute-start.20 = (bf16[2,64,512]{2,1,0:T(8,128)(2,1)S(1)}, bf16[2,64,512]{2,1,0:T(8,128)(2,1)S(1)}, u32[]{:S(2)}, u32[]{:S(2)}) collective-permute-start(bf16[2,64,512]{2,1,0:T(8,128)(2,1)S(1)} %collective-permute-done.19.refs_1_), channel_id=1, source_target_pairs={{0,384},{128,0},{256,128},{384,256},{1,385},{129,1},{257,129},{385... | collective-permute-start | bytes 393224 | tf_op jit(solution)/shard_map/spread_weight/ppermute | solution.py:22
  144.0 4.1 %collective-permute-start.24 = (bf16[2,64,512]{2,1,0:T(8,128)(2,1)S(1)}, bf16[2,64,512]{2,1,0:T(8,128)(2,1)S(1)}, u32[]{:S(2)}, u32[]{:S(2)}) collective-permute-start(bf16[2,64,512]{2,1,0:T(8,128)(2,1)S(1)} %get-tuple-element.11.refs_0_), channel_id=1, source_target_pairs={{0,384},{128,0},{256,128},{384,256},{1,385},{129,1},{257,129},{385... | collective-permute-start | bytes 393224 | tf_op jit(solution)/shard_map/spread_weight/ppermute | solution.py:22
  148.1 5.1 %collective-permute-start.23 = (bf16[2,64,512]{2,1,0:T(8,128)(2,1)S(1)}, bf16[2,64,512]{2,1,0:T(8,128)(2,1)S(1)}, u32[]{:S(2)}, u32[]{:S(2)}) collective-permute-start(bf16[2,64,512]{2,1,0:T(8,128)(2,1)S(1)} %collective-permute-done.19.refs_1_), channel_id=1, source_target_pairs={{0,128},{128,256},{256,384},{384,0},{1,129},{129,257},{257,385},{3... | collective-permute-start | bytes 393224 | tf_op jit(solution)/shard_map/spread_weight/ppermute | solution.py:22
  153.2 3.7 %collective-permute-start.25 = (bf16[2,64,512]{2,1,0:T(8,128)(2,1)S(1)}, bf16[2,64,512]{2,1,0:T(8,128)(2,1)S(1)}, u32[]{:S(2)}, u32[]{:S(2)}) collective-permute-start(bf16[2,64,512]{2,1,0:T(8,128)(2,1)S(1)} %collective-permute-done.22.refs_2_), channel_id=1, source_target_pairs={{0,128},{128,256},{256,384},{384,0},{1,129},{129,257},{257,385},{3... | collective-permute-start | bytes 393224 | tf_op jit(solution)/shard_map/spread_weight/ppermute | solution.py:22
  156.9 6.5 %collective-permute-done.20.refs_5_ = bf16[2,64,512]{2,1,0:T(8,128)(2,1)S(1)} collective-permute-done((bf16[2,64,512]{2,1,0:T(8,128)(2,1)S(1)}, bf16[2,64,512]{2,1,0:T(8,128)(2,1)S(1)}, u32[]{:S(2)}, u32[]{:S(2)}) %collective-permute-start.20) | collective-permute-done | bytes 131104 | tf_op jit(solution)/shard_map/spread_weight/ppermute | solution.py:22
  163.4 6.2 %collective-permute-start.21 = (bf16[2,64,512]{2,1,0:T(8,128)(2,1)S(1)}, bf16[2,64,512]{2,1,0:T(8,128)(2,1)S(1)}, u32[]{:S(2)}, u32[]{:S(2)}) collective-permute-start(bf16[2,64,512]{2,1,0:T(8,128)(2,1)S(1)} %collective-permute-done.20.refs_5_), channel_id=1, source_target_pairs={{0,384},{128,0},{256,128},{384,256},{1,385},{129,1},{257,129},{385... | collective-permute-start | bytes 393224 | tf_op jit(solution)/shard_map/spread_weight/ppermute | solution.py:22
  175.4 5.1 %collective-permute-done.21.piece = bf16[2,64,512]{2,1,0:T(8,128)(2,1)S(1)} collective-permute-done((bf16[2,64,512]{2,1,0:T(8,128)(2,1)S(1)}, bf16[2,64,512]{2,1,0:T(8,128)(2,1)S(1)}, u32[]{:S(2)}, u32[]{:S(2)}) %collective-permute-start.21) | collective-permute-done | bytes 131104 | tf_op jit(solution)/shard_map/spread_weight/ppermute | solution.py:22
  (63 shorter events, 34.3 us)
Async XLA Ops:
  1.9 10.7 %collective-permute-start = (bf16[4,2,96,512]{3,2,1,0:T(8,128)(2,1)S(1)}, bf16[4,2,96,512]{3,2,1,0:T(8,128)(2,1)S(1)}, u32[]{:S(2)}, u32[]{:S(2)}) collective-permute-start(bf16[4,2,96,512]{3,2,1,0:T(8,128)(2,1)S(1)} %pad_maximum_fusion.1), channel_id=1, source_target_pairs={{0,4},{4,0},{8,12},{12,8},{16,20},{20,16},{24,28},{28,24},{32,36},... | collective-permute-start | bytes 2359304 | tf_op jit(solution)/shard_map/swap_modes/ppermute | solution.py:26
  20.1 16.8 %collective-permute-start.2 = (bf16[2,2,4,2,16,512]{5,4,3,2,1,0:T(8,128)(2,1)S(1)}, bf16[2,2,4,2,16,512]{5,4,3,2,1,0:T(8,128)(2,1)S(1)}, u32[]{:S(2)}, u32[]{:S(2)}) collective-permute-start(bf16[2,2,4,2,16,512]{5,4,3,2,1,0:T(8,128)(2,1)S(1)} %pad_maximum_fusion.3), channel_id=1, source_target_pairs={{0,24},{4,100},{8,16},{12,108},{16,8},{20,116},{24,0},{28,124},{32... | collective-permute-start | bytes 1572872 | tf_op jit(solution)/shard_map/gather_grad/ppermute | solution.py:42
  22.2 25.5 %collective-permute-start.8 = (bf16[2,2,2,16,512]{4,3,2,1,0:T(8,128)(2,1)S(1)}, bf16[2,2,2,16,512]{4,3,2,1,0:T(8,128)(2,1)S(1)}, u32[]{:S(2)}, u32[]{:S(2)}) collective-permute-start(bf16[2,2,2,16,512]{4,3,2,1,0:T(8,128)(2,1)S(1)} %pad_maximum_fusion.11), channel_id=1, source_target_pairs={{0,384},{128,0},{256,128},{384,256},{1,385},{129,1},{257,129},{385... | collective-permute-start | bytes 393224 | tf_op jit(solution)/shard_map/exchange_modes/ppermute | solution.py:22
  32.0 23.1 %collective-permute-start.7 = (bf16[2,2,2,16,512]{4,3,2,1,0:T(8,128)(2,1)S(1)}, bf16[2,2,2,16,512]{4,3,2,1,0:T(8,128)(2,1)S(1)}, u32[]{:S(2)}, u32[]{:S(2)}) collective-permute-start(bf16[2,2,2,16,512]{4,3,2,1,0:T(8,128)(2,1)S(1)} %pad_maximum_fusion.10), channel_id=1, source_target_pairs={{0,256},{128,384},{256,0},{384,128},{1,257},{129,385},{257,1},{385... | collective-permute-start | bytes 393224 | tf_op jit(solution)/shard_map/exchange_modes/ppermute | solution.py:22
  37.1 36.1 %collective-permute-start.3 = (bf16[4,2,4,2,16,512]{5,4,3,2,1,0:T(8,128)(2,1)S(1)}, bf16[4,2,4,2,16,512]{5,4,3,2,1,0:T(8,128)(2,1)S(1)}, u32[]{:S(2)}, u32[]{:S(2)}) collective-permute-start(bf16[4,2,4,2,16,512]{5,4,3,2,1,0:T(8,128)(2,1)S(1)} %pad_maximum_fusion.refs_0_), channel_id=1, source_target_pairs={{0,32},{4,12},{8,40},{12,20},{16,48},{20,28},{24,56},{28,4},{32,64... | collective-permute-start | bytes 3145736 | tf_op jit(solution)/shard_map/gather_grad/ppermute | solution.py:42
  40.2 32.9 %collective-permute-start.4 = (bf16[4,2,4,2,16,512]{5,4,3,2,1,0:T(8,128)(2,1)S(1)}, bf16[4,2,4,2,16,512]{5,4,3,2,1,0:T(8,128)(2,1)S(1)}, u32[]{:S(2)}, u32[]{:S(2)}) collective-permute-start(bf16[4,2,4,2,16,512]{5,4,3,2,1,0:T(8,128)(2,1)S(1)} %pad_maximum_fusion.refs_0_), channel_id=1, source_target_pairs={{0,64},{4,20},{8,72},{12,28},{16,80},{20,4},{24,88},{28,12},{32,96... | collective-permute-start | bytes 3145736 | tf_op jit(solution)/shard_map/gather_grad/ppermute | solution.py:42
  44.6 28.6 %collective-permute-start.5 = (bf16[4,2,4,2,16,512]{5,4,3,2,1,0:T(8,128)(2,1)S(1)}, bf16[4,2,4,2,16,512]{5,4,3,2,1,0:T(8,128)(2,1)S(1)}, u32[]{:S(2)}, u32[]{:S(2)}) collective-permute-start(bf16[4,2,4,2,16,512]{5,4,3,2,1,0:T(8,128)(2,1)S(1)} %pad_maximum_fusion.refs_0_), channel_id=1, source_target_pairs={{0,96},{4,28},{8,104},{12,4},{16,112},{20,12},{24,120},{28,20},{32... | collective-permute-start | bytes 3145736 | tf_op jit(solution)/shard_map/gather_grad/ppermute | solution.py:42
  47.7 11.4 %collective-permute-start.6 = (bf16[2,2,2,16,512]{4,3,2,1,0:T(8,128)(2,1)S(1)}, bf16[2,2,2,16,512]{4,3,2,1,0:T(8,128)(2,1)S(1)}, u32[]{:S(2)}, u32[]{:S(2)}) collective-permute-start(bf16[2,2,2,16,512]{4,3,2,1,0:T(8,128)(2,1)S(1)} %pad_maximum_fusion.9), channel_id=1, source_target_pairs={{0,128},{128,256},{256,384},{384,0},{1,129},{129,257},{257,385},{3... | collective-permute-start | bytes 393224 | tf_op jit(solution)/shard_map/exchange_modes/ppermute | solution.py:22
  59.1 22.1 %collective-permute-start.9 = (bf16[2,4,2,16,512]{4,3,2,1,0:T(8,128)(2,1)S(1)}, bf16[2,4,2,16,512]{4,3,2,1,0:T(8,128)(2,1)S(1)}, u32[]{:S(2)}, u32[]{:S(2)}) collective-permute-start(bf16[2,4,2,16,512]{4,3,2,1,0:T(8,128)(2,1)S(1)} %get-tuple-element.15.refs_8_), channel_id=1, source_target_pairs={{0,2},{1,3},{2,0},{3,1},{4,6},{5,7},{6,4},{7,5},{8,10},{9,11},{10,... | collective-permute-start | bytes 786440 | tf_op jit(solution)/shard_map/gather_rows/ppermute | solution.py:26
  71.1 12.0 %collective-permute-start.13 = (bf16[3,2,2,16,512]{4,3,2,1,0:T(8,128)(2,1)S(1)}, bf16[3,2,2,16,512]{4,3,2,1,0:T(8,128)(2,1)S(1)}, u32[]{:S(2)}, u32[]{:S(2)}) collective-permute-start(bf16[3,2,2,16,512]{4,3,2,1,0:T(8,128)(2,1)S(1)} %get-tuple-element.32), channel_id=1, source_target_pairs={{0,8},{4,36},{8,0},{12,44},{16,24},{20,52},{24,16},{28,60},{32,40}... | collective-permute-start | bytes 589832 | tf_op jit(solution)/shard_map/gather_late_grad/ppermute | solution.py:42
  81.2 26.2 %collective-permute-start.10 = (f32[2,4,2,2,16,512]{5,4,3,2,1,0:T(8,128)S(1)}, f32[2,4,2,2,16,512]{5,4,3,2,1,0:T(8,128)S(1)}, u32[]{:S(2)}, u32[]{:S(2)}) collective-permute-start(f32[2,4,2,2,16,512]{5,4,3,2,1,0:T(8,128)S(1)} %get-tuple-element.9), channel_id=1, source_target_pairs={{0,1},{1,0},{2,3},{3,2},{4,5},{5,4},{6,7},{7,6},{8,9},{9,8},{10,11... | collective-permute-start | bytes 3145736 | tf_op jit(solution)/shard_map/sum_input/ppermute | solution.py:26
  83.1 10.0 %collective-permute-start.14 = (bf16[2,3,2,2,16,512]{5,4,3,2,1,0:T(8,128)(2,1)S(1)}, bf16[2,3,2,2,16,512]{5,4,3,2,1,0:T(8,128)(2,1)S(1)}, u32[]{:S(2)}, u32[]{:S(2)}) collective-permute-start(bf16[2,3,2,2,16,512]{5,4,3,2,1,0:T(8,128)(2,1)S(1)} %pad_maximum_fusion.5), channel_id=1, source_target_pairs={{0,24},{4,100},{8,16},{12,108},{16,8},{20,116},{24,0},{28,124},{32... | collective-permute-start | bytes 1179656 | tf_op jit(solution)/shard_map/gather_late_grad/ppermute | solution.py:42
  93.2 34.2 %collective-permute-start.15 = (bf16[4,3,2,2,16,512]{5,4,3,2,1,0:T(8,128)(2,1)S(1)}, bf16[4,3,2,2,16,512]{5,4,3,2,1,0:T(8,128)(2,1)S(1)}, u32[]{:S(2)}, u32[]{:S(2)}) collective-permute-start(bf16[4,3,2,2,16,512]{5,4,3,2,1,0:T(8,128)(2,1)S(1)} %pad_maximum_fusion.2.refs_4_), channel_id=1, source_target_pairs={{0,32},{4,12},{8,40},{12,20},{16,48},{20,28},{24,56},{28,4},{32,64... | collective-permute-start | bytes 2359304 | tf_op jit(solution)/shard_map/gather_late_grad/ppermute | solution.py:42
  95.2 32.3 %collective-permute-start.16 = (bf16[4,3,2,2,16,512]{5,4,3,2,1,0:T(8,128)(2,1)S(1)}, bf16[4,3,2,2,16,512]{5,4,3,2,1,0:T(8,128)(2,1)S(1)}, u32[]{:S(2)}, u32[]{:S(2)}) collective-permute-start(bf16[4,3,2,2,16,512]{5,4,3,2,1,0:T(8,128)(2,1)S(1)} %pad_maximum_fusion.2.refs_4_), channel_id=1, source_target_pairs={{0,64},{4,20},{8,72},{12,28},{16,80},{20,4},{24,88},{28,12},{32,96... | collective-permute-start | bytes 2359304 | tf_op jit(solution)/shard_map/gather_late_grad/ppermute | solution.py:42
  101.6 25.9 %collective-permute-start.17 = (bf16[4,3,2,2,16,512]{5,4,3,2,1,0:T(8,128)(2,1)S(1)}, bf16[4,3,2,2,16,512]{5,4,3,2,1,0:T(8,128)(2,1)S(1)}, u32[]{:S(2)}, u32[]{:S(2)}) collective-permute-start(bf16[4,3,2,2,16,512]{5,4,3,2,1,0:T(8,128)(2,1)S(1)} %pad_maximum_fusion.2.refs_4_), channel_id=1, source_target_pairs={{0,96},{4,28},{8,104},{12,4},{16,112},{20,12},{24,120},{28,20},{32... | collective-permute-start | bytes 2359304 | tf_op jit(solution)/shard_map/gather_late_grad/ppermute | solution.py:42
  103.6 23.9 %collective-permute-start.18 = (bf16[2,2,4,2,16,512]{5,4,3,2,1,0:T(8,128)(2,1)S(1)}, bf16[2,2,4,2,16,512]{5,4,3,2,1,0:T(8,128)(2,1)S(1)}, u32[]{:S(2)}, u32[]{:S(2)}) collective-permute-start(bf16[2,2,4,2,16,512]{5,4,3,2,1,0:T(8,128)(2,1)S(1)} %pad_maximum_fusion.4), channel_id=1, source_target_pairs={{0,1},{1,0},{2,3},{3,2},{4,5},{5,4},{6,7},{7,6},{8,9},{9,8},{10,11... | collective-permute-start | bytes 1572872 | tf_op jit(solution)/shard_map/gather_rows/ppermute | solution.py:26
  107.4 62.2 %collective-permute-start.11 = (f32[4,2,2,16,512]{4,3,2,1,0:T(8,128)S(1)}, f32[4,2,2,16,512]{4,3,2,1,0:T(8,128)S(1)}, u32[]{:S(2)}, u32[]{:S(2)}) collective-permute-start(f32[4,2,2,16,512]{4,3,2,1,0:T(8,128)S(1)} %fusion), channel_id=1, source_target_pairs={{0,2},{1,3},{2,0},{3,1},{4,6},{5,7},{6,4},{7,5},{8,10},{9,11},{10,... | collective-permute-start | bytes 1572872 | tf_op jit(solution)/shard_map/sum_input/ppermute | solution.py:26
  134.8 18.4 %collective-permute-start.22 = (bf16[2,64,512]{2,1,0:T(8,128)(2,1)S(1)}, bf16[2,64,512]{2,1,0:T(8,128)(2,1)S(1)}, u32[]{:S(2)}, u32[]{:S(2)}) collective-permute-start(bf16[2,64,512]{2,1,0:T(8,128)(2,1)S(1)} %get-tuple-element.11.refs_0_), channel_id=1, source_target_pairs={{0,128},{128,256},{256,384},{384,0},{1,129},{129,257},{257,385},{3... | collective-permute-start | bytes 393224 | tf_op jit(solution)/shard_map/spread_weight/ppermute | solution.py:22
  138.5 24.9 %collective-permute-start.20 = (bf16[2,64,512]{2,1,0:T(8,128)(2,1)S(1)}, bf16[2,64,512]{2,1,0:T(8,128)(2,1)S(1)}, u32[]{:S(2)}, u32[]{:S(2)}) collective-permute-start(bf16[2,64,512]{2,1,0:T(8,128)(2,1)S(1)} %collective-permute-done.19.refs_1_), channel_id=1, source_target_pairs={{0,384},{128,0},{256,128},{384,256},{1,385},{129,1},{257,129},{385... | collective-permute-start | bytes 393224 | tf_op jit(solution)/shard_map/spread_weight/ppermute | solution.py:22
  144.0 28.7 %collective-permute-start.24 = (bf16[2,64,512]{2,1,0:T(8,128)(2,1)S(1)}, bf16[2,64,512]{2,1,0:T(8,128)(2,1)S(1)}, u32[]{:S(2)}, u32[]{:S(2)}) collective-permute-start(bf16[2,64,512]{2,1,0:T(8,128)(2,1)S(1)} %get-tuple-element.11.refs_0_), channel_id=1, source_target_pairs={{0,384},{128,0},{256,128},{384,256},{1,385},{129,1},{257,129},{385... | collective-permute-start | bytes 393224 | tf_op jit(solution)/shard_map/spread_weight/ppermute | solution.py:22
  148.1 24.6 %collective-permute-start.23 = (bf16[2,64,512]{2,1,0:T(8,128)(2,1)S(1)}, bf16[2,64,512]{2,1,0:T(8,128)(2,1)S(1)}, u32[]{:S(2)}, u32[]{:S(2)}) collective-permute-start(bf16[2,64,512]{2,1,0:T(8,128)(2,1)S(1)} %collective-permute-done.19.refs_1_), channel_id=1, source_target_pairs={{0,128},{128,256},{256,384},{384,0},{1,129},{129,257},{257,385},{3... | collective-permute-start | bytes 393224 | tf_op jit(solution)/shard_map/spread_weight/ppermute | solution.py:22
  153.2 19.5 %collective-permute-start.25 = (bf16[2,64,512]{2,1,0:T(8,128)(2,1)S(1)}, bf16[2,64,512]{2,1,0:T(8,128)(2,1)S(1)}, u32[]{:S(2)}, u32[]{:S(2)}) collective-permute-start(bf16[2,64,512]{2,1,0:T(8,128)(2,1)S(1)} %collective-permute-done.22.refs_2_), channel_id=1, source_target_pairs={{0,128},{128,256},{256,384},{384,0},{1,129},{129,257},{257,385},{3... | collective-permute-start | bytes 393224 | tf_op jit(solution)/shard_map/spread_weight/ppermute | solution.py:22
  163.4 17.1 %collective-permute-start.21 = (bf16[2,64,512]{2,1,0:T(8,128)(2,1)S(1)}, bf16[2,64,512]{2,1,0:T(8,128)(2,1)S(1)}, u32[]{:S(2)}, u32[]{:S(2)}) collective-permute-start(bf16[2,64,512]{2,1,0:T(8,128)(2,1)S(1)} %collective-permute-done.20.refs_5_), channel_id=1, source_target_pairs={{0,384},{128,0},{256,128},{384,256},{1,385},{129,1},{257,129},{385... | collective-permute-start | bytes 393224 | tf_op jit(solution)/shard_map/spread_weight/ppermute | solution.py:22
  169.8 12.1 %collective-permute-start.12 = (bf16[4,2,16,512]{3,2,1,0:T(8,128)(2,1)S(1)}, bf16[4,2,16,512]{3,2,1,0:T(8,128)(2,1)S(1)}, u32[]{:S(2)}, u32[]{:S(2)}) collective-permute-start(bf16[4,2,16,512]{3,2,1,0:T(8,128)(2,1)S(1)} %get-tuple-element.17), channel_id=1, source_target_pairs={{0,4},{4,0},{8,12},{12,8},{16,20},{20,16},{24,28},{28,24},{32,36},... | collective-permute-start | bytes 393224 | tf_op jit(solution)/shard_map/sum_input/ppermute | solution.py:26
  (5 other events, 42.0 us)

commit v7 on v5

--- a/solution.py
+++ b/solution.py
@@ -278,7 +278,7 @@
         [here, other, back_0, back_1, ahead_0, ahead_1, far_0],
         position,
     )
-    weight_grad = place_call(place_last, "place_last", [far_1], position, placed)
+    weight_grad = place_call(place_last, "place_last", [far_1], after(position, spectrum_grad), placed)
     return (spectrum_grad, weight_grad)
 
 

time: 184 us -> 184 us (level)
  transfers between devices with their start and end apart: 26 -> 26, of which waited for: 9 -> 9; matrix products, arithmetic and copies ran while one was open for 0% -> 1% of each run, Pallas kernels for 6% -> 5%
where the time goes in v7:
time: 184 us; the launch traced here: 182 us
  starting transfers between devices  113 us (61%)
  waiting for transfers between devices  53.5 us (29%)
  Pallas kernels  11.2 us (6%)
    ppermute x9, starting transfers between devices, ring(): return lax.ppermute(value, axis, [(i, (i + shift) % 4) for i in range(4)])  49.6 us
    ppermute x7, starting transfers between devices, flip(): return lax.ppermute(value, axis, [(i, i ^ bits) for i in range(size)])  35 us
    ppermute x10, starting transfers between devices, hop(): return lax.ppermute(value, 'cin', pairs)  28.5 us
    ppermute x7, waiting for transfers between devices, flip(): return lax.ppermute(value, axis, [(i, i ^ bits) for i in range(size)])  24.9 us
    ppermute x9, waiting for transfers between devices, ring(): return lax.ppermute(value, axis, [(i, (i + shift) % 4) for i in range(4)])  15 us
    ppermute x10, waiting for transfers between devices, hop(): return lax.ppermute(value, 'cin', pairs)  13.6 us
    pallas_call x1, Pallas kernels, on_device(): pl.pallas_call(weight_terms, out_shape=[jax.ShapeDtypeStruct((2, 64, 512)...  4.24 us
    pallas_call x2, Pallas kernels, place_call(): pl.pallas_call(body, out_shape=jax.ShapeDtypeStruct((8, 2, 64, 512), jnp....  4.1 us
  transfers between devices with their start and end apart: 26, of which 9 were waited for; matrix products, arithmetic and copies ran while one was open for 1% of the time, Pallas kernels for 5%

profile of v7, /device:TPU:1, one launch (start us, length us, event | category | flops | bytes accessed | tf_op | source)
XLA Modules:
  0.0 181.9 jit_solution(5794154029713508294)
XLA Ops:
  1.9 8.8 %collective-permute-start = (bf16[4,2,96,512]{3,2,1,0:T(8,128)(2,1)S(1)}, bf16[4,2,96,512]{3,2,1,0:T(8,128)(2,1)S(1)}, u32[]{:S(2)}, u32[]{:S(2)}) collective-permute-start(bf16[4,2,96,512]{3,2,1,0:T(8,128)(2,1)S(1)} %pad_maximum_fusion.1), channel_id=1, source_target_pairs={{0,4},{4,0},{8,12},{12,8},{16,20},{20,16},{24,28},{28,24},{32,36},... | collective-permute-start | bytes 2359304 | tf_op jit(solution)/shard_map/swap_modes/ppermute | solution.py:26
  14.6 5.5 %collective-permute-done.1 = bf16[2,4,2,16,512]{4,3,2,1,0:T(8,128)(2,1)S(1)} collective-permute-done((bf16[2,4,2,16,512]{4,3,2,1,0:T(8,128)(2,1)S(1)}, bf16[2,4,2,16,512]{4,3,2,1,0:T(8,128)(2,1)S(1)}, u32[]{:S(2)}, u32[]{:S(2)}) %collective-permute-start.1) | collective-permute-done | bytes 262176 | tf_op jit(solution)/shard_map/gather_grad/ppermute | solution.py:42
  22.2 9.8 %collective-permute-start.8 = (bf16[2,2,2,16,512]{4,3,2,1,0:T(8,128)(2,1)S(1)}, bf16[2,2,2,16,512]{4,3,2,1,0:T(8,128)(2,1)S(1)}, u32[]{:S(2)}, u32[]{:S(2)}) collective-permute-start(bf16[2,2,2,16,512]{4,3,2,1,0:T(8,128)(2,1)S(1)} %pad_maximum_fusion.11), channel_id=1, source_target_pairs={{0,384},{128,0},{256,128},{384,256},{1,385},{129,1},{257,129},{385... | collective-permute-start | bytes 393224 | tf_op jit(solution)/shard_map/exchange_modes/ppermute | solution.py:22
  32.0 4.9 %collective-permute-start.7 = (bf16[2,2,2,16,512]{4,3,2,1,0:T(8,128)(2,1)S(1)}, bf16[2,2,2,16,512]{4,3,2,1,0:T(8,128)(2,1)S(1)}, u32[]{:S(2)}, u32[]{:S(2)}) collective-permute-start(bf16[2,2,2,16,512]{4,3,2,1,0:T(8,128)(2,1)S(1)} %pad_maximum_fusion.10), channel_id=1, source_target_pairs={{0,256},{128,384},{256,0},{384,128},{1,257},{129,385},{257,1},{385... | collective-permute-start | bytes 393224 | tf_op jit(solution)/shard_map/exchange_modes/ppermute | solution.py:22
  37.1 3.1 %collective-permute-start.3 = (bf16[4,2,4,2,16,512]{5,4,3,2,1,0:T(8,128)(2,1)S(1)}, bf16[4,2,4,2,16,512]{5,4,3,2,1,0:T(8,128)(2,1)S(1)}, u32[]{:S(2)}, u32[]{:S(2)}) collective-permute-start(bf16[4,2,4,2,16,512]{5,4,3,2,1,0:T(8,128)(2,1)S(1)} %pad_maximum_fusion.refs_0_), channel_id=1, source_target_pairs={{0,32},{4,12},{8,40},{12,20},{16,48},{20,28},{24,56},{28,4},{32,64... | collective-permute-start | bytes 3145736 | tf_op jit(solution)/shard_map/gather_grad/ppermute | solution.py:42
  40.2 4.4 %collective-permute-start.4 = (bf16[4,2,4,2,16,512]{5,4,3,2,1,0:T(8,128)(2,1)S(1)}, bf16[4,2,4,2,16,512]{5,4,3,2,1,0:T(8,128)(2,1)S(1)}, u32[]{:S(2)}, u32[]{:S(2)}) collective-permute-start(bf16[4,2,4,2,16,512]{5,4,3,2,1,0:T(8,128)(2,1)S(1)} %pad_maximum_fusion.refs_0_), channel_id=1, source_target_pairs={{0,64},{4,20},{8,72},{12,28},{16,80},{20,4},{24,88},{28,12},{32,96... | collective-permute-start | bytes 3145736 | tf_op jit(solution)/shard_map/gather_grad/ppermute | solution.py:42
  47.7 7.4 %collective-permute-start.6 = (bf16[2,2,2,16,512]{4,3,2,1,0:T(8,128)(2,1)S(1)}, bf16[2,2,2,16,512]{4,3,2,1,0:T(8,128)(2,1)S(1)}, u32[]{:S(2)}, u32[]{:S(2)}) collective-permute-start(bf16[2,2,2,16,512]{4,3,2,1,0:T(8,128)(2,1)S(1)} %pad_maximum_fusion.9), channel_id=1, source_target_pairs={{0,128},{128,256},{256,384},{384,0},{1,129},{129,257},{257,385},{3... | collective-permute-start | bytes 393224 | tf_op jit(solution)/shard_map/exchange_modes/ppermute | solution.py:22
  55.1 3.9 %collective-permute-done.6 = bf16[2,2,2,16,512]{4,3,2,1,0:T(8,128)(2,1)S(1)} collective-permute-done((bf16[2,2,2,16,512]{4,3,2,1,0:T(8,128)(2,1)S(1)}, bf16[2,2,2,16,512]{4,3,2,1,0:T(8,128)(2,1)S(1)}, u32[]{:S(2)}, u32[]{:S(2)}) %collective-permute-start.6) | collective-permute-done | bytes 131104 | tf_op jit(solution)/shard_map/exchange_modes/ppermute | solution.py:22
  59.1 12.0 %collective-permute-start.9 = (bf16[2,4,2,16,512]{4,3,2,1,0:T(8,128)(2,1)S(1)}, bf16[2,4,2,16,512]{4,3,2,1,0:T(8,128)(2,1)S(1)}, u32[]{:S(2)}, u32[]{:S(2)}) collective-permute-start(bf16[2,4,2,16,512]{4,3,2,1,0:T(8,128)(2,1)S(1)} %get-tuple-element.17.refs_8_), channel_id=1, source_target_pairs={{0,2},{1,3},{2,0},{3,1},{4,6},{5,7},{6,4},{7,5},{8,10},{9,11},{10,... | collective-permute-start | bytes 786440 | tf_op jit(solution)/shard_map/gather_rows/ppermute | solution.py:26
  76.0 5.1 %collective-permute-done.9.refs_9_ = bf16[2,4,2,16,512]{4,3,2,1,0:T(8,128)(2,1)S(1)} collective-permute-done((bf16[2,4,2,16,512]{4,3,2,1,0:T(8,128)(2,1)S(1)}, bf16[2,4,2,16,512]{4,3,2,1,0:T(8,128)(2,1)S(1)}, u32[]{:S(2)}, u32[]{:S(2)}) %collective-permute-start.9) | collective-permute-done | bytes 262176 | tf_op jit(solution)/shard_map/gather_rows/ppermute | solution.py:26
  85.1 8.1 %collective-permute-done.14 = bf16[2,3,2,2,16,512]{5,4,3,2,1,0:T(8,128)(2,1)S(1)} collective-permute-done((bf16[2,3,2,2,16,512]{5,4,3,2,1,0:T(8,128)(2,1)S(1)}, bf16[2,3,2,2,16,512]{5,4,3,2,1,0:T(8,128)(2,1)S(1)}, u32[]{:S(2)}, u32[]{:S(2)}) %collective-permute-start.14) | collective-permute-done | bytes 393248 | tf_op jit(solution)/shard_map/gather_late_grad/ppermute | solution.py:42
  95.2 6.4 %collective-permute-start.16 = (bf16[4,3,2,2,16,512]{5,4,3,2,1,0:T(8,128)(2,1)S(1)}, bf16[4,3,2,2,16,512]{5,4,3,2,1,0:T(8,128)(2,1)S(1)}, u32[]{:S(2)}, u32[]{:S(2)}) collective-permute-start(bf16[4,3,2,2,16,512]{5,4,3,2,1,0:T(8,128)(2,1)S(1)} %pad_maximum_fusion.2.refs_4_), channel_id=1, source_target_pairs={{0,64},{4,20},{8,72},{12,28},{16,80},{20,4},{24,88},{28,12},{32,96... | collective-permute-start | bytes 2359304 | tf_op jit(solution)/shard_map/gather_late_grad/ppermute | solution.py:42
  103.6 3.4 %collective-permute-start.18 = (bf16[2,2,4,2,16,512]{5,4,3,2,1,0:T(8,128)(2,1)S(1)}, bf16[2,2,4,2,16,512]{5,4,3,2,1,0:T(8,128)(2,1)S(1)}, u32[]{:S(2)}, u32[]{:S(2)}) collective-permute-start(bf16[2,2,4,2,16,512]{5,4,3,2,1,0:T(8,128)(2,1)S(1)} %pad_maximum_fusion.4), channel_id=1, source_target_pairs={{0,1},{1,0},{2,3},{3,2},{4,5},{5,4},{6,7},{7,6},{8,9},{9,8},{10,11... | collective-permute-start | bytes 1572872 | tf_op jit(solution)/shard_map/gather_rows/ppermute | solution.py:26
  110.0 17.5 %collective-permute-done.18.refs_10_ = bf16[2,2,4,2,16,512]{5,4,3,2,1,0:T(8,128)(2,1)S(1)} collective-permute-done((bf16[2,2,4,2,16,512]{5,4,3,2,1,0:T(8,128)(2,1)S(1)}, bf16[2,2,4,2,16,512]{5,4,3,2,1,0:T(8,128)(2,1)S(1)}, u32[]{:S(2)}, u32[]{:S(2)}) %collective-permute-start.18) | collective-permute-done | bytes 524320 | tf_op jit(solution)/shard_map/gather_rows/ppermute | solution.py:26
  127.5 4.2 %weight_terms.1 = (bf16[2,64,512]{2,1,0:T(8,128)(2,1)S(1)}, bf16[2,64,512]{2,1,0:T(8,128)(2,1)S(1)}) custom-call(s32[3]{0:T(128)S(1)} %pad_add_fusion.position, bf16[4,2,4,2,16,512]{5,4,3,2,1,0:T(8,128)(2,1)S(1)} %pad_maximum_fusion.refs_0_, bf16[4,2,4,2,16,512]{5,4,3,2,1,0:T(8,128)(2,1)S(1)} %collective-permute-done.3.refs_1_, ...), custom_call_target="tpu_custom_call" | custom-call | flops 1073741824 | bytes 5242880 | tf_op jit(solution)/shard_map/weight_terms/pallas_call | solution.py:255
  134.8 3.7 %collective-permute-start.22 = (bf16[2,64,512]{2,1,0:T(8,128)(2,1)S(1)}, bf16[2,64,512]{2,1,0:T(8,128)(2,1)S(1)}, u32[]{:S(2)}, u32[]{:S(2)}) collective-permute-start(bf16[2,64,512]{2,1,0:T(8,128)(2,1)S(1)} %get-tuple-element.13.refs_0_), channel_id=1, source_target_pairs={{0,128},{128,256},{256,384},{384,0},{1,129},{129,257},{257,385},{3... | collective-permute-start | bytes 393224 | tf_op jit(solution)/shard_map/spread_weight/ppermute | solution.py:22
  138.5 5.5 %collective-permute-start.24 = (bf16[2,64,512]{2,1,0:T(8,128)(2,1)S(1)}, bf16[2,64,512]{2,1,0:T(8,128)(2,1)S(1)}, u32[]{:S(2)}, u32[]{:S(2)}) collective-permute-start(bf16[2,64,512]{2,1,0:T(8,128)(2,1)S(1)} %get-tuple-element.13.refs_0_), channel_id=1, source_target_pairs={{0,384},{128,0},{256,128},{384,256},{1,385},{129,1},{257,129},{385... | collective-permute-start | bytes 393224 | tf_op jit(solution)/shard_map/spread_weight/ppermute | solution.py:22
  144.0 3.9 %collective-permute-start.20 = (bf16[2,64,512]{2,1,0:T(8,128)(2,1)S(1)}, bf16[2,64,512]{2,1,0:T(8,128)(2,1)S(1)}, u32[]{:S(2)}, u32[]{:S(2)}) collective-permute-start(bf16[2,64,512]{2,1,0:T(8,128)(2,1)S(1)} %collective-permute-done.19.refs_1_), channel_id=1, source_target_pairs={{0,384},{128,0},{256,128},{384,256},{1,385},{129,1},{257,129},{385... | collective-permute-start | bytes 393224 | tf_op jit(solution)/shard_map/spread_weight/ppermute | solution.py:22
  147.9 5.3 %collective-permute-start.23 = (bf16[2,64,512]{2,1,0:T(8,128)(2,1)S(1)}, bf16[2,64,512]{2,1,0:T(8,128)(2,1)S(1)}, u32[]{:S(2)}, u32[]{:S(2)}) collective-permute-start(bf16[2,64,512]{2,1,0:T(8,128)(2,1)S(1)} %collective-permute-done.19.refs_1_), channel_id=1, source_target_pairs={{0,128},{128,256},{256,384},{384,0},{1,129},{129,257},{257,385},{3... | collective-permute-start | bytes 393224 | tf_op jit(solution)/shard_map/spread_weight/ppermute | solution.py:22
  153.2 3.7 %collective-permute-start.25 = (bf16[2,64,512]{2,1,0:T(8,128)(2,1)S(1)}, bf16[2,64,512]{2,1,0:T(8,128)(2,1)S(1)}, u32[]{:S(2)}, u32[]{:S(2)}) collective-permute-start(bf16[2,64,512]{2,1,0:T(8,128)(2,1)S(1)} %collective-permute-done.22.refs_2_), channel_id=1, source_target_pairs={{0,128},{128,256},{256,384},{384,0},{1,129},{129,257},{257,385},{3... | collective-permute-start | bytes 393224 | tf_op jit(solution)/shard_map/spread_weight/ppermute | solution.py:22
  157.1 3.3 %collective-permute-start.12 = (bf16[4,2,16,512]{3,2,1,0:T(8,128)(2,1)S(1)}, bf16[4,2,16,512]{3,2,1,0:T(8,128)(2,1)S(1)}, u32[]{:S(2)}, u32[]{:S(2)}) collective-permute-start(bf16[4,2,16,512]{3,2,1,0:T(8,128)(2,1)S(1)} %get-tuple-element.19), channel_id=1, source_target_pairs={{0,4},{4,0},{8,12},{12,8},{16,20},{20,16},{24,28},{28,24},{32,36},... | collective-permute-start | bytes 393224 | tf_op jit(solution)/shard_map/sum_input/ppermute | solution.py:26
  160.5 6.5 %collective-permute-done.20.refs_5_ = bf16[2,64,512]{2,1,0:T(8,128)(2,1)S(1)} collective-permute-done((bf16[2,64,512]{2,1,0:T(8,128)(2,1)S(1)}, bf16[2,64,512]{2,1,0:T(8,128)(2,1)S(1)}, u32[]{:S(2)}, u32[]{:S(2)}) %collective-permute-start.20) | collective-permute-done | bytes 131104 | tf_op jit(solution)/shard_map/spread_weight/ppermute | solution.py:22
  167.0 5.4 %collective-permute-start.21 = (bf16[2,64,512]{2,1,0:T(8,128)(2,1)S(1)}, bf16[2,64,512]{2,1,0:T(8,128)(2,1)S(1)}, u32[]{:S(2)}, u32[]{:S(2)}) collective-permute-start(bf16[2,64,512]{2,1,0:T(8,128)(2,1)S(1)} %collective-permute-done.20.refs_5_), channel_id=1, source_target_pairs={{0,384},{128,0},{256,128},{384,256},{1,385},{129,1},{257,129},{385... | collective-permute-start | bytes 393224 | tf_op jit(solution)/shard_map/spread_weight/ppermute | solution.py:22
  175.9 4.6 %collective-permute-done.21.piece = bf16[2,64,512]{2,1,0:T(8,128)(2,1)S(1)} collective-permute-done((bf16[2,64,512]{2,1,0:T(8,128)(2,1)S(1)}, bf16[2,64,512]{2,1,0:T(8,128)(2,1)S(1)}, u32[]{:S(2)}, u32[]{:S(2)}) %collective-permute-start.21) | collective-permute-done | bytes 131104 | tf_op jit(solution)/shard_map/spread_weight/ppermute | solution.py:22
  (63 shorter events, 34.3 us)
Async XLA Ops:
  1.9 10.7 %collective-permute-start = (bf16[4,2,96,512]{3,2,1,0:T(8,128)(2,1)S(1)}, bf16[4,2,96,512]{3,2,1,0:T(8,128)(2,1)S(1)}, u32[]{:S(2)}, u32[]{:S(2)}) collective-permute-start(bf16[4,2,96,512]{3,2,1,0:T(8,128)(2,1)S(1)} %pad_maximum_fusion.1), channel_id=1, source_target_pairs={{0,4},{4,0},{8,12},{12,8},{16,20},{20,16},{24,28},{28,24},{32,36},... | collective-permute-start | bytes 2359304 | tf_op jit(solution)/shard_map/swap_modes/ppermute | solution.py:26
  20.1 16.8 %collective-permute-start.2 = (bf16[2,2,4,2,16,512]{5,4,3,2,1,0:T(8,128)(2,1)S(1)}, bf16[2,2,4,2,16,512]{5,4,3,2,1,0:T(8,128)(2,1)S(1)}, u32[]{:S(2)}, u32[]{:S(2)}) collective-permute-start(bf16[2,2,4,2,16,512]{5,4,3,2,1,0:T(8,128)(2,1)S(1)} %pad_maximum_fusion.3), channel_id=1, source_target_pairs={{0,24},{4,100},{8,16},{12,108},{16,8},{20,116},{24,0},{28,124},{32... | collective-permute-start | bytes 1572872 | tf_op jit(solution)/shard_map/gather_grad/ppermute | solution.py:42
  22.2 25.5 %collective-permute-start.8 = (bf16[2,2,2,16,512]{4,3,2,1,0:T(8,128)(2,1)S(1)}, bf16[2,2,2,16,512]{4,3,2,1,0:T(8,128)(2,1)S(1)}, u32[]{:S(2)}, u32[]{:S(2)}) collective-permute-start(bf16[2,2,2,16,512]{4,3,2,1,0:T(8,128)(2,1)S(1)} %pad_maximum_fusion.11), channel_id=1, source_target_pairs={{0,384},{128,0},{256,128},{384,256},{1,385},{129,1},{257,129},{385... | collective-permute-start | bytes 393224 | tf_op jit(solution)/shard_map/exchange_modes/ppermute | solution.py:22
  32.0 23.1 %collective-permute-start.7 = (bf16[2,2,2,16,512]{4,3,2,1,0:T(8,128)(2,1)S(1)}, bf16[2,2,2,16,512]{4,3,2,1,0:T(8,128)(2,1)S(1)}, u32[]{:S(2)}, u32[]{:S(2)}) collective-permute-start(bf16[2,2,2,16,512]{4,3,2,1,0:T(8,128)(2,1)S(1)} %pad_maximum_fusion.10), channel_id=1, source_target_pairs={{0,256},{128,384},{256,0},{384,128},{1,257},{129,385},{257,1},{385... | collective-permute-start | bytes 393224 | tf_op jit(solution)/shard_map/exchange_modes/ppermute | solution.py:22
  37.1 36.1 %collective-permute-start.3 = (bf16[4,2,4,2,16,512]{5,4,3,2,1,0:T(8,128)(2,1)S(1)}, bf16[4,2,4,2,16,512]{5,4,3,2,1,0:T(8,128)(2,1)S(1)}, u32[]{:S(2)}, u32[]{:S(2)}) collective-permute-start(bf16[4,2,4,2,16,512]{5,4,3,2,1,0:T(8,128)(2,1)S(1)} %pad_maximum_fusion.refs_0_), channel_id=1, source_target_pairs={{0,32},{4,12},{8,40},{12,20},{16,48},{20,28},{24,56},{28,4},{32,64... | collective-permute-start | bytes 3145736 | tf_op jit(solution)/shard_map/gather_grad/ppermute | solution.py:42
  40.2 32.9 %collective-permute-start.4 = (bf16[4,2,4,2,16,512]{5,4,3,2,1,0:T(8,128)(2,1)S(1)}, bf16[4,2,4,2,16,512]{5,4,3,2,1,0:T(8,128)(2,1)S(1)}, u32[]{:S(2)}, u32[]{:S(2)}) collective-permute-start(bf16[4,2,4,2,16,512]{5,4,3,2,1,0:T(8,128)(2,1)S(1)} %pad_maximum_fusion.refs_0_), channel_id=1, source_target_pairs={{0,64},{4,20},{8,72},{12,28},{16,80},{20,4},{24,88},{28,12},{32,96... | collective-permute-start | bytes 3145736 | tf_op jit(solution)/shard_map/gather_grad/ppermute | solution.py:42
  44.6 28.6 %collective-permute-start.5 = (bf16[4,2,4,2,16,512]{5,4,3,2,1,0:T(8,128)(2,1)S(1)}, bf16[4,2,4,2,16,512]{5,4,3,2,1,0:T(8,128)(2,1)S(1)}, u32[]{:S(2)}, u32[]{:S(2)}) collective-permute-start(bf16[4,2,4,2,16,512]{5,4,3,2,1,0:T(8,128)(2,1)S(1)} %pad_maximum_fusion.refs_0_), channel_id=1, source_target_pairs={{0,96},{4,28},{8,104},{12,4},{16,112},{20,12},{24,120},{28,20},{32... | collective-permute-start | bytes 3145736 | tf_op jit(solution)/shard_map/gather_grad/ppermute | solution.py:42
  47.7 11.4 %collective-permute-start.6 = (bf16[2,2,2,16,512]{4,3,2,1,0:T(8,128)(2,1)S(1)}, bf16[2,2,2,16,512]{4,3,2,1,0:T(8,128)(2,1)S(1)}, u32[]{:S(2)}, u32[]{:S(2)}) collective-permute-start(bf16[2,2,2,16,512]{4,3,2,1,0:T(8,128)(2,1)S(1)} %pad_maximum_fusion.9), channel_id=1, source_target_pairs={{0,128},{128,256},{256,384},{384,0},{1,129},{129,257},{257,385},{3... | collective-permute-start | bytes 393224 | tf_op jit(solution)/shard_map/exchange_modes/ppermute | solution.py:22
  59.1 22.1 %collective-permute-start.9 = (bf16[2,4,2,16,512]{4,3,2,1,0:T(8,128)(2,1)S(1)}, bf16[2,4,2,16,512]{4,3,2,1,0:T(8,128)(2,1)S(1)}, u32[]{:S(2)}, u32[]{:S(2)}) collective-permute-start(bf16[2,4,2,16,512]{4,3,2,1,0:T(8,128)(2,1)S(1)} %get-tuple-element.17.refs_8_), channel_id=1, source_target_pairs={{0,2},{1,3},{2,0},{3,1},{4,6},{5,7},{6,4},{7,5},{8,10},{9,11},{10,... | collective-permute-start | bytes 786440 | tf_op jit(solution)/shard_map/gather_rows/ppermute | solution.py:26
  71.2 11.9 %collective-permute-start.13 = (bf16[3,2,2,16,512]{4,3,2,1,0:T(8,128)(2,1)S(1)}, bf16[3,2,2,16,512]{4,3,2,1,0:T(8,128)(2,1)S(1)}, u32[]{:S(2)}, u32[]{:S(2)}) collective-permute-start(bf16[3,2,2,16,512]{4,3,2,1,0:T(8,128)(2,1)S(1)} %get-tuple-element.34), channel_id=1, source_target_pairs={{0,8},{4,36},{8,0},{12,44},{16,24},{20,52},{24,16},{28,60},{32,40}... | collective-permute-start | bytes 589832 | tf_op jit(solution)/shard_map/gather_late_grad/ppermute | solution.py:42
  81.2 26.2 %collective-permute-start.10 = (f32[2,4,2,2,16,512]{5,4,3,2,1,0:T(8,128)S(1)}, f32[2,4,2,2,16,512]{5,4,3,2,1,0:T(8,128)S(1)}, u32[]{:S(2)}, u32[]{:S(2)}) collective-permute-start(f32[2,4,2,2,16,512]{5,4,3,2,1,0:T(8,128)S(1)} %get-tuple-element.10), channel_id=1, source_target_pairs={{0,1},{1,0},{2,3},{3,2},{4,5},{5,4},{6,7},{7,6},{8,9},{9,8},{10,11... | collective-permute-start | bytes 3145736 | tf_op jit(solution)/shard_map/sum_input/ppermute | solution.py:26
  93.2 34.2 %collective-permute-start.15 = (bf16[4,3,2,2,16,512]{5,4,3,2,1,0:T(8,128)(2,1)S(1)}, bf16[4,3,2,2,16,512]{5,4,3,2,1,0:T(8,128)(2,1)S(1)}, u32[]{:S(2)}, u32[]{:S(2)}) collective-permute-start(bf16[4,3,2,2,16,512]{5,4,3,2,1,0:T(8,128)(2,1)S(1)} %pad_maximum_fusion.2.refs_4_), channel_id=1, source_target_pairs={{0,32},{4,12},{8,40},{12,20},{16,48},{20,28},{24,56},{28,4},{32,64... | collective-permute-start | bytes 2359304 | tf_op jit(solution)/shard_map/gather_late_grad/ppermute | solution.py:42
  95.2 32.3 %collective-permute-start.16 = (bf16[4,3,2,2,16,512]{5,4,3,2,1,0:T(8,128)(2,1)S(1)}, bf16[4,3,2,2,16,512]{5,4,3,2,1,0:T(8,128)(2,1)S(1)}, u32[]{:S(2)}, u32[]{:S(2)}) collective-permute-start(bf16[4,3,2,2,16,512]{5,4,3,2,1,0:T(8,128)(2,1)S(1)} %pad_maximum_fusion.2.refs_4_), channel_id=1, source_target_pairs={{0,64},{4,20},{8,72},{12,28},{16,80},{20,4},{24,88},{28,12},{32,96... | collective-permute-start | bytes 2359304 | tf_op jit(solution)/shard_map/gather_late_grad/ppermute | solution.py:42
  101.6 25.9 %collective-permute-start.17 = (bf16[4,3,2,2,16,512]{5,4,3,2,1,0:T(8,128)(2,1)S(1)}, bf16[4,3,2,2,16,512]{5,4,3,2,1,0:T(8,128)(2,1)S(1)}, u32[]{:S(2)}, u32[]{:S(2)}) collective-permute-start(bf16[4,3,2,2,16,512]{5,4,3,2,1,0:T(8,128)(2,1)S(1)} %pad_maximum_fusion.2.refs_4_), channel_id=1, source_target_pairs={{0,96},{4,28},{8,104},{12,4},{16,112},{20,12},{24,120},{28,20},{32... | collective-permute-start | bytes 2359304 | tf_op jit(solution)/shard_map/gather_late_grad/ppermute | solution.py:42
  103.6 23.9 %collective-permute-start.18 = (bf16[2,2,4,2,16,512]{5,4,3,2,1,0:T(8,128)(2,1)S(1)}, bf16[2,2,4,2,16,512]{5,4,3,2,1,0:T(8,128)(2,1)S(1)}, u32[]{:S(2)}, u32[]{:S(2)}) collective-permute-start(bf16[2,2,4,2,16,512]{5,4,3,2,1,0:T(8,128)(2,1)S(1)} %pad_maximum_fusion.4), channel_id=1, source_target_pairs={{0,1},{1,0},{2,3},{3,2},{4,5},{5,4},{6,7},{7,6},{8,9},{9,8},{10,11... | collective-permute-start | bytes 1572872 | tf_op jit(solution)/shard_map/gather_rows/ppermute | solution.py:26
  107.4 49.5 %collective-permute-start.11 = (f32[4,2,2,16,512]{4,3,2,1,0:T(8,128)S(1)}, f32[4,2,2,16,512]{4,3,2,1,0:T(8,128)S(1)}, u32[]{:S(2)}, u32[]{:S(2)}) collective-permute-start(f32[4,2,2,16,512]{4,3,2,1,0:T(8,128)S(1)} %fusion), channel_id=1, source_target_pairs={{0,2},{1,3},{2,0},{3,1},{4,6},{5,7},{6,4},{7,5},{8,10},{9,11},{10,... | collective-permute-start | bytes 1572872 | tf_op jit(solution)/shard_map/sum_input/ppermute | solution.py:26
  131.7 12.3 %collective-permute-start.19 = (bf16[2,64,512]{2,1,0:T(8,128)(2,1)S(1)}, bf16[2,64,512]{2,1,0:T(8,128)(2,1)S(1)}, u32[]{:S(2)}, u32[]{:S(2)}) collective-permute-start(bf16[2,64,512]{2,1,0:T(8,128)(2,1)S(1)} %get-tuple-element.12), channel_id=1, source_target_pairs={{0,4},{4,0},{8,12},{12,8},{16,20},{20,16},{24,28},{28,24},{32,36},... | collective-permute-start | bytes 393224 | tf_op jit(solution)/shard_map/spread_weight/ppermute | solution.py:26
  134.8 18.4 %collective-permute-start.22 = (bf16[2,64,512]{2,1,0:T(8,128)(2,1)S(1)}, bf16[2,64,512]{2,1,0:T(8,128)(2,1)S(1)}, u32[]{:S(2)}, u32[]{:S(2)}) collective-permute-start(bf16[2,64,512]{2,1,0:T(8,128)(2,1)S(1)} %get-tuple-element.13.refs_0_), channel_id=1, source_target_pairs={{0,128},{128,256},{256,384},{384,0},{1,129},{129,257},{257,385},{3... | collective-permute-start | bytes 393224 | tf_op jit(solution)/shard_map/spread_weight/ppermute | solution.py:22
  138.5 33.9 %collective-permute-start.24 = (bf16[2,64,512]{2,1,0:T(8,128)(2,1)S(1)}, bf16[2,64,512]{2,1,0:T(8,128)(2,1)S(1)}, u32[]{:S(2)}, u32[]{:S(2)}) collective-permute-start(bf16[2,64,512]{2,1,0:T(8,128)(2,1)S(1)} %get-tuple-element.13.refs_0_), channel_id=1, source_target_pairs={{0,384},{128,0},{256,128},{384,256},{1,385},{129,1},{257,129},{385... | collective-permute-start | bytes 393224 | tf_op jit(solution)/shard_map/spread_weight/ppermute | solution.py:22
  144.0 23.0 %collective-permute-start.20 = (bf16[2,64,512]{2,1,0:T(8,128)(2,1)S(1)}, bf16[2,64,512]{2,1,0:T(8,128)(2,1)S(1)}, u32[]{:S(2)}, u32[]{:S(2)}) collective-permute-start(bf16[2,64,512]{2,1,0:T(8,128)(2,1)S(1)} %collective-permute-done.19.refs_1_), channel_id=1, source_target_pairs={{0,384},{128,0},{256,128},{384,256},{1,385},{129,1},{257,129},{385... | collective-permute-start | bytes 393224 | tf_op jit(solution)/shard_map/spread_weight/ppermute | solution.py:22
  147.9 24.5 %collective-permute-start.23 = (bf16[2,64,512]{2,1,0:T(8,128)(2,1)S(1)}, bf16[2,64,512]{2,1,0:T(8,128)(2,1)S(1)}, u32[]{:S(2)}, u32[]{:S(2)}) collective-permute-start(bf16[2,64,512]{2,1,0:T(8,128)(2,1)S(1)} %collective-permute-done.19.refs_1_), channel_id=1, source_target_pairs={{0,128},{128,256},{256,384},{384,0},{1,129},{129,257},{257,385},{3... | collective-permute-start | bytes 393224 | tf_op jit(solution)/shard_map/spread_weight/ppermute | solution.py:22
  153.2 19.2 %collective-permute-start.25 = (bf16[2,64,512]{2,1,0:T(8,128)(2,1)S(1)}, bf16[2,64,512]{2,1,0:T(8,128)(2,1)S(1)}, u32[]{:S(2)}, u32[]{:S(2)}) collective-permute-start(bf16[2,64,512]{2,1,0:T(8,128)(2,1)S(1)} %collective-permute-done.22.refs_2_), channel_id=1, source_target_pairs={{0,128},{128,256},{256,384},{384,0},{1,129},{129,257},{257,385},{3... | collective-permute-start | bytes 393224 | tf_op jit(solution)/shard_map/spread_weight/ppermute | solution.py:22
  157.1 18.0 %collective-permute-start.12 = (bf16[4,2,16,512]{3,2,1,0:T(8,128)(2,1)S(1)}, bf16[4,2,16,512]{3,2,1,0:T(8,128)(2,1)S(1)}, u32[]{:S(2)}, u32[]{:S(2)}) collective-permute-start(bf16[4,2,16,512]{3,2,1,0:T(8,128)(2,1)S(1)} %get-tuple-element.19), channel_id=1, source_target_pairs={{0,4},{4,0},{8,12},{12,8},{16,20},{20,16},{24,28},{28,24},{32,36},... | collective-permute-start | bytes 393224 | tf_op jit(solution)/shard_map/sum_input/ppermute | solution.py:26
  167.0 13.5 %collective-permute-start.21 = (bf16[2,64,512]{2,1,0:T(8,128)(2,1)S(1)}, bf16[2,64,512]{2,1,0:T(8,128)(2,1)S(1)}, u32[]{:S(2)}, u32[]{:S(2)}) collective-permute-start(bf16[2,64,512]{2,1,0:T(8,128)(2,1)S(1)} %collective-permute-done.20.refs_5_), channel_id=1, source_target_pairs={{0,384},{128,0},{256,128},{384,256},{1,385},{129,1},{257,129},{385... | collective-permute-start | bytes 393224 | tf_op jit(solution)/shard_map/spread_weight/ppermute | solution.py:22
  (5 other events, 45.3 us)
